TPU v7x, 256 devices: a whole 4x4x8 slice. The times are simulated.
256 devices in a mesh: table: 32 (over x, z), rep: 8 (over y, core).
Axes of the slice: x: 4, y: 4, z: 8, core: 2. Of those that a mesh axis runs over, the one named last changes fastest.
Arguments:
- lengths: int32 [256, 2], P(('table', 'rep')), may hold values from 1 to 256, 320 in all within a row
- slots: int32 [512, 256], P(('table', 'rep')), may hold values from 0 to 1023, as said below
- requests: int32 [256, 32, 32], P(('table', 'rep')), may hold values from 0 to 2047, as said below
- counts: int32 [256, 32], P(('table', 'rep')), may hold values from 1 to 32, as said below
- codes: bfloat16 [65536, 256], P('table'), may hold values from -4 to 4
- scales: bfloat16 [65536, 8], P('table'), may hold values from 0.25 to 1
- accum: float32 [65536], P('table'), may hold values from 1 to 64
- conv_weight: bfloat16 [4, 3, 256, 256], replicated, may hold values from -0.21875 to 0.21875
- norm_gain: float32 [4, 256], replicated, may hold values from 0.5 to 1.5
- upstream: bfloat16 [512, 256, 256], P(('table', 'rep')), may hold values from -6 to 6
Outputs:
- new_rows: float32 [65536, 256], P('table')
- new_accum: float32 [65536], P('table')
- grad_conv: float32 [4, 3, 256, 256], replicated
- grad_gain: float32 [4, 256], replicated
Inputs may be any that keep to these rules, and one draw needn't show every extreme that they name: requests[d, p, j] lies in [j * 64, (j + 1) * 64), so one device's requests to one owner are distinct; entries with j >= counts[d, p] are not in use. `counts`: one owner, the same for every device, gets 32 requests from each device. `slots`: every entry is p * 32 + j with j < counts[d, p] of the session's device d.
All inputs are finite; a program needn't handle non-finite values.
Results may differ from a plain program's by a relative error of at most 0.02.
Values may be sent and summed in bfloat16 or wider, within the bound.
No kernel may reach another device: no remote copies, remote signals or barrier semaphores. Data moves between devices by JAX's collectives and lax.ppermute only.
A program may use at most 64 MiB of HBM per device.

v0:
```python
import jax
import jax.numpy as jnp
from jax import lax
from jax.sharding import PartitionSpec as P

DILATIONS = (1, 2, 4, 8)
LEARN_RATE = 0.5


def dequantize(row_codes, row_scales):
    count, channels = row_codes.shape
    groups = row_scales.shape[1]
    spread = row_codes.astype(jnp.float32).reshape(count, groups, channels // groups)
    return (spread * row_scales.astype(jnp.float32)[:, :, None]).reshape(count, channels)


def shift_time(values, offset):
    padded = jnp.pad(values, ((0, 0), (offset, 0), (0, 0)))
    return padded[:, : values.shape[1], :]


def dilated(values, kernel, spread):
    sessions, steps_len, channels = values.shape
    total = jnp.zeros((sessions * steps_len, kernel.shape[2]), jnp.float32)
    for tap in range(kernel.shape[0]):
        moved = shift_time(values, tap * spread).reshape(sessions * steps_len, channels)
        total = total + jnp.dot(moved, kernel[tap], preferred_element_type=jnp.float32)
    return total.reshape(sessions, steps_len, kernel.shape[2])


def normed(values, gain):
    center = values - jnp.mean(values, axis=-1, keepdims=True)
    spread = jnp.mean(center * center, axis=-1, keepdims=True)
    return center * lax.rsqrt(spread + 1e-05) * gain


def stack(inputs, kernels, gains):
    hidden = inputs
    for block_index in range(2):
        lower = 2 * block_index
        first = dilated(hidden, kernels[lower], DILATIONS[lower])
        first = jax.nn.silu(normed(first, gains[lower])).astype(jnp.bfloat16)
        second = dilated(first, kernels[lower + 1], DILATIONS[lower + 1])
        second = jax.nn.silu(normed(second, gains[lower + 1]))
        hidden = (second + hidden.astype(jnp.float32)).astype(jnp.bfloat16)
    return hidden


def embed(fetched, sess_slots, sess_lengths):
    gathered = fetched.astype(jnp.bfloat16)[sess_slots]
    inside = jnp.arange(sess_slots.shape[1], dtype=jnp.int32)[None, :] < sess_lengths[:, None]
    return (jnp.where(inside[:, :, None], gathered, jnp.zeros_like(gathered)), inside)


def slot_sums(input_grad, inside, sess_slots, slot_total):
    channels = input_grad.shape[2]
    masked = input_grad.astype(jnp.float32) * inside[:, :, None].astype(jnp.float32)
    return jax.ops.segment_sum(
        masked.reshape(-1, channels), sess_slots.reshape(-1), num_segments=slot_total
    )


def adagrad(rows_now, accum_now, gradient):
    accum_next = accum_now + jnp.mean(gradient * gradient, axis=1)
    return (rows_now - LEARN_RATE * gradient * lax.rsqrt(accum_next)[:, None], accum_next)


def body(lengths, slots, requests, counts, codes, scales, accum, conv_weight, norm_gain, upstream):
    owners = lax.axis_size("table")
    capacity = requests.shape[2]
    row_count, channels = codes.shape
    outgoing = requests[0]
    outgoing_counts = counts[0][:, None]
    asked, asked_counts = (
        lax.all_to_all(outgoing, "table", split_axis=0, concat_axis=0, tiled=True),
        lax.all_to_all(outgoing_counts, "table", split_axis=0, concat_axis=0, tiled=True),
    )
    filled = jnp.arange(capacity, dtype=jnp.int32)[None, :] < asked_counts
    row_codes = jnp.where(filled[:, :, None], codes[asked], jnp.zeros((), codes.dtype))
    row_scales = jnp.where(filled[:, :, None], scales[asked], jnp.zeros((), scales.dtype))
    got_codes, got_scales = (
        lax.all_to_all(row_codes, "table", split_axis=0, concat_axis=0, tiled=True),
        lax.all_to_all(row_scales, "table", split_axis=0, concat_axis=0, tiled=True),
    )
    fetched = dequantize(
        got_codes.reshape(owners * capacity, channels),
        got_scales.reshape(owners * capacity, scales.shape[1]),
    )
    inputs, inside = embed(fetched, slots, lengths[0])
    cotangent = jnp.where(inside[:, :, None], upstream, jnp.zeros_like(upstream))
    states, pullback = jax.vjp(stack, inputs, conv_weight, norm_gain)
    input_grad, weight_grad, gain_grad = pullback(cotangent)
    grad_conv, grad_gain = lax.psum((weight_grad.astype(jnp.float32), gain_grad), ("table", "rep"))
    slot_grad = slot_sums(input_grad, inside, slots, owners * capacity).astype(jnp.bfloat16)
    returned = lax.all_to_all(
        slot_grad.reshape(owners, capacity, channels),
        "table",
        split_axis=0,
        concat_axis=0,
        tiled=True,
    )
    weighted = returned.astype(jnp.float32) * filled[:, :, None].astype(jnp.float32)
    local_table = (
        jnp.zeros((row_count, channels), jnp.float32)
        .at[asked.reshape(-1)]
        .add(weighted.reshape(-1, channels))
    )
    table_grad = lax.psum(local_table.astype(jnp.bfloat16), "rep").astype(jnp.float32)
    new_rows, new_accum = adagrad(dequantize(codes, scales), accum, table_grad)
    return (new_rows, new_accum, grad_conv, grad_gain)


def solution(mesh):
    return jax.shard_map(
        body,
        mesh=mesh,
        in_specs=(
            P(("table", "rep"), None),
            P(("table", "rep"), None),
            P(("table", "rep"), None, None),
            P(("table", "rep"), None),
            P("table", None),
            P("table", None),
            P("table"),
            P(),
            P(),
            P(("table", "rep"), None, None),
        ),
        out_specs=(P("table", None), P("table"), P(), P()),
        check_vma=False,
    )
```

profile of v0, /device:TPU:1, one launch (start us, length us, event | category | flops | bytes accessed | tf_op | source)
XLA Modules:
  0.0 552.9 jit_solution(18144567519183177569)
XLA Ops:
  8.5 11.9 %all-to-all-start.1 = ((s32[32,1,1]{2,1,0:T(1,128)}), s32[32,1,1]{2,1,0:T(1,128)S(1)}, u32[]{:S(2)}, u32[]{:S(2)}) async-start(s32[32,1,1]{2,1,0:T(1,128)} %copy.144), calls=%async_computation.1 | async-start | bytes 32768 | tf_op jit(solution)/shard_map/all_to_all | solution.py:76
  21.4 7.5 %all-to-all-done.1 = s32[32,1,1]{2,1,0:T(1,128)S(1)} async-done(((s32[32,1,1]{2,1,0:T(1,128)}), s32[32,1,1]{2,1,0:T(1,128)S(1)}, u32[]{:S(2)}, u32[]{:S(2)}) %all-to-all-start.1) | async-done | bytes 160 | tf_op jit(solution)/shard_map/all_to_all | solution.py:76
  28.9 3.8 all-to-all-start
  33.5 7.8 %all-to-all-done = s32[32,1,32]{2,1,0:T(1,128)S(1)} async-done(((s32[32,1,32]{2,1,0:T(1,128)}), s32[32,1,32]{2,1,0:T(1,128)S(1)}, u32[]{:S(2)}, u32[]{:S(2)}) %all-to-all-start) | async-done | bytes 4128 | tf_op jit(solution)/shard_map/all_to_all | solution.py:75
  41.4 3.2 gather_fusion.1
  45.5 3.8 all-to-all-start.3
  49.4 3.9 gather_fusion
  54.4 3.6 all-to-all-done.3
  57.9 5.7 %all-to-all-start.2 = ((bf16[32,32,256]{2,1,0:T(8,128)(2,1)}), bf16[32,32,256]{2,1,0:T(8,128)(2,1)S(1)}, u32[]{:S(2)}, u32[]{:S(2)}) async-start(bf16[32,32,256]{2,1,0:T(8,128)(2,1)} %broadcast_select_fusion), calls=%async_computation.2 | async-start | bytes 1048576 | tf_op jit(solution)/shard_map/all_to_all | solution.py:82
  68.9 1.6 copy.148
  70.5 4.8 all-to-all-done.2
  75.4 2.1 gather_fusion.2
  79.6 1.8 copy.151
  81.4 1.8 copy.152
  87.0 2.2 fusion.49
  91.2 1.8 copy.154
  93.0 1.8 copy.155
  94.8 1.4 convolution_add_fusion.5
  103.7 1.4 fusion.51
  108.1 2.1 fusion.50
  113.1 1.5 convolution_add_fusion.1
  117.9 2.1 multiply_reduce_fusion.3
  119.9 1.4 fusion.112
  123.6 1.9 convolution_convert_fusion.9
  125.4 1.9 convolution_convert_fusion.10
  129.6 1.8 copy.165
  132.2 1.5 multiply_reduce_fusion.6
  134.9 1.9 convolution_convert_fusion.6
  136.7 1.9 convolution_convert_fusion.7
  140.9 1.8 copy.169
  143.5 2.3 multiply_reduce_fusion.1
  146.9 1.9 convolution_convert_fusion.3
  154.1 1.5 multiply_reduce_fusion.4
  156.8 1.9 convolution_convert_fusion
  167.3 4.8 scatter_custom_fusion
  172.1 2.1 convert_element_type.217
  174.2 7.2 %all-to-all-start.4 = ((bf16[32,32,256]{2,1,0:T(8,128)(2,1)}), bf16[32,32,256]{2,1,0:T(8,128)(2,1)}, u32[]{:S(2)}, u32[]{:S(2)}) async-start(bf16[32,32,256]{2,1,0:T(8,128)(2,1)} %bitcast.292), calls=%async_computation.4 | async-start | bytes 1048576 | tf_op jit(solution)/shard_map/all_to_all | solution.py:95
  188.8 4.0 all-to-all-done.4
  192.9 2.2 convert_multiply_fusion.3
  195.1 7.0 %scatter_custom_fusion.1 = f32[2048,256]{1,0:T(8,128)S(1)} fusion(s32[1024]{0:T(1024)} %bitcast.344, f32[1024,256]{1,0:T(8,128)} %bitcast.296, f32[]{:T(128)} %constant.54.clone.1), kind=kCustom, calls=%fused_computation.69 | custom fusion | flops 262144 | bytes 2097664 | tf_op jit(solution)/shard_map/scatter-add | solution.py:106
  205.0 1.9 add_convert_fusion
  207.7 1.6 mul.381
  209.3 1.9 copy.142
  211.3 81.5 %psum.23 = f32[4,256]{1,0:T(4,128)} all-reduce(f32[4,256]{1,0:T(4,128)S(1)} %pad_add_fusion), channel_id=1, replica_groups=mesh['table'=32,'rep'=8] {'table','rep'}, use_global_device_ids=true, to_apply=%region_25.26 | all-reduce | flops 1024 | bytes 8192 | tf_op jit(solution)/shard_map/psum | solution.py:93
  292.7 1.7 fusion
  295.0 1.8 fusion.1
  296.8 245.4 %all-reduce.41.cloned.1.call-done = f32[4,3,256,256]{3,2,1,0:T(8,128)} async-done(((f32[4,3,256,256]{3,2,1,0:T(8,128)}), f32[4,3,256,256]{3,2,1,0:T(8,128)}) %all-reduce.41.cloned.1.call-update) | async-done | bytes 3145744 | tf_op jit(solution)/shard_map/psum | solution.py:93
  542.3 3.8 copy.208
  (216 shorter events, 71.9 us)
Async XLA Ops:
  8.5 20.4 %all-to-all-start.1 = ((s32[32,1,1]{2,1,0:T(1,128)}), s32[32,1,1]{2,1,0:T(1,128)S(1)}, u32[]{:S(2)}, u32[]{:S(2)}) async-start(s32[32,1,1]{2,1,0:T(1,128)} %copy.144), calls=%async_computation.1 | async-start | bytes 32768 | tf_op jit(solution)/shard_map/all_to_all | solution.py:76
  21.4 28.0 %copy-start = (bf16[2048,256]{1,0:T(8,128)(2,1)S(1)}, bf16[2048,256]{1,0:T(8,128)(2,1)}, u32[]{:S(2)}) copy-start(bf16[2048,256]{1,0:T(8,128)(2,1)} %param.14) | copy-start | bytes 3145732
  28.9 12.4 %all-to-all-start = ((s32[32,1,32]{2,1,0:T(1,128)}), s32[32,1,32]{2,1,0:T(1,128)S(1)}, u32[]{:S(2)}, u32[]{:S(2)}) async-start(s32[32,1,32]{2,1,0:T(1,128)} %bitcast.336), calls=%async_computation | async-start | bytes 32768 | tf_op jit(solution)/shard_map/all_to_all | solution.py:75
  45.5 12.4 %all-to-all-start.3 = ((bf16[32,2,128]{2,1,0:T(2,128)(2,1)}), bf16[32,2,128]{2,1,0:T(2,128)(2,1)S(1)}, u32[]{:S(2)}, u32[]{:S(2)}) async-start(bf16[32,2,128]{2,1,0:T(2,128)(2,1)} %reshape.647), calls=%async_computation.3 | async-start | bytes 32768 | tf_op jit(solution)/shard_map/all_to_all | solution.py:83
  53.3 10.3 %copy-start.32 = (s32[2,256]{1,0:T(2,128)S(1)}, s32[2,256]{1,0:T(2,128)}, u32[]{:S(2)}) copy-start(s32[2,256]{1,0:T(2,128)} %param.11) | copy-start | bytes 6148
  53.3 10.9 %copy-start.39 = (s32[1,2]{1,0:T(1,128)S(1)}, s32[1,2]{1,0:T(1,128)}, u32[]{:S(2)}) copy-start(s32[1,2]{1,0:T(1,128)} %param.10) | copy-start | bytes 28
  53.4 11.5 %copy-start.30 = (bf16[2,256,256]{2,1,0:T(8,128)(2,1)S(1)}, bf16[2,256,256]{2,1,0:T(8,128)(2,1)}, u32[]{:S(2)}) copy-start(bf16[2,256,256]{2,1,0:T(8,128)(2,1)} %param.19) | copy-start | bytes 786436
  53.4 12.3 %copy-start.36 = (f32[4,256]{1,0:T(4,128)S(1)}, f32[4,256]{1,0:T(4,128)}, u32[]{:S(2)}) copy-start(f32[4,256]{1,0:T(4,128)} %param.18) | copy-start | bytes 12292
  57.9 17.3 %all-to-all-start.2 = ((bf16[32,32,256]{2,1,0:T(8,128)(2,1)}), bf16[32,32,256]{2,1,0:T(8,128)(2,1)S(1)}, u32[]{:S(2)}, u32[]{:S(2)}) async-start(bf16[32,32,256]{2,1,0:T(8,128)(2,1)} %broadcast_select_fusion), calls=%async_computation.2 | async-start | bytes 1048576 | tf_op jit(solution)/shard_map/all_to_all | solution.py:82
  77.6 0.7 copy-start.24
  78.4 5.0 copy-start.17
  78.4 4.8 copy-start.12
  83.2 1.4 copy-start.21
  85.0 0.8 copy-start.14
  89.5 0.7 copy-start.1
  94.8 1.4 copy-start.22
  99.8 4.0 copy-start.13
  101.1 0.7 copy-start.5
  103.7 1.5 copy-start.20
  105.2 1.2 copy-start.19
  110.4 0.7 copy-start.7
  113.1 1.5 copy-start.23
  115.8 0.8 copy-start.15
  117.9 3.5 copy-start.3
  136.7 6.8 %copy-start.4 = (bf16[2,256,256]{1,2,0:T(8,128)(2,1)S(1)}, bf16[2,256,256]{1,2,0:T(8,128)(2,1)}, u32[]{:S(2)}) copy-start(bf16[2,256,256]{1,2,0:T(8,128)(2,1)} %copy.143) | copy-start | bytes 786436
  156.8 5.5 copy-start.2
  161.0 2.2 copy-start.18
  172.1 10.3 %copy-start.6 = (bf16[2,256,256]{1,2,0:T(8,128)(2,1)S(1)}, bf16[2,256,256]{1,2,0:T(8,128)(2,1)}, u32[]{:S(2)}) copy-start(bf16[2,256,256]{1,2,0:T(8,128)(2,1)} %copy-done.5) | copy-start | bytes 786436
  174.2 10.1 %copy-start.8 = (bf16[2,256,256]{1,2,0:T(8,128)(2,1)S(1)}, bf16[2,256,256]{1,2,0:T(8,128)(2,1)}, u32[]{:S(2)}) copy-start(bf16[2,256,256]{1,2,0:T(8,128)(2,1)} %copy-done.7) | copy-start | bytes 786436
  174.2 10.1 %copy-start.10 = (bf16[2,256,256]{1,2,0:T(8,128)(2,1)S(1)}, bf16[2,256,256]{1,2,0:T(8,128)(2,1)}, u32[]{:S(2)}) copy-start(bf16[2,256,256]{1,2,0:T(8,128)(2,1)} %broadcast_add_fusion.3) | copy-start | bytes 786436
  174.2 18.7 %all-to-all-start.4 = ((bf16[32,32,256]{2,1,0:T(8,128)(2,1)}), bf16[32,32,256]{2,1,0:T(8,128)(2,1)}, u32[]{:S(2)}, u32[]{:S(2)}) async-start(bf16[32,32,256]{2,1,0:T(8,128)(2,1)} %bitcast.292), calls=%async_computation.4 | async-start | bytes 1048576 | tf_op jit(solution)/shard_map/all_to_all | solution.py:95
  181.4 111.4 %all-reduce.39.cloned.1.call-start = ((), (), s32[]{:S(2)}) async-start(), calls=%async_computation.5 | async-start | bytes 2097152 | tf_op jit(solution)/shard_map/psum | solution.py:108
  203.2 1.4 copy-start.9
  203.2 1.4 copy-start.11
  203.2 1.7 copy-start.25
  203.2 1.7 copy-start.26
  203.2 1.7 copy-start.27
  203.2 1.7 copy-start.28
  203.2 1.7 copy-start.29
  203.3 339.0 %all-reduce.41.cloned.1.call-start = ((), (), s32[]{:S(2)}) async-start(), calls=%async_computation.6 | async-start | bytes 6291456 | tf_op jit(solution)/shard_map/psum | solution.py:93
  206.9 0.8 copy-start.31
  209.2 2.0 copy-start.34
  209.2 2.0 copy-start.35
  209.2 2.0 copy-start.37
  209.2 2.0 copy-start.38
  209.2 85.1 %copy-start.33 = (f32[2048]{0:T(1024)S(1)}, f32[2048]{0:T(1024)}, u32[]{:S(2)}) copy-start(f32[2048]{0:T(1024)} %param.16) | copy-start | bytes 24580
  292.7 2.3 copy-start.16
Sparse Core Ops, SparseCore 0:
  203.4 68.7 all-reduce.38
  278.2 264.0 all-reduce.40
where the time goes:
time: 556 us; the launch traced here: 553 us
  waiting for transfers between devices  273 us (49%)
  blocking collectives  81.5 us (15%)
  local copies, waits for them, and re-layouts  61.5 us (11%)
  other arithmetic  46.3 us (8%)
  matrix products  43 us (8%)
  starting transfers between devices  32.5 us (6%)
  between operations  15 us (3%)
    psum x1, waiting for transfers between devices, body(): lax.psum((weight_grad.astype(jnp.float32), gain_grad), ('table', 'rep'))  245 us
    psum x1, blocking collectives, body(): lax.psum((weight_grad.astype(jnp.float32), gain_grad), ('table', 'rep'))  81.5 us
    dot_general x36, matrix products, dilated(): jnp.dot(moved, kernel[tap], preferred_element_type=jnp.float32)  43 us
    slice x12, local copies, waits for them, and re-layouts, shift_time(): return padded[:, :values.shape[1], :]  13 us
    reshape x12, local copies, waits for them, and re-layouts, dilated(): shift_time(values, tap * spread).reshape(sessions * steps_len, channels)  12.2 us
    all_to_all x1, starting transfers between devices, body(): lax.all_to_all(outgoing_counts, 'table', split_axis=0, concat_axis=0, til...  11.9 us
    unnamed x87, local copies, waits for them, and re-layouts  11.8 us
  transfers between devices with their start and end apart: 7, of which 6 were waited for; matrix products, arithmetic and copies ran while one was open for 6% of the time, Pallas kernels for 0%

commit v1 on v0

v1 whole, which is shorter than its diff:
```python
import functools

import jax
import jax.numpy as jnp
from jax import lax
from jax.experimental import pallas as pl
from jax.experimental.pallas import tpu as pltpu
from jax.sharding import Mesh
from jax.sharding import PartitionSpec as P

DILATIONS = (1, 2, 4, 8)
LEARN_RATE = 0.5
BF = jnp.bfloat16
F32 = jnp.float32
LAYERS, TAPS, C = 4, 3, 256
GROUP = 32
LEN = 256
PACKED = 320
STEP = 64
PIECE = 96
TAIL = 8
SLAB = PIECE + TAIL
NT = (((1,), (1,)), ((), ()))
TN = (((0,), (0,)), ((), ()))
PARAMS = pltpu.CompilerParams(vmem_limit_bytes=40 * 1024 * 1024)
SMEM = pl.BlockSpec(memory_space=pltpu.SMEM)
VMEM = pl.BlockSpec(memory_space=pltpu.VMEM)


def call(kernel, outs, args, scalars=0, scratch=(), flops=0):
    specs = [SMEM] * scalars + [VMEM] * (len(args) - scalars)
    return pl.pallas_call(
        kernel,
        out_shape=outs,
        in_specs=specs,
        out_specs=jax.tree.map(lambda _: VMEM, outs),
        scratch_shapes=list(scratch),
        compiler_params=PARAMS,
        cost_estimate=pl.CostEstimate(flops=flops, bytes_accessed=1 << 20, transcendentals=0),
    )(*args)


def shape(dims, dtype):
    return jax.ShapeDtypeStruct(dims, dtype)


def iota(dims, axis):
    return lax.broadcasted_iota(jnp.int32, dims, axis)


def dequantize_kernel(codes_ref, scales_ref, wide_ref, narrow_ref):
    groups = scales_ref.shape[1]
    spread = (iota((groups, C), 1) // GROUP == iota((groups, C), 0)).astype(F32).astype(BF)
    rows = codes_ref.shape[0]
    for start in range(0, rows, 256):
        part = pl.ds(start, 256)
        scale = jnp.dot(scales_ref[part, :], spread, preferred_element_type=F32)
        wide = codes_ref[part, :].astype(F32) * scale
        wide_ref[part, :] = wide
        narrow_ref[part, :] = wide.astype(BF)


def fetch_kernel(asked_ref, table_ref, out_ref):
    senders, cap = asked_ref.shape
    rows = table_ref.shape[0]
    stride = rows // cap
    asked = asked_ref[...].astype(F32).astype(BF)
    part = 256
    for start in range(0, senders * cap, part):
        line = iota((part, senders), 0) + start
        pick = (line // cap == iota((part, senders), 1)).astype(F32).astype(BF)
        lists = jnp.dot(pick, asked, preferred_element_type=F32)
        entry = (iota((part, cap), 0) + start) % cap
        own = jnp.where(entry == iota((part, cap), 1), lists, 0.0)
        offset = jnp.sum(own, axis=1, keepdims=True).astype(jnp.int32)
        entry = (iota((part, 1), 0) + start) % cap
        target = jnp.where(offset >= 0, entry * stride + offset, -1)
        chosen = (iota((part, rows), 1) == target).astype(F32).astype(BF)
        got = jnp.dot(chosen, table_ref[...], preferred_element_type=F32)
        out_ref[pl.ds(start, part), :] = got.astype(BF)


def sigmoid(values):
    return 0.5 + 0.5 * jnp.tanh(0.5 * values)


def train_kernel(
    place_ref,
    slot_col_ref,
    slot_row_ref,
    fetched_ref,
    weight_ref,
    gain_ref,
    upstream_ref,
    slot_grad_ref,
    keep_ref,
    send_ref,
    held_ref,
    conv_ref,
    unit_ref,
    scale_ref,
    grad_ref,
    wide_ref,
    weight_grad_ref,
):
    split, x, y, core = place_ref[0], place_ref[1], place_ref[2], place_ref[3]
    steps = range(0, PACKED, STEP)
    line = iota((PACKED, C), 0)
    since = jnp.where(line >= split, line - split, line)
    until = jnp.where(line >= split, PACKED - line, split - line)

    slots = fetched_ref.shape[0]
    chosen = (iota((PACKED, slots), 1) == slot_col_ref[...]).astype(F32).astype(BF)
    first = jnp.dot(chosen, fetched_ref[...], preferred_element_type=F32)
    held_ref[0] = first.astype(BF)

    for layer in range(LAYERS):
        gap = DILATIONS[layer]
        now = held_ref[layer].astype(F32)
        taps = [held_ref[layer]]
        for tap in (1, 2):
            moved = pltpu.roll(now, tap * gap, 0)
            taps.append(jnp.where(since >= tap * gap, moved, 0.0).astype(BF))
        base = layer * TAPS * C
        conv_ref[...] = jnp.dot(
            jnp.concatenate(taps, axis=1),
            weight_ref[pl.ds(base, TAPS * C), :],
            preferred_element_type=F32,
        )
        gain = gain_ref[pl.ds(layer, 1), :]
        for start in steps:
            part = pl.ds(start, STEP)
            value = conv_ref[part, :]
            center = value - jnp.mean(value, axis=1, keepdims=True)
            spread = jnp.mean(center * center, axis=1, keepdims=True)
            scale = lax.rsqrt(spread + 1e-5)
            unit = center * scale
            unit_ref[layer, part, :] = unit
            scale_ref[layer, part, :] = jnp.broadcast_to(scale, (STEP, 128))
            if layer + 1 < LAYERS:
                gained = unit * gain
                after = gained * sigmoid(gained)
                if layer % 2 == 1:
                    after = after + held_ref[layer - 1, part, :].astype(F32)
                held_ref[layer + 1, part, :] = after.astype(BF)

    source = iota((PACKED, 1), 0)
    source = jnp.where(source >= split, source + (LEN - split), source)
    packer = (iota((PACKED, 2 * LEN), 1) == source).astype(F32).astype(BF)
    grad_ref[...] = jnp.dot(packer, upstream_ref[...], preferred_element_type=F32)

    gain_rows = [None] * LAYERS
    for layer in reversed(range(LAYERS)):
        gap = DILATIONS[layer]
        gain = gain_ref[pl.ds(layer, 1), :]
        total = jnp.zeros((8, C), F32)
        for start in steps:
            part = pl.ds(start, STEP)
            unit = unit_ref[layer, part, :]
            scale = scale_ref[layer, part, :]
            gained = unit * gain
            gate = sigmoid(gained)
            inner = grad_ref[part, :] * (gate * (1.0 + gained * (1.0 - gate)))
            total = total + jnp.sum((inner * unit).reshape(STEP // 8, 8, C), axis=0)
            inner = inner * gain
            mean = jnp.mean(inner, axis=1, keepdims=True)
            slope = jnp.mean(inner * unit, axis=1, keepdims=True)
            outer = inner - mean - unit * slope
            conv_ref[part, :] = outer * jnp.concatenate([scale, scale], axis=1)
        gain_rows[layer] = jnp.sum(total, axis=0, keepdims=True)
        now = conv_ref[...]
        wide_ref[:, 0:C] = now.astype(BF)
        for tap in (1, 2):
            moved = pltpu.roll(now, PACKED - tap * gap, 0)
            moved = jnp.where(until > tap * gap, moved, 0.0)
            wide_ref[:, tap * C : (tap + 1) * C] = moved.astype(BF)

        below = jnp.zeros((PACKED, C), F32)
        for tap in range(TAPS):
            kernel = weight_ref[pl.ds((layer * TAPS + tap) * C, C), :]
            below = below + lax.dot_general(
                wide_ref[:, tap * C : (tap + 1) * C], kernel, NT, preferred_element_type=F32
            )
        if layer % 2 == 0:
            if layer == 2:
                skip = jnp.dot(packer, upstream_ref[...], preferred_element_type=F32)
            else:
                skip = held_ref[4].astype(F32)
            below = below + skip
        rounded = below.astype(BF)
        grad_ref[...] = rounded.astype(F32)
        if layer == 2:
            held_ref[4] = rounded

        weight_grad = lax.dot_general(
            held_ref[layer], wide_ref[...], TN, preferred_element_type=F32
        )
        for tap in range(TAPS):
            weight_grad_ref[pl.ds(tap * C, C), :] = weight_grad[:, tap * C : (tap + 1) * C]

        for pair in range(4):
            even = weight_grad_ref[pl.ds(2 * pair * PIECE, PIECE), :]
            odd = weight_grad_ref[pl.ds((2 * pair + 1) * PIECE, PIECE), :]
            tail = jnp.zeros((TAIL, C), F32)
            even_tail = tail
            if layer == 0 and pair == 0:
                exact = jnp.concatenate(gain_rows + gain_rows, axis=0)
                high = exact.astype(BF).astype(F32)
                even_tail = jnp.where(iota((TAIL, C), 0) < LAYERS, high, exact - high)
            even = jnp.concatenate([even, even_tail], axis=0)
            odd = jnp.concatenate([odd, tail], axis=0)
            place = ((layer - x + 4) % 4) * 4 + (pair - y + 4) % 4
            keep_ref[place] = jnp.where(core == 0, even, odd).astype(BF)
            send_ref[place] = jnp.where(core == 0, odd, even).astype(BF)

    mine = grad_ref[...].astype(BF)
    for start in range(0, slots, 256):
        here = iota((256, PACKED), 0) + start == slot_row_ref[...]
        here = here.astype(F32).astype(BF)
        summed = jnp.dot(here, mine, preferred_element_type=F32)
        slot_grad_ref[pl.ds(start, 256), :] = summed.astype(BF)


def settle(total):
    tail = total[PIECE:SLAB, :]
    exact = tail + pltpu.roll(tail, LAYERS, 0)
    high = exact.astype(BF).astype(F32)
    tail = jnp.where(iota((TAIL, C), 0) < LAYERS, high, exact - high)
    return jnp.concatenate([total[:PIECE, :], tail], axis=0).astype(BF)


def core_sum_kernel(keep_ref, got_ref, *out_refs):
    for at in range(16):
        total = keep_ref[at].astype(F32) + got_ref[at].astype(F32)
        out_refs[at // 4][at % 4] = settle(total)


def four_sum_kernel(a_ref, b_ref, c_ref, d_ref, *out_refs):
    for at in range(a_ref.shape[0]):
        left = a_ref[at].astype(F32) + b_ref[at].astype(F32)
        right = c_ref[at].astype(F32) + d_ref[at].astype(F32)
        out_refs[at][0] = settle(left + right)


def two_sum_kernel(a_ref, b_ref, out_ref):
    out_ref[0] = settle(a_ref[0].astype(F32) + b_ref[0].astype(F32))


def spread_kernel(place_ref, *refs):
    blocks, conv_ref, gain_ref = refs[:8], refs[8], refs[9]
    x, y, core = place_ref[1], place_ref[2], place_ref[3]
    for at in range(8):
        layer = (x + at % 4) % 4
        side = core if at < 4 else 1 - core
        for inner in range(4):
            number = layer * 8 + ((y + inner) % 4) * 2 + side
            block = blocks[at][inner].astype(F32)
            conv_ref[pl.ds(pl.multiple_of(number * PIECE, PIECE), PIECE), :] = block[:PIECE, :]

            @pl.when(number == 0)
            def _():
                tail = block[PIECE:, :]
                gain_ref[...] = (tail + pltpu.roll(tail, LAYERS, 0))[:LAYERS, :]


def scatter_kernel(place_ref, asked_ref, got_ref, keep_ref, send_ref):
    y, core = place_ref[2], place_ref[3]
    lines = asked_ref.shape[1]
    for pair in range(4):
        parts = []
        for side in range(2):
            row = iota((256, lines), 0) + (2 * pair + side) * 256
            here = (row == asked_ref[...]).astype(F32).astype(BF)
            parts.append(jnp.dot(here, got_ref[...], preferred_element_type=F32))
        even, odd = parts
        place = (pair - y + 4) % 4
        keep_ref[place] = jnp.where(core == 0, even, odd).astype(BF)
        send_ref[place] = jnp.where(core == 0, odd, even).astype(BF)


def row_core_sum_kernel(keep_ref, got_ref, *out_refs):
    for at in range(4):
        out_refs[at][...] = (keep_ref[at].astype(F32) + got_ref[at].astype(F32)).astype(BF)


def row_four_sum_kernel(a_ref, b_ref, c_ref, d_ref, out_ref):
    left = a_ref[...].astype(F32) + b_ref[...].astype(F32)
    right = c_ref[...].astype(F32) + d_ref[...].astype(F32)
    out_ref[...] = (left + right).astype(BF)


def adagrad_kernel(place_ref, *refs):
    blocks, table_ref, accum_ref, rows_ref, next_ref = refs[:8], *refs[8:]
    y, core = place_ref[2], place_ref[3]
    for at in range(8):
        side = core if at < 4 else 1 - core
        number = ((y + at % 4) % 4) * 2 + side
        part = pl.ds(pl.multiple_of(number * 256, 256), 256)
        gradient = blocks[at][...].astype(F32)
        grown = accum_ref[part, :] + jnp.mean(gradient * gradient, axis=1, keepdims=True)
        next_ref[part, :] = grown
        rows_ref[part, :] = table_ref[part, :] - LEARN_RATE * gradient * lax.rsqrt(grown)


def shifted(values, axis, size, offset):
    return lax.ppermute(values, axis, [(i, (i + offset) % size) for i in range(size)])


def crossed(values, axis, size, bits):
    return lax.ppermute(values, axis, [(i, i ^ bits) for i in range(size)])


def body(lengths, slots, requests, counts, codes, scales, accum, conv_weight, norm_gain, upstream):
    table_axes = ("x", "z")
    owners = requests.shape[1]
    cap = requests.shape[2]
    rows = codes.shape[0]
    stride = rows // cap
    split = lengths[0, 0]
    place = jnp.stack(
        [split, lax.axis_index("x"), lax.axis_index("y"), lax.axis_index("core")]
    ).astype(jnp.int32)

    entry = jnp.arange(cap, dtype=jnp.int32)[None, :]
    wanted = jnp.where(entry < counts[0][:, None], requests[0] - entry * stride, -1)
    asked = lax.all_to_all(wanted, table_axes, split_axis=0, concat_axis=0, tiled=True)

    wide, narrow = call(
        dequantize_kernel,
        [shape((rows, C), F32), shape((rows, C), BF)],
        [codes, scales],
        flops=1 << 24,
    )
    order = jnp.arange(PACKED, dtype=jnp.int32)
    order = order + jnp.where(order >= split, LEN - split, 0)
    match = order[:, None] == jnp.arange(2 * LEN, dtype=jnp.int32)[None, :]
    packed = jnp.sum(jnp.where(match, slots.reshape(1, 2 * LEN), 0), axis=1)

    sending = call(fetch_kernel, shape((owners * cap, C), BF), [asked, narrow], flops=1 << 30)
    fetched = lax.all_to_all(
        sending.reshape(owners, cap, C), table_axes, split_axis=0, concat_axis=0, tiled=True
    ).reshape(owners * cap, C)

    slab16 = shape((16, SLAB, C), BF)
    slot_grad, keep, send = call(
        train_kernel,
        [shape((owners * cap, C), BF), slab16, slab16],
        [
            place,
            packed.reshape(PACKED, 1),
            packed.reshape(1, PACKED),
            fetched,
            conv_weight.reshape(LAYERS * TAPS * C, C),
            norm_gain,
            upstream.reshape(2 * LEN, C),
        ],
        scalars=1,
        scratch=[
            pltpu.VMEM((LAYERS + 1, PACKED, C), BF),
            pltpu.VMEM((PACKED, C), F32),
            pltpu.VMEM((LAYERS, PACKED, C), F32),
            pltpu.VMEM((LAYERS, PACKED, 128), F32),
            pltpu.VMEM((PACKED, C), F32),
            pltpu.VMEM((PACKED, TAPS * C), BF),
            pltpu.VMEM((TAPS * C, C), F32),
        ],
        flops=1 << 32,
    )

    got = crossed(send, "core", 2, 1)
    returned = lax.all_to_all(
        slot_grad.reshape(owners, cap, C), table_axes, split_axis=0, concat_axis=0, tiled=True
    ).reshape(owners * cap, C)

    slab4, slab1 = shape((4, SLAB, C), BF), shape((1, SLAB, C), BF)
    parts = call(core_sum_kernel, [slab4] * 4, [keep, got])
    parts = [parts[0]] + [shifted(parts[k], "x", 4, k) for k in (1, 2, 3)]
    parts = call(four_sum_kernel, [slab1] * 4, parts)
    parts = [parts[0]] + [shifted(parts[k], "y", 4, k) for k in (1, 2, 3)]
    (part,) = call(four_sum_kernel, [slab1], parts)
    (part,) = call(
        four_sum_kernel, [slab1], [part] + [crossed(part, "z", 8, k) for k in (1, 2, 3)]
    )
    part = call(two_sum_kernel, slab1, [part, crossed(part, "z", 8, 4)])
    parts = jnp.concatenate([part] + [shifted(part, "y", 4, -k) for k in (1, 2, 3)], axis=0)
    parts = [parts] + [shifted(parts, "x", 4, -k) for k in (1, 2, 3)]
    parts = parts + [crossed(part, "core", 2, 1) for part in parts]
    grad_conv, grad_gain = call(
        spread_kernel,
        [shape((LAYERS * TAPS * C, C), F32), shape((LAYERS, C), F32)],
        [place] + parts,
        scalars=1,
    )

    target = jnp.where(asked >= 0, asked + entry * stride, -1).reshape(1, owners * cap)
    block4, block1 = shape((4, 256, C), BF), shape((256, C), BF)
    keep_rows, send_rows = call(
        scatter_kernel, [block4, block4], [place, target, returned], scalars=1, flops=1 << 30
    )
    got_rows = crossed(send_rows, "core", 2, 1)
    sums = call(row_core_sum_kernel, [block1] * 4, [keep_rows, got_rows])
    sums = [sums[0]] + [shifted(sums[k], "y", 4, k) for k in (1, 2, 3)]
    mine = call(row_four_sum_kernel, block1, sums)
    blocks = [mine] + [shifted(mine, "y", 4, -k) for k in (1, 2, 3)]
    blocks = blocks + [crossed(block, "core", 2, 1) for block in blocks]
    new_rows, new_accum = call(
        adagrad_kernel,
        [shape((rows, C), F32), shape((rows, 1), F32)],
        [place] + blocks + [wide, accum.reshape(rows, 1)],
        scalars=1,
    )
    return (
        new_rows,
        new_accum.reshape(rows),
        grad_conv.reshape(conv_weight.shape),
        grad_gain,
    )


def solution(mesh):
    fine = Mesh(mesh.devices.reshape(4, 8, 4, 2), ("x", "z", "y", "core"))
    every = ("x", "z", "y", "core")
    table = ("x", "z")
    return jax.shard_map(
        body,
        mesh=fine,
        in_specs=(
            P(every, None),
            P(every, None),
            P(every, None, None),
            P(every, None),
            P(table, None),
            P(table, None),
            P(table),
            P(),
            P(),
            P(every, None, None),
        ),
        out_specs=(P(table, None), P(table), P(), P()),
        check_vma=False,
    )
```

time: 556 us -> 161 us (0.29)
  waiting for transfers between devices: 273 us -> 39.6 us
  blocking collectives: 81.5 us -> 0 us
  starting transfers between devices: 32.5 us -> 76.9 us
  local copies, waits for them, and re-layouts: 61.5 us -> 18 us
  matrix products: 43 us -> 0 us
  other arithmetic: 46.3 us -> 4.7 us
  Pallas kernels: 0 us -> 19.7 us
  between operations: 15 us -> 0.93 us
    psum x2 -> x0, waiting for transfers between devices: 245 us -> none  [the longest x1 245 us: body(): lax.psum((weight_grad.astype(jnp.float32), gain_grad), ('table', 'rep'))]
    psum x1 -> x0, blocking collectives: 81.5 us -> none  [body(): lax.psum((weight_grad.astype(jnp.float32), gain_grad), ('table', 'rep'))]
    ppermute x0 -> x32, starting transfers between devices: none -> 55.7 us  [the longest x14 29.4 us: crossed(): return lax.ppermute(values, axis, [(i, i ^ bits) for i in range(size)])]
    dot_general x36 -> x0, matrix products: 43 us -> none  [dilated(): jnp.dot(moved, kernel[tap], preferred_element_type=jnp.float32)]
    pallas_call x0 -> x13, Pallas kernels: none -> 19.7 us  [call(): pl.pallas_call(kernel, out_shape=outs, in_specs=specs, out_specs=jax.tree...]
    ppermute x0 -> x32, waiting for transfers between devices: none -> 16.6 us  [the longest x18 9.53 us: shifted(): lax.ppermute(values, axis, [(i, (i + offset) % size) for i in range(size)])]
    reshape x17 -> x3, local copies, waits for them, and re-layouts: 16.2 us -> 1.15 us  [the longest x1 0.78 us: body(): packed.reshape(PACKED, 1)]
    reduce_sum x13 -> x1, other arithmetic: 14.5 us -> 0.23 us  [body(): packed = jnp.sum(jnp.where(match, slots.reshape(1, 2 * LEN), 0), axis=1)]
  transfers between devices with their start and end apart: 7 -> 35, of which waited for: 6 -> 13; matrix products, arithmetic and copies ran while one was open for 6% -> 2% of each run, Pallas kernels for 0% -> 5%
where the time goes in v1:
time: 161 us; the launch traced here: 160 us
  starting transfers between devices  76.9 us (48%)
  waiting for transfers between devices  39.6 us (25%)
  Pallas kernels  19.7 us (12%)
  local copies, waits for them, and re-layouts  18 us (11%)
  other arithmetic  4.7 us (3%)
    ppermute x14, starting transfers between devices, crossed(): return lax.ppermute(values, axis, [(i, i ^ bits) for i in range(size)])  29.4 us
    ppermute x18, starting transfers between devices, shifted(): lax.ppermute(values, axis, [(i, (i + offset) % size) for i in range(size)])  26.3 us
    pallas_call x13, Pallas kernels, call(): pl.pallas_call(kernel, out_shape=outs, in_specs=specs, out_specs=jax.tree...  19.7 us
    unnamed x48, local copies, waits for them, and re-layouts  16.2 us
    all_to_all x1, waiting for transfers between devices, body(): lax.all_to_all(sending.reshape(owners, cap, C), table_axes, split_axis=0,...  12.2 us
    all_to_all x1, starting transfers between devices, body(): lax.all_to_all(wanted, table_axes, split_axis=0, concat_axis=0, tiled=True)  11.9 us
    ppermute x18, waiting for transfers between devices, shifted(): lax.ppermute(values, axis, [(i, (i + offset) % size) for i in range(size)])  9.53 us
    ppermute x14, waiting for transfers between devices, crossed(): return lax.ppermute(values, axis, [(i, i ^ bits) for i in range(size)])  7.07 us
  transfers between devices with their start and end apart: 35, of which 13 were waited for; matrix products, arithmetic and copies ran while one was open for 2% of the time, Pallas kernels for 5%

profile of v1, /device:TPU:1, one launch (start us, length us, event | category | flops | bytes accessed | tf_op | source)
XLA Modules:
  0.0 159.8 jit_solution(17833245412286610206)
XLA Ops:
  0.6 1.4 compare_select_fusion
  2.1 11.9 %all-to-all-start = ((s32[32,1,32]{2,1,0:T(1,128)}), s32[32,1,32]{2,1,0:T(1,128)S(1)}, u32[]{:S(2)}, u32[]{:S(2)}) async-start(s32[32,1,32]{2,1,0:T(1,128)} %compare_select_fusion), calls=%async_computation | async-start | bytes 32768 | tf_op jit(solution)/shard_map/all_to_all | solution.py:326
  15.0 1.2 copy-done
  17.6 4.9 %all-to-all-done = s32[32,1,32]{2,1,0:T(1,128)S(1)} async-done(((s32[32,1,32]{2,1,0:T(1,128)}), s32[32,1,32]{2,1,0:T(1,128)S(1)}, u32[]{:S(2)}, u32[]{:S(2)}) %all-to-all-start) | async-done | bytes 4128 | tf_op jit(solution)/shard_map/all_to_all | solution.py:326
  22.5 1.2 copy-done.17
  23.7 2.5 %shard_map.130 = bf16[1024,256]{1,0:T(8,128)(2,1)} custom-call(s32[32,32]{1,0:T(8,128)S(1)} %bitcast.21, bf16[2048,256]{1,0:T(8,128)(2,1)S(1)} %copy-done.17), custom_call_target="tpu_custom_call" | custom-call | flops 1073741824 | bytes 1048576 | tf_op jit(solution)/shard_map/pallas_call | solution.py:32
  26.2 4.3 %all-to-all-start.1 = ((bf16[32,32,256]{2,1,0:T(8,128)(2,1)}), bf16[32,32,256]{2,1,0:T(8,128)(2,1)S(1)}, u32[]{:S(2)}, u32[]{:S(2)}) async-start(bf16[32,32,256]{2,1,0:T(8,128)(2,1)} %bitcast.8), calls=%async_computation.1 | async-start | bytes 1048576 | tf_op jit(solution)/shard_map/all_to_all | solution.py:340
  31.7 12.2 %all-to-all-done.1 = bf16[32,32,256]{2,1,0:T(8,128)(2,1)S(1)} async-done(((bf16[32,32,256]{2,1,0:T(8,128)(2,1)}), bf16[32,32,256]{2,1,0:T(8,128)(2,1)S(1)}, u32[]{:S(2)}, u32[]{:S(2)}) %all-to-all-start.1) | async-done | bytes 524320 | tf_op jit(solution)/shard_map/all_to_all | solution.py:340
  44.9 1.4 copy-done.15
  47.2 6.3 %shard_map.131 = (bf16[1024,256]{1,0:T(8,128)(2,1)}, bf16[16,104,256]{2,1,0:T(8,128)(2,1)S(1)}, bf16[16,104,256]{2,1,0:T(8,128)(2,1)}) custom-call(s32[4]{0:T(128)S(1)} %pad_add_fusion.place_ref, s32[320,1]{1,0:T(8,128)S(1)} %copy-done.14, s32[1,320]{1,0:T(1,128)S(1)} %reshape.159.slot_row_ref, bf16[1024,256]{1,0:T(8,128)(2,1)S(1)} %bitcast.20, ...), custom_call_target="tpu_custom_call" | custom-call | flops 4294967296 | bytes 1048576 | tf_op jit(solution)/shard_map/pallas_call | solution.py:32
  53.5 4.8 %collective-permute-start.11 = (bf16[16,104,256]{2,1,0:T(8,128)(2,1)}, bf16[16,104,256]{2,1,0:T(8,128)(2,1)}, u32[]{:S(2)}, u32[]{:S(2)}) collective-permute-start(bf16[16,104,256]{2,1,0:T(8,128)(2,1)} %get-tuple-element.39), channel_id=1, source_target_pairs={{0,1},{1,0},{2,3},{3,2},{4,5},{5,4},{6,7},{7,6},{8,9},{9,8},{10,11... | collective-permute-start | bytes 2555912 | tf_op jit(solution)/shard_map/ppermute | solution.py:310
  58.3 5.0 %all-to-all-start.2 = ((bf16[32,32,256]{2,1,0:T(8,128)(2,1)}), bf16[32,32,256]{2,1,0:T(8,128)(2,1)S(1)}, u32[]{:S(2)}, u32[]{:S(2)}) async-start(bf16[32,32,256]{2,1,0:T(8,128)(2,1)} %bitcast.12), calls=%async_computation.2 | async-start | bytes 1048576 | tf_op jit(solution)/shard_map/all_to_all | solution.py:371
  64.6 2.1 %shard_map.136 = (bf16[4,104,256]{2,1,0:T(8,128)(2,1)S(1)}, bf16[4,104,256]{2,1,0:T(8,128)(2,1)}, bf16[4,104,256]{2,1,0:T(8,128)(2,1)}, bf16[4,104,256]{2,1,0:T(8,128)(2,1)}) custom-call(bf16[16,104,256]{2,1,0:T(8,128)(2,1)S(1)} %get-tuple-element.38.keep_ref, bf16[16,104,256]{2,1,0:T(8,128)(2,1)} %collective-permute-done.11.got_ref), custom_call_target="tpu_custom_call" | custom-call | bytes 1048576 | tf_op jit(solution)/shard_map/pallas_call | solution.py:32
  67.4 1.2 collective-permute-start.12
  68.6 2.4 %collective-permute-start.13 = (bf16[4,104,256]{2,1,0:T(8,128)(2,1)}, bf16[4,104,256]{2,1,0:T(8,128)(2,1)S(1)}, u32[]{:S(2)}, u32[]{:S(2)}) collective-permute-start(bf16[4,104,256]{2,1,0:T(8,128)(2,1)} %get-tuple-element.42), channel_id=1, source_target_pairs={{0,128},{64,192},{128,0},{192,64},{1,129},{65,193},{129,1},{193,65... | collective-permute-start | bytes 638984 | tf_op jit(solution)/shard_map/ppermute | solution.py:306
  71.0 1.1 collective-permute-start.14
  72.2 5.9 %all-to-all-done.2 = bf16[32,32,256]{2,1,0:T(8,128)(2,1)S(1)} async-done(((bf16[32,32,256]{2,1,0:T(8,128)(2,1)}), bf16[32,32,256]{2,1,0:T(8,128)(2,1)S(1)}, u32[]{:S(2)}, u32[]{:S(2)}) %all-to-all-start.2) | async-done | bytes 524320 | tf_op jit(solution)/shard_map/all_to_all | solution.py:371
  78.1 1.8 %shard_map.132 = (bf16[4,256,256]{2,1,0:T(8,128)(2,1)S(1)}, bf16[4,256,256]{2,1,0:T(8,128)(2,1)S(1)}) custom-call(s32[4]{0:T(128)S(1)} %pad_add_fusion.place_ref, s32[1,1024]{1,0:T(1,128)S(1)} %compare_select_fusion.1.asked_ref, bf16[1024,256]{1,0:T(8,128)(2,1)S(1)} %bitcast.19), custom_call_target="tpu_custom_call" | custom-call | flops 1073741824 | bytes 1048576 | tf_op jit(solution)/shard_map/pallas_call | solution.py:32
  79.9 3.1 %collective-permute-start = (bf16[4,256,256]{2,1,0:T(8,128)(2,1)S(1)}, bf16[4,256,256]{2,1,0:T(8,128)(2,1)S(1)}, u32[]{:S(2)}, u32[]{:S(2)}) collective-permute-start(bf16[4,256,256]{2,1,0:T(8,128)(2,1)S(1)} %get-tuple-element.30), channel_id=1, source_target_pairs={{0,1},{1,0},{2,3},{3,2},{4,5},{5,4},{6,7},{7,6},{8,9},{9,8},{10,11... | collective-permute-start | bytes 1572872 | tf_op jit(solution)/shard_map/ppermute | solution.py:310
  83.0 1.8 %collective-permute-done.13.c_ref = bf16[4,104,256]{2,1,0:T(8,128)(2,1)S(1)} collective-permute-done((bf16[4,104,256]{2,1,0:T(8,128)(2,1)}, bf16[4,104,256]{2,1,0:T(8,128)(2,1)S(1)}, u32[]{:S(2)}, u32[]{:S(2)}) %collective-permute-start.13) | collective-permute-done | bytes 213024 | tf_op jit(solution)/shard_map/ppermute | solution.py:306
  85.0 1.4 collective-permute-start.15
  86.3 2.6 %collective-permute-start.16 = (bf16[1,104,256]{2,1,0:T(8,128)(2,1)S(1)}, bf16[1,104,256]{2,1,0:T(8,128)(2,1)S(1)}, u32[]{:S(2)}, u32[]{:S(2)}) collective-permute-start(bf16[1,104,256]{2,1,0:T(8,128)(2,1)S(1)} %get-tuple-element.46), channel_id=1, source_target_pairs={{0,4},{2,6},{4,0},{6,2},{1,5},{3,7},{5,1},{7,3},{8,12},{10,14},{12... | collective-permute-start | bytes 159752 | tf_op jit(solution)/shard_map/ppermute | solution.py:306
  88.9 1.1 collective-permute-start.17
  90.0 1.1 collective-permute-done.16.c_ref
  91.1 1.2 collective-permute-done.17.d_ref
  92.3 2.5 %collective-permute-start.20 = (bf16[1,104,256]{2,1,0:T(8,128)(2,1)S(1)}, bf16[1,104,256]{2,1,0:T(8,128)(2,1)S(1)}, u32[]{:S(2)}, u32[]{:S(2)}) collective-permute-start(bf16[1,104,256]{2,1,0:T(8,128)(2,1)S(1)} %shard_map.138.a_ref), channel_id=1, source_target_pairs={{0,24},{8,16},{16,8},{24,0},{32,56},{40,48},{48,40},{56,32},{1,25}... | collective-permute-start | bytes 159752 | tf_op jit(solution)/shard_map/ppermute | solution.py:310
  94.8 1.1 collective-permute-start.18
  95.9 1.2 collective-permute-done.20.d_ref
  97.1 1.7 %collective-permute-done.19.c_ref = bf16[1,104,256]{2,1,0:T(8,128)(2,1)S(1)} collective-permute-done((bf16[1,104,256]{2,1,0:T(8,128)(2,1)S(1)}, bf16[1,104,256]{2,1,0:T(8,128)(2,1)S(1)}, u32[]{:S(2)}, u32[]{:S(2)}) %collective-permute-start.19) | collective-permute-done | bytes 53280 | tf_op jit(solution)/shard_map/ppermute | solution.py:310
  98.9 3.0 %collective-permute-start.21 = (bf16[1,104,256]{2,1,0:T(8,128)(2,1)S(1)}, bf16[1,104,256]{2,1,0:T(8,128)(2,1)S(1)}, u32[]{:S(2)}, u32[]{:S(2)}) collective-permute-start(bf16[1,104,256]{2,1,0:T(8,128)(2,1)S(1)} %shard_map.139.a_ref), channel_id=1, source_target_pairs={{0,32},{8,40},{16,48},{24,56},{32,0},{40,8},{48,16},{56,24},{1,33}... | collective-permute-start | bytes 159752 | tf_op jit(solution)/shard_map/ppermute | solution.py:310
  101.9 4.1 %collective-permute-done.21.b_ref = bf16[1,104,256]{2,1,0:T(8,128)(2,1)S(1)} collective-permute-done((bf16[1,104,256]{2,1,0:T(8,128)(2,1)S(1)}, bf16[1,104,256]{2,1,0:T(8,128)(2,1)S(1)}, u32[]{:S(2)}, u32[]{:S(2)}) %collective-permute-start.21) | collective-permute-done | bytes 53280 | tf_op jit(solution)/shard_map/ppermute | solution.py:310
  106.1 3.4 %collective-permute-start.23 = (bf16[1,104,256]{2,1,0:T(8,128)(2,1)S(1)}, bf16[1,104,256]{2,1,0:T(8,128)(2,1)S(1)}, u32[]{:S(2)}, u32[]{:S(2)}) collective-permute-start(bf16[1,104,256]{2,1,0:T(8,128)(2,1)S(1)} %shard_map.140), channel_id=1, source_target_pairs={{0,4},{2,6},{4,0},{6,2},{1,5},{3,7},{5,1},{7,3},{8,12},{10,14},{12... | collective-permute-start | bytes 159752 | tf_op jit(solution)/shard_map/ppermute | solution.py:306
  110.3 1.3 collective-permute-done.23
  113.3 2.3 %collective-permute-start.26 = (bf16[4,104,256]{2,1,0:T(8,128)(2,1)S(1)}, bf16[4,104,256]{2,1,0:T(8,128)(2,1)S(1)}, u32[]{:S(2)}, u32[]{:S(2)}) collective-permute-start(bf16[4,104,256]{2,1,0:T(8,128)(2,1)S(1)} %pad_maximum_fusion.refs_0_), channel_id=1, source_target_pairs={{0,128},{64,192},{128,0},{192,64},{1,129},{65,193},{129,1},{193,65... | collective-permute-start | bytes 638984 | tf_op jit(solution)/shard_map/ppermute | solution.py:306
  116.0 2.7 %collective-permute-start.2 = (bf16[256,256]{1,0:T(8,128)(2,1)S(1)}, bf16[256,256]{1,0:T(8,128)(2,1)S(1)}, u32[]{:S(2)}, u32[]{:S(2)}) collective-permute-start(bf16[256,256]{1,0:T(8,128)(2,1)S(1)} %get-tuple-element.33), channel_id=1, source_target_pairs={{0,4},{2,6},{4,0},{6,2},{1,5},{3,7},{5,1},{7,3},{8,12},{10,14},{12... | collective-permute-start | bytes 393224 | tf_op jit(solution)/shard_map/ppermute | solution.py:306
  118.7 6.9 %collective-permute-start.28 = (bf16[4,104,256]{2,1,0:T(8,128)(2,1)S(1)}, bf16[4,104,256]{2,1,0:T(8,128)(2,1)S(1)}, u32[]{:S(2)}, u32[]{:S(2)}) collective-permute-start(bf16[4,104,256]{2,1,0:T(8,128)(2,1)S(1)} %pad_maximum_fusion.refs_0_), channel_id=1, source_target_pairs={{0,1},{1,0},{2,3},{3,2},{4,5},{5,4},{6,7},{7,6},{8,9},{9,8},{10,11... | collective-permute-start | bytes 638984 | tf_op jit(solution)/shard_map/ppermute | solution.py:310
  125.6 1.0 collective-permute-start.25
  126.6 2.1 %collective-permute-start.31 = (bf16[4,104,256]{2,1,0:T(8,128)(2,1)S(1)}, bf16[4,104,256]{2,1,0:T(8,128)(2,1)S(1)}, u32[]{:S(2)}, u32[]{:S(2)}) collective-permute-start(bf16[4,104,256]{2,1,0:T(8,128)(2,1)S(1)} %collective-permute-done.27.refs_3_), channel_id=1, source_target_pairs={{0,1},{1,0},{2,3},{3,2},{4,5},{5,4},{6,7},{7,6},{8,9},{9,8},{10,11... | collective-permute-start | bytes 638984 | tf_op jit(solution)/shard_map/ppermute | solution.py:310
  128.7 1.1 collective-permute-start.3
  130.4 2.5 %collective-permute-done.3.d_ref = bf16[256,256]{1,0:T(8,128)(2,1)S(1)} collective-permute-done((bf16[256,256]{1,0:T(8,128)(2,1)S(1)}, bf16[256,256]{1,0:T(8,128)(2,1)S(1)}, u32[]{:S(2)}, u32[]{:S(2)}) %collective-permute-start.3) | collective-permute-done | bytes 131104 | tf_op jit(solution)/shard_map/ppermute | solution.py:306
  133.0 1.2 collective-permute-start.6
  134.9 2.9 %collective-permute-start.5 = (bf16[256,256]{1,0:T(8,128)(2,1)S(1)}, bf16[256,256]{1,0:T(8,128)(2,1)}, u32[]{:S(2)}, u32[]{:S(2)}) collective-permute-start(bf16[256,256]{1,0:T(8,128)(2,1)S(1)} %shard_map.134.refs_0_), channel_id=1, source_target_pairs={{0,4},{2,6},{4,0},{6,2},{1,5},{3,7},{5,1},{7,3},{8,12},{10,14},{12... | collective-permute-start | bytes 393224 | tf_op jit(solution)/shard_map/ppermute | solution.py:306
  139.2 1.7 %collective-permute-start.29 = (bf16[4,104,256]{2,1,0:T(8,128)(2,1)}, bf16[4,104,256]{2,1,0:T(8,128)(2,1)}, u32[]{:S(2)}, u32[]{:S(2)}) collective-permute-start(bf16[4,104,256]{2,1,0:T(8,128)(2,1)} %collective-permute-done.25.refs_1_), channel_id=1, source_target_pairs={{0,1},{1,0},{2,3},{3,2},{4,5},{5,4},{6,7},{7,6},{8,9},{9,8},{10,11... | collective-permute-start | bytes 638984 | tf_op jit(solution)/shard_map/ppermute | solution.py:310
  141.6 1.4 collective-permute-start.10
  143.0 1.4 collective-permute-start.9
  150.3 3.1 %shard_map.141 = (f32[3072,256]{1,0:T(8,128)}, f32[4,256]{1,0:T(4,128)}) custom-call(s32[4]{0:T(128)S(1)} %pad_add_fusion.place_ref, bf16[4,104,256]{2,1,0:T(8,128)(2,1)S(1)} %pad_maximum_fusion.refs_0_, bf16[4,104,256]{2,1,0:T(8,128)(2,1)} %collective-permute-done.25.refs_1_, bf16[4,104,256]{2,1,0:T(8,128)(2,1)S(1)} %copy-done.5, ...), custom_call_target="tpu_custom_call" | custom-call | bytes 1048576 | tf_op jit(solution)/shard_map/pallas_call | solution.py:32
  153.4 3.2 %shard_map.135 = (f32[2048,256]{1,0:T(8,128)}, f32[2048,1]{1,0:T(8,128)S(1)}) custom-call(s32[4]{0:T(128)S(1)} %pad_add_fusion.place_ref, bf16[256,256]{1,0:T(8,128)(2,1)S(1)} %shard_map.134.refs_0_, bf16[256,256]{1,0:T(8,128)(2,1)} %collective-permute-done.4.refs_1_, bf16[256,256]{1,0:T(8,128)(2,1)} %collective-permute-done.5.refs_2_, ...), custom_call_target="tpu_custom_call" | custom-call | bytes 1048576 | tf_op jit(solution)/shard_map/pallas_call | solution.py:32
  157.6 2.2 %reduce.1 = f32[2048]{0:T(1024)} reduce(f32[2048,1]{1,0:T(8,128)} %copy-done.1, f32[]{:T(128)} %constant.27), dimensions={1}, to_apply=%get-tuple-element.37.reduce_sub_computation | reduce | bytes 16388 | tf_op jit(solution)/shard_map/pallas_call | solution.py:32
  (99 shorter events, 21.2 us)
Async XLA Ops:
  2.1 20.4 %all-to-all-start = ((s32[32,1,32]{2,1,0:T(1,128)}), s32[32,1,32]{2,1,0:T(1,128)S(1)}, u32[]{:S(2)}, u32[]{:S(2)}) async-start(s32[32,1,32]{2,1,0:T(1,128)} %compare_select_fusion), calls=%async_computation | async-start | bytes 32768 | tf_op jit(solution)/shard_map/all_to_all | solution.py:326
  15.0 1.2 copy-start
  16.6 1.0 copy-start.16
  22.5 1.2 copy-start.17
  23.7 6.8 %copy-start.21 = (s32[2,256]{1,0:T(2,128)S(1)}, s32[2,256]{1,0:T(2,128)}, u32[]{:S(2)}) copy-start(s32[2,256]{1,0:T(2,128)} %param.11) | copy-start | bytes 6148
  23.7 6.8 %copy-start.22 = (s32[1,2]{1,0:T(1,128)S(1)}, s32[1,2]{1,0:T(1,128)}, u32[]{:S(2)}) copy-start(s32[1,2]{1,0:T(1,128)} %param.10) | copy-start | bytes 28
  23.7 20.2 %copy-start.19 = (f32[4,256]{1,0:T(4,128)S(1)}, f32[4,256]{1,0:T(4,128)}, u32[]{:S(2)}) copy-start(f32[4,256]{1,0:T(4,128)} %gain_ref.1) | copy-start | bytes 12292
  26.2 17.7 %all-to-all-start.1 = ((bf16[32,32,256]{2,1,0:T(8,128)(2,1)}), bf16[32,32,256]{2,1,0:T(8,128)(2,1)S(1)}, u32[]{:S(2)}, u32[]{:S(2)}) async-start(bf16[32,32,256]{2,1,0:T(8,128)(2,1)} %bitcast.8), calls=%async_computation.1 | async-start | bytes 1048576 | tf_op jit(solution)/shard_map/all_to_all | solution.py:340
  44.9 1.4 copy-start.15
  46.3 0.9 copy-start.18
  53.5 11.1 %collective-permute-start.11 = (bf16[16,104,256]{2,1,0:T(8,128)(2,1)}, bf16[16,104,256]{2,1,0:T(8,128)(2,1)}, u32[]{:S(2)}, u32[]{:S(2)}) collective-permute-start(bf16[16,104,256]{2,1,0:T(8,128)(2,1)} %get-tuple-element.39), channel_id=1, source_target_pairs={{0,1},{1,0},{2,3},{3,2},{4,5},{5,4},{6,7},{7,6},{8,9},{9,8},{10,11... | collective-permute-start | bytes 2555912 | tf_op jit(solution)/shard_map/ppermute | solution.py:310
  58.3 19.8 %all-to-all-start.2 = ((bf16[32,32,256]{2,1,0:T(8,128)(2,1)}), bf16[32,32,256]{2,1,0:T(8,128)(2,1)S(1)}, u32[]{:S(2)}, u32[]{:S(2)}) async-start(bf16[32,32,256]{2,1,0:T(8,128)(2,1)} %bitcast.12), calls=%async_computation.2 | async-start | bytes 1048576 | tf_op jit(solution)/shard_map/all_to_all | solution.py:371
  67.4 17.5 %copy-start.13 = (bf16[4,104,256]{2,1,0:T(8,128)(2,1)S(1)}, bf16[4,104,256]{2,1,0:T(8,128)(2,1)}, u32[]{:S(2)}) copy-start(bf16[4,104,256]{2,1,0:T(8,128)(2,1)} %copy-done.12) | copy-start | bytes 638980
  67.4 15.7 %collective-permute-start.12 = (bf16[4,104,256]{2,1,0:T(8,128)(2,1)}, bf16[4,104,256]{2,1,0:T(8,128)(2,1)S(1)}, u32[]{:S(2)}, u32[]{:S(2)}) collective-permute-start(bf16[4,104,256]{2,1,0:T(8,128)(2,1)} %get-tuple-element.41), channel_id=1, source_target_pairs={{0,64},{64,128},{128,192},{192,0},{1,65},{65,129},{129,193},{193,1... | collective-permute-start | bytes 638984 | tf_op jit(solution)/shard_map/ppermute | solution.py:306
  68.6 16.2 %collective-permute-start.13 = (bf16[4,104,256]{2,1,0:T(8,128)(2,1)}, bf16[4,104,256]{2,1,0:T(8,128)(2,1)S(1)}, u32[]{:S(2)}, u32[]{:S(2)}) collective-permute-start(bf16[4,104,256]{2,1,0:T(8,128)(2,1)} %get-tuple-element.42), channel_id=1, source_target_pairs={{0,128},{64,192},{128,0},{192,64},{1,129},{65,193},{129,1},{193,65... | collective-permute-start | bytes 638984 | tf_op jit(solution)/shard_map/ppermute | solution.py:306
  71.0 13.8 %collective-permute-start.14 = (bf16[4,104,256]{2,1,0:T(8,128)(2,1)}, bf16[4,104,256]{2,1,0:T(8,128)(2,1)S(1)}, u32[]{:S(2)}, u32[]{:S(2)}) collective-permute-start(bf16[4,104,256]{2,1,0:T(8,128)(2,1)} %get-tuple-element.43), channel_id=1, source_target_pairs={{0,192},{64,0},{128,64},{192,128},{1,193},{65,1},{129,65},{193,129... | collective-permute-start | bytes 638984 | tf_op jit(solution)/shard_map/ppermute | solution.py:306
  79.9 65.3 %copy-start.20 = (f32[2048]{0:T(1024)S(1)}, f32[2048]{0:T(1024)}, u32[]{:S(2)}) copy-start(f32[2048]{0:T(1024)} %param.16) | copy-start | bytes 24580
  79.9 35.6 %collective-permute-start = (bf16[4,256,256]{2,1,0:T(8,128)(2,1)S(1)}, bf16[4,256,256]{2,1,0:T(8,128)(2,1)S(1)}, u32[]{:S(2)}, u32[]{:S(2)}) collective-permute-start(bf16[4,256,256]{2,1,0:T(8,128)(2,1)S(1)} %get-tuple-element.30), channel_id=1, source_target_pairs={{0,1},{1,0},{2,3},{3,2},{4,5},{5,4},{6,7},{7,6},{8,9},{9,8},{10,11... | collective-permute-start | bytes 1572872 | tf_op jit(solution)/shard_map/ppermute | solution.py:310
  85.0 5.1 %collective-permute-start.15 = (bf16[1,104,256]{2,1,0:T(8,128)(2,1)S(1)}, bf16[1,104,256]{2,1,0:T(8,128)(2,1)S(1)}, u32[]{:S(2)}, u32[]{:S(2)}) collective-permute-start(bf16[1,104,256]{2,1,0:T(8,128)(2,1)S(1)} %get-tuple-element.45), channel_id=1, source_target_pairs={{0,2},{2,4},{4,6},{6,0},{1,3},{3,5},{5,7},{7,1},{8,10},{10,12},{12... | collective-permute-start | bytes 159752 | tf_op jit(solution)/shard_map/ppermute | solution.py:306
  86.3 4.7 %collective-permute-start.16 = (bf16[1,104,256]{2,1,0:T(8,128)(2,1)S(1)}, bf16[1,104,256]{2,1,0:T(8,128)(2,1)S(1)}, u32[]{:S(2)}, u32[]{:S(2)}) collective-permute-start(bf16[1,104,256]{2,1,0:T(8,128)(2,1)S(1)} %get-tuple-element.46), channel_id=1, source_target_pairs={{0,4},{2,6},{4,0},{6,2},{1,5},{3,7},{5,1},{7,3},{8,12},{10,14},{12... | collective-permute-start | bytes 159752 | tf_op jit(solution)/shard_map/ppermute | solution.py:306
  88.9 3.3 %collective-permute-start.17 = (bf16[1,104,256]{2,1,0:T(8,128)(2,1)S(1)}, bf16[1,104,256]{2,1,0:T(8,128)(2,1)S(1)}, u32[]{:S(2)}, u32[]{:S(2)}) collective-permute-start(bf16[1,104,256]{2,1,0:T(8,128)(2,1)S(1)} %get-tuple-element.47), channel_id=1, source_target_pairs={{0,6},{2,0},{4,2},{6,4},{1,7},{3,1},{5,3},{7,5},{8,14},{10,8},{12,... | collective-permute-start | bytes 159752 | tf_op jit(solution)/shard_map/ppermute | solution.py:306
  92.3 4.9 %collective-permute-start.20 = (bf16[1,104,256]{2,1,0:T(8,128)(2,1)S(1)}, bf16[1,104,256]{2,1,0:T(8,128)(2,1)S(1)}, u32[]{:S(2)}, u32[]{:S(2)}) collective-permute-start(bf16[1,104,256]{2,1,0:T(8,128)(2,1)S(1)} %shard_map.138.a_ref), channel_id=1, source_target_pairs={{0,24},{8,16},{16,8},{24,0},{32,56},{40,48},{48,40},{56,32},{1,25}... | collective-permute-start | bytes 159752 | tf_op jit(solution)/shard_map/ppermute | solution.py:310
  94.8 4.1 %collective-permute-start.19 = (bf16[1,104,256]{2,1,0:T(8,128)(2,1)S(1)}, bf16[1,104,256]{2,1,0:T(8,128)(2,1)S(1)}, u32[]{:S(2)}, u32[]{:S(2)}) collective-permute-start(bf16[1,104,256]{2,1,0:T(8,128)(2,1)S(1)} %shard_map.138.a_ref), channel_id=1, source_target_pairs={{0,16},{8,24},{16,0},{24,8},{32,48},{40,56},{48,32},{56,40},{1,17}... | collective-permute-start | bytes 159752 | tf_op jit(solution)/shard_map/ppermute | solution.py:310
  94.8 4.1 %collective-permute-start.18 = (bf16[1,104,256]{2,1,0:T(8,128)(2,1)S(1)}, bf16[1,104,256]{2,1,0:T(8,128)(2,1)S(1)}, u32[]{:S(2)}, u32[]{:S(2)}) collective-permute-start(bf16[1,104,256]{2,1,0:T(8,128)(2,1)S(1)} %shard_map.138.a_ref), channel_id=1, source_target_pairs={{0,8},{8,0},{16,24},{24,16},{32,40},{40,32},{48,56},{56,48},{1,9},... | collective-permute-start | bytes 159752 | tf_op jit(solution)/shard_map/ppermute | solution.py:310
  98.9 7.1 %collective-permute-start.21 = (bf16[1,104,256]{2,1,0:T(8,128)(2,1)S(1)}, bf16[1,104,256]{2,1,0:T(8,128)(2,1)S(1)}, u32[]{:S(2)}, u32[]{:S(2)}) collective-permute-start(bf16[1,104,256]{2,1,0:T(8,128)(2,1)S(1)} %shard_map.139.a_ref), channel_id=1, source_target_pairs={{0,32},{8,40},{16,48},{24,56},{32,0},{40,8},{48,16},{56,24},{1,33}... | collective-permute-start | bytes 159752 | tf_op jit(solution)/shard_map/ppermute | solution.py:310
  106.0 4.3 %collective-permute-start.24 = (bf16[1,104,256]{2,1,0:T(8,128)(2,1)S(1)}, bf16[1,104,256]{2,1,0:T(8,128)(2,1)S(1)}, u32[]{:S(2)}, u32[]{:S(2)}) collective-permute-start(bf16[1,104,256]{2,1,0:T(8,128)(2,1)S(1)} %shard_map.140), channel_id=1, source_target_pairs={{0,2},{2,4},{4,6},{6,0},{1,3},{3,5},{5,7},{7,1},{8,10},{10,12},{12... | collective-permute-start | bytes 159752 | tf_op jit(solution)/shard_map/ppermute | solution.py:306
  106.1 5.5 %collective-permute-start.23 = (bf16[1,104,256]{2,1,0:T(8,128)(2,1)S(1)}, bf16[1,104,256]{2,1,0:T(8,128)(2,1)S(1)}, u32[]{:S(2)}, u32[]{:S(2)}) collective-permute-start(bf16[1,104,256]{2,1,0:T(8,128)(2,1)S(1)} %shard_map.140), channel_id=1, source_target_pairs={{0,4},{2,6},{4,0},{6,2},{1,5},{3,7},{5,1},{7,3},{8,12},{10,14},{12... | collective-permute-start | bytes 159752 | tf_op jit(solution)/shard_map/ppermute | solution.py:306
  109.5 3.0 %collective-permute-start.22 = (bf16[1,104,256]{2,1,0:T(8,128)(2,1)S(1)}, bf16[1,104,256]{2,1,0:T(8,128)(2,1)S(1)}, u32[]{:S(2)}, u32[]{:S(2)}) collective-permute-start(bf16[1,104,256]{2,1,0:T(8,128)(2,1)S(1)} %shard_map.140), channel_id=1, source_target_pairs={{0,6},{2,0},{4,2},{6,4},{1,7},{3,1},{5,3},{7,5},{8,14},{10,8},{12,... | collective-permute-start | bytes 159752 | tf_op jit(solution)/shard_map/ppermute | solution.py:306
  112.5 13.1 %collective-permute-start.27 = (bf16[4,104,256]{2,1,0:T(8,128)(2,1)S(1)}, bf16[4,104,256]{2,1,0:T(8,128)(2,1)S(1)}, u32[]{:S(2)}, u32[]{:S(2)}) collective-permute-start(bf16[4,104,256]{2,1,0:T(8,128)(2,1)S(1)} %pad_maximum_fusion.refs_0_), channel_id=1, source_target_pairs={{0,64},{64,128},{128,192},{192,0},{1,65},{65,129},{129,193},{193,1... | collective-permute-start | bytes 638984 | tf_op jit(solution)/shard_map/ppermute | solution.py:306
  113.3 13.4 %collective-permute-start.26 = (bf16[4,104,256]{2,1,0:T(8,128)(2,1)S(1)}, bf16[4,104,256]{2,1,0:T(8,128)(2,1)S(1)}, u32[]{:S(2)}, u32[]{:S(2)}) collective-permute-start(bf16[4,104,256]{2,1,0:T(8,128)(2,1)S(1)} %pad_maximum_fusion.refs_0_), channel_id=1, source_target_pairs={{0,128},{64,192},{128,0},{192,64},{1,129},{65,193},{129,1},{193,65... | collective-permute-start | bytes 638984 | tf_op jit(solution)/shard_map/ppermute | solution.py:306
  115.7 13.0 %collective-permute-start.1 = (bf16[256,256]{1,0:T(8,128)(2,1)S(1)}, bf16[256,256]{1,0:T(8,128)(2,1)S(1)}, u32[]{:S(2)}, u32[]{:S(2)}) collective-permute-start(bf16[256,256]{1,0:T(8,128)(2,1)S(1)} %get-tuple-element.32), channel_id=1, source_target_pairs={{0,2},{2,4},{4,6},{6,0},{1,3},{3,5},{5,7},{7,1},{8,10},{10,12},{12... | collective-permute-start | bytes 393224 | tf_op jit(solution)/shard_map/ppermute | solution.py:306
  116.0 13.7 %collective-permute-start.2 = (bf16[256,256]{1,0:T(8,128)(2,1)S(1)}, bf16[256,256]{1,0:T(8,128)(2,1)S(1)}, u32[]{:S(2)}, u32[]{:S(2)}) collective-permute-start(bf16[256,256]{1,0:T(8,128)(2,1)S(1)} %get-tuple-element.33), channel_id=1, source_target_pairs={{0,4},{2,6},{4,0},{6,2},{1,5},{3,7},{5,1},{7,3},{8,12},{10,14},{12... | collective-permute-start | bytes 393224 | tf_op jit(solution)/shard_map/ppermute | solution.py:306
  118.7 15.4 %collective-permute-start.28 = (bf16[4,104,256]{2,1,0:T(8,128)(2,1)S(1)}, bf16[4,104,256]{2,1,0:T(8,128)(2,1)S(1)}, u32[]{:S(2)}, u32[]{:S(2)}) collective-permute-start(bf16[4,104,256]{2,1,0:T(8,128)(2,1)S(1)} %pad_maximum_fusion.refs_0_), channel_id=1, source_target_pairs={{0,1},{1,0},{2,3},{3,2},{4,5},{5,4},{6,7},{7,6},{8,9},{9,8},{10,11... | collective-permute-start | bytes 638984 | tf_op jit(solution)/shard_map/ppermute | solution.py:310
  125.6 19.6 %copy-start.2 = (bf16[4,104,256]{2,1,0:T(8,128)(2,1)}, bf16[4,104,256]{2,1,0:T(8,128)(2,1)S(1)}, u32[]{:S(2)}) copy-start(bf16[4,104,256]{2,1,0:T(8,128)(2,1)S(1)} %collective-permute-done.27.refs_3_) | copy-start | bytes 638980
  125.6 12.1 %collective-permute-start.25 = (bf16[4,104,256]{2,1,0:T(8,128)(2,1)S(1)}, bf16[4,104,256]{2,1,0:T(8,128)(2,1)}, u32[]{:S(2)}, u32[]{:S(2)}) collective-permute-start(bf16[4,104,256]{2,1,0:T(8,128)(2,1)S(1)} %pad_maximum_fusion.refs_0_), channel_id=1, source_target_pairs={{0,192},{64,0},{128,64},{192,128},{1,193},{65,1},{129,65},{193,129... | collective-permute-start | bytes 638984 | tf_op jit(solution)/shard_map/ppermute | solution.py:306
  126.6 18.6 %copy-start.4 = (bf16[4,104,256]{2,1,0:T(8,128)(2,1)}, bf16[4,104,256]{2,1,0:T(8,128)(2,1)S(1)}, u32[]{:S(2)}) copy-start(bf16[4,104,256]{2,1,0:T(8,128)(2,1)S(1)} %collective-permute-done.26.refs_2_) | copy-start | bytes 638980
  126.6 11.9 %collective-permute-start.31 = (bf16[4,104,256]{2,1,0:T(8,128)(2,1)S(1)}, bf16[4,104,256]{2,1,0:T(8,128)(2,1)S(1)}, u32[]{:S(2)}, u32[]{:S(2)}) collective-permute-start(bf16[4,104,256]{2,1,0:T(8,128)(2,1)S(1)} %collective-permute-done.27.refs_3_), channel_id=1, source_target_pairs={{0,1},{1,0},{2,3},{3,2},{4,5},{5,4},{6,7},{7,6},{8,9},{9,8},{10,11... | collective-permute-start | bytes 638984 | tf_op jit(solution)/shard_map/ppermute | solution.py:310
  128.7 4.2 %collective-permute-start.3 = (bf16[256,256]{1,0:T(8,128)(2,1)S(1)}, bf16[256,256]{1,0:T(8,128)(2,1)S(1)}, u32[]{:S(2)}, u32[]{:S(2)}) collective-permute-start(bf16[256,256]{1,0:T(8,128)(2,1)S(1)} %get-tuple-element.34), channel_id=1, source_target_pairs={{0,6},{2,0},{4,2},{6,4},{1,7},{3,1},{5,3},{7,5},{8,14},{10,8},{12,... | collective-permute-start | bytes 393224 | tf_op jit(solution)/shard_map/ppermute | solution.py:306
  129.8 11.1 %collective-permute-start.30 = (bf16[4,104,256]{2,1,0:T(8,128)(2,1)S(1)}, bf16[4,104,256]{2,1,0:T(8,128)(2,1)S(1)}, u32[]{:S(2)}, u32[]{:S(2)}) collective-permute-start(bf16[4,104,256]{2,1,0:T(8,128)(2,1)S(1)} %collective-permute-done.26.refs_2_), channel_id=1, source_target_pairs={{0,1},{1,0},{2,3},{3,2},{4,5},{5,4},{6,7},{7,6},{8,9},{9,8},{10,11... | collective-permute-start | bytes 638984 | tf_op jit(solution)/shard_map/ppermute | solution.py:310
  133.0 8.6 %collective-permute-start.6 = (bf16[256,256]{1,0:T(8,128)(2,1)S(1)}, bf16[256,256]{1,0:T(8,128)(2,1)}, u32[]{:S(2)}, u32[]{:S(2)}) collective-permute-start(bf16[256,256]{1,0:T(8,128)(2,1)S(1)} %shard_map.134.refs_0_), channel_id=1, source_target_pairs={{0,2},{2,4},{4,6},{6,0},{1,3},{3,5},{5,7},{7,1},{8,10},{10,12},{12... | collective-permute-start | bytes 393224 | tf_op jit(solution)/shard_map/ppermute | solution.py:306
  134.9 8.1 %collective-permute-start.5 = (bf16[256,256]{1,0:T(8,128)(2,1)S(1)}, bf16[256,256]{1,0:T(8,128)(2,1)}, u32[]{:S(2)}, u32[]{:S(2)}) collective-permute-start(bf16[256,256]{1,0:T(8,128)(2,1)S(1)} %shard_map.134.refs_0_), channel_id=1, source_target_pairs={{0,4},{2,6},{4,0},{6,2},{1,5},{3,7},{5,1},{7,3},{8,12},{10,14},{12... | collective-permute-start | bytes 393224 | tf_op jit(solution)/shard_map/ppermute | solution.py:306
  137.7 6.7 %collective-permute-start.4 = (bf16[256,256]{1,0:T(8,128)(2,1)S(1)}, bf16[256,256]{1,0:T(8,128)(2,1)}, u32[]{:S(2)}, u32[]{:S(2)}) collective-permute-start(bf16[256,256]{1,0:T(8,128)(2,1)S(1)} %shard_map.134.refs_0_), channel_id=1, source_target_pairs={{0,6},{2,0},{4,2},{6,4},{1,7},{3,1},{5,3},{7,5},{8,14},{10,8},{12,... | collective-permute-start | bytes 393224 | tf_op jit(solution)/shard_map/ppermute | solution.py:306
  139.2 6.4 %collective-permute-start.29 = (bf16[4,104,256]{2,1,0:T(8,128)(2,1)}, bf16[4,104,256]{2,1,0:T(8,128)(2,1)}, u32[]{:S(2)}, u32[]{:S(2)}) collective-permute-start(bf16[4,104,256]{2,1,0:T(8,128)(2,1)} %collective-permute-done.25.refs_1_), channel_id=1, source_target_pairs={{0,1},{1,0},{2,3},{3,2},{4,5},{5,4},{6,7},{7,6},{8,9},{9,8},{10,11... | collective-permute-start | bytes 638984 | tf_op jit(solution)/shard_map/ppermute | solution.py:310
  141.6 11.8 %collective-permute-start.7 = (bf16[256,256]{1,0:T(8,128)(2,1)S(1)}, bf16[256,256]{1,0:T(8,128)(2,1)}, u32[]{:S(2)}, u32[]{:S(2)}) collective-permute-start(bf16[256,256]{1,0:T(8,128)(2,1)S(1)} %shard_map.134.refs_0_), channel_id=1, source_target_pairs={{0,1},{1,0},{2,3},{3,2},{4,5},{5,4},{6,7},{7,6},{8,9},{9,8},{10,11... | collective-permute-start | bytes 393224 | tf_op jit(solution)/shard_map/ppermute | solution.py:310
  141.6 11.8 %collective-permute-start.10 = (bf16[256,256]{1,0:T(8,128)(2,1)}, bf16[256,256]{1,0:T(8,128)(2,1)}, u32[]{:S(2)}, u32[]{:S(2)}) collective-permute-start(bf16[256,256]{1,0:T(8,128)(2,1)} %collective-permute-done.6.refs_3_), channel_id=1, source_target_pairs={{0,1},{1,0},{2,3},{3,2},{4,5},{5,4},{6,7},{7,6},{8,9},{9,8},{10,11... | collective-permute-start | bytes 393224 | tf_op jit(solution)/shard_map/ppermute | solution.py:310
  143.0 10.4 %collective-permute-start.9 = (bf16[256,256]{1,0:T(8,128)(2,1)}, bf16[256,256]{1,0:T(8,128)(2,1)}, u32[]{:S(2)}, u32[]{:S(2)}) collective-permute-start(bf16[256,256]{1,0:T(8,128)(2,1)} %collective-permute-done.5.refs_2_), channel_id=1, source_target_pairs={{0,1},{1,0},{2,3},{3,2},{4,5},{5,4},{6,7},{7,6},{8,9},{9,8},{10,11... | collective-permute-start | bytes 393224 | tf_op jit(solution)/shard_map/ppermute | solution.py:310
  144.4 9.0 %collective-permute-start.8 = (bf16[256,256]{1,0:T(8,128)(2,1)}, bf16[256,256]{1,0:T(8,128)(2,1)}, u32[]{:S(2)}, u32[]{:S(2)}) collective-permute-start(bf16[256,256]{1,0:T(8,128)(2,1)} %collective-permute-done.4.refs_1_), channel_id=1, source_target_pairs={{0,1},{1,0},{2,3},{3,2},{4,5},{5,4},{6,7},{7,6},{8,9},{9,8},{10,11... | collective-permute-start | bytes 393224 | tf_op jit(solution)/shard_map/ppermute | solution.py:310
  156.6 1.0 copy-start.1
  (10 other events, 8.3 us)

commit v2 on v1

v2 whole, which is shorter than its diff:
```python
import functools

import jax
import jax.numpy as jnp
from jax import lax
from jax.experimental import pallas as pl
from jax.experimental.pallas import tpu as pltpu
from jax.sharding import Mesh
from jax.sharding import PartitionSpec as P

DILATIONS = (1, 2, 4, 8)
LEARN_RATE = 0.5
BF = jnp.bfloat16
F32 = jnp.float32
LAYERS, TAPS, C = 4, 3, 256
GROUP = 32
LEN = 256
PACKED = 320
STEP = 64
PIECE = 96
TAIL = 8
SLAB = PIECE + TAIL
NT = (((1,), (1,)), ((), ()))
TN = (((0,), (0,)), ((), ()))
SMEM = pl.BlockSpec(memory_space=pltpu.SMEM)
VMEM = pl.BlockSpec(memory_space=pltpu.VMEM)
ANY = pl.BlockSpec(memory_space=pl.ANY)
HBM = pl.BlockSpec(memory_space=pltpu.HBM)


def call(kernel, outs, args, specs=None, out_specs=None, scratch=(), flops=0, limit=8):
    if specs is None:
        specs = [VMEM] * len(args)
    if out_specs is None:
        out_specs = jax.tree.map(lambda _: VMEM, outs)
    return pl.pallas_call(
        kernel,
        out_shape=outs,
        in_specs=specs,
        out_specs=out_specs,
        scratch_shapes=list(scratch),
        compiler_params=pltpu.CompilerParams(vmem_limit_bytes=limit * 1024 * 1024),
        cost_estimate=pl.CostEstimate(flops=flops, bytes_accessed=1 << 20, transcendentals=0),
    )(*args)


def shape(dims, dtype):
    return jax.ShapeDtypeStruct(dims, dtype)


def iota(dims, axis):
    return lax.broadcasted_iota(jnp.int32, dims, axis)


def spreader(groups):
    return (iota((groups, C), 1) // GROUP == iota((groups, C), 0)).astype(F32).astype(BF)


def dequantized(codes, scales, spread):
    return codes.astype(F32) * jnp.dot(scales, spread, preferred_element_type=F32)


def fetch_kernel(asked_ref, codes_hbm, scales_hbm, out_ref, codes_ref, scales_ref, sems):
    senders, cap = asked_ref.shape
    rows, groups = scales_ref.shape
    stride = rows // cap
    part = 256
    copies = [pltpu.make_async_copy(scales_hbm, scales_ref, sems.at[0])]
    for at in range(rows // 512):
        block = pl.ds(at * 512, 512)
        copies.append(
            pltpu.make_async_copy(codes_hbm.at[block], codes_ref.at[block], sems.at[at + 1])
        )
    for copy in copies:
        copy.start()
    asked = asked_ref[...].astype(F32).astype(BF)
    targets = []
    for start in range(0, senders * cap, part):
        line = iota((part, senders), 0) + start
        pick = (line // cap == iota((part, senders), 1)).astype(F32).astype(BF)
        lists = jnp.dot(pick, asked, preferred_element_type=F32)
        entry = (iota((part, cap), 0) + start) % cap
        own = jnp.where(entry == iota((part, cap), 1), lists, 0.0)
        offset = jnp.sum(own, axis=1, keepdims=True).astype(jnp.int32)
        entry = (iota((part, 1), 0) + start) % cap
        targets.append(jnp.where(offset >= 0, entry * stride + offset, -1))
    spread = spreader(groups)
    for copy in copies:
        copy.wait()
    tables = []
    for start in range(0, rows, 256):
        block = pl.ds(start, 256)
        tables.append(dequantized(codes_ref[block, :], scales_ref[block, :], spread).astype(BF))
    table = jnp.concatenate(tables, axis=0)
    for at, target in enumerate(targets):
        chosen = (iota((part, rows), 1) == target).astype(F32).astype(BF)
        got = jnp.dot(chosen, table, preferred_element_type=F32)
        out_ref[pl.ds(at * part, part), :] = got.astype(BF)


def sigmoid(values):
    return 0.5 + 0.5 * jnp.tanh(0.5 * values)


def train_kernel(
    place_ref,
    slots_ref,
    code_ref,
    fetched_ref,
    weight_hbm,
    gain_ref,
    upstream_hbm,
    slot_grad_ref,
    keep_ref,
    send_ref,
    held_ref,
    conv_ref,
    unit_ref,
    scale_ref,
    grad_ref,
    wide_ref,
    weight_grad_ref,
    weight_ref,
    upstream_ref,
    sems,
):
    block = TAPS * C
    copies = [
        pltpu.make_async_copy(
            weight_hbm.at[pl.ds(layer * block, block)],
            weight_ref.at[pl.ds(layer * block, block)],
            sems.at[layer],
        )
        for layer in range(LAYERS)
    ]
    copies.append(pltpu.make_async_copy(upstream_hbm, upstream_ref, sems.at[LAYERS]))
    for copy in copies:
        copy.start()
    split, x, y, core = place_ref[0], place_ref[1], place_ref[2], place_ref[3]
    steps = range(0, PACKED, STEP)
    line = iota((PACKED, C), 0)
    since = jnp.where(line >= split, line - split, line)
    until = jnp.where(line >= split, PACKED - line, split - line)

    source = iota((PACKED, 1), 0)
    source = jnp.where(source >= split, source + (LEN - split), source)
    match = iota((PACKED, 2 * LEN), 1) == source
    packer = match.astype(F32).astype(BF)
    slot = jnp.where(match, slots_ref[...].astype(F32), 0.0)
    slot = jnp.sum(slot, axis=1, keepdims=True).astype(jnp.int32)
    slots = fetched_ref.shape[0]
    chosen = (iota((PACKED, slots), 1) == slot).astype(F32).astype(BF)
    first = jnp.dot(chosen, fetched_ref[...], preferred_element_type=F32)
    held_ref[0] = first.astype(BF)

    for layer in range(LAYERS):
        gap = DILATIONS[layer]
        now = held_ref[layer].astype(F32)
        taps = [held_ref[layer]]
        for tap in (1, 2):
            moved = pltpu.roll(now, tap * gap, 0)
            taps.append(jnp.where(since >= tap * gap, moved, 0.0).astype(BF))
        base = layer * TAPS * C
        copies[layer].wait()
        conv_ref[...] = jnp.dot(
            jnp.concatenate(taps, axis=1),
            weight_ref[pl.ds(base, TAPS * C), :],
            preferred_element_type=F32,
        )
        gain = gain_ref[pl.ds(layer, 1), :]
        for start in steps:
            part = pl.ds(start, STEP)
            value = conv_ref[part, :]
            center = value - jnp.mean(value, axis=1, keepdims=True)
            spread = jnp.mean(center * center, axis=1, keepdims=True)
            scale = lax.rsqrt(spread + 1e-5)
            unit = center * scale
            unit_ref[layer, part, :] = unit
            scale_ref[layer, part, :] = jnp.broadcast_to(scale, (STEP, 128))
            if layer + 1 < LAYERS:
                gained = unit * gain
                after = gained * sigmoid(gained)
                if layer % 2 == 1:
                    after = after + held_ref[layer - 1, part, :].astype(F32)
                held_ref[layer + 1, part, :] = after.astype(BF)

    copies[LAYERS].wait()
    grad_ref[...] = jnp.dot(packer, upstream_ref[...], preferred_element_type=F32)

    gain_rows = [None] * LAYERS
    for layer in reversed(range(LAYERS)):
        gap = DILATIONS[layer]
        gain = gain_ref[pl.ds(layer, 1), :]
        total = jnp.zeros((8, C), F32)
        for start in steps:
            part = pl.ds(start, STEP)
            unit = unit_ref[layer, part, :]
            scale = scale_ref[layer, part, :]
            gained = unit * gain
            gate = sigmoid(gained)
            inner = grad_ref[part, :] * (gate * (1.0 + gained * (1.0 - gate)))
            total = total + jnp.sum((inner * unit).reshape(STEP // 8, 8, C), axis=0)
            inner = inner * gain
            mean = jnp.mean(inner, axis=1, keepdims=True)
            slope = jnp.mean(inner * unit, axis=1, keepdims=True)
            outer = inner - mean - unit * slope
            conv_ref[part, :] = outer * jnp.concatenate([scale, scale], axis=1)
        gain_rows[layer] = jnp.sum(total, axis=0, keepdims=True)
        now = conv_ref[...]
        wide_ref[:, 0:C] = now.astype(BF)
        for tap in (1, 2):
            moved = pltpu.roll(now, PACKED - tap * gap, 0)
            moved = jnp.where(until > tap * gap, moved, 0.0)
            wide_ref[:, tap * C : (tap + 1) * C] = moved.astype(BF)

        below = jnp.zeros((PACKED, C), F32)
        for tap in range(TAPS):
            kernel = weight_ref[pl.ds((layer * TAPS + tap) * C, C), :]
            below = below + lax.dot_general(
                wide_ref[:, tap * C : (tap + 1) * C], kernel, NT, preferred_element_type=F32
            )
        if layer % 2 == 0:
            if layer == 2:
                skip = jnp.dot(packer, upstream_ref[...], preferred_element_type=F32)
            else:
                skip = held_ref[4].astype(F32)
            below = below + skip
        rounded = below.astype(BF)
        grad_ref[...] = rounded.astype(F32)
        if layer == 2:
            held_ref[4] = rounded

        weight_grad = lax.dot_general(
            held_ref[layer], wide_ref[...], TN, preferred_element_type=F32
        )
        for tap in range(TAPS):
            weight_grad_ref[pl.ds(tap * C, C), :] = weight_grad[:, tap * C : (tap + 1) * C]

        for pair in range(4):
            even = weight_grad_ref[pl.ds(2 * pair * PIECE, PIECE), :]
            odd = weight_grad_ref[pl.ds((2 * pair + 1) * PIECE, PIECE), :]
            tail = jnp.zeros((TAIL, C), F32)
            even_tail = tail
            if layer == 0 and pair == 0:
                exact = jnp.concatenate(gain_rows + gain_rows, axis=0)
                high = exact.astype(BF).astype(F32)
                even_tail = jnp.where(iota((TAIL, C), 0) < LAYERS, high, exact - high)
            even = jnp.concatenate([even, even_tail], axis=0)
            odd = jnp.concatenate([odd, tail], axis=0)
            place = ((layer - x + 4) % 4) * 4 + (pair - y + 4) % 4
            keep_ref[place] = jnp.where(core == 0, even, odd).astype(BF)
            send_ref[place] = jnp.where(core == 0, odd, even).astype(BF)

    mine = grad_ref[...].astype(BF)
    half = C // 2
    low = iota((32, 8, half), 1) < 4
    for start in range(0, slots, 256):
        here = iota((256, PACKED), 0) + start == code_ref[...]
        here = here.astype(F32).astype(BF)
        summed = jnp.dot(here, mine, preferred_element_type=F32)
        left = summed[:, :half].reshape(32, 8, half)
        right = summed[:, half:].reshape(32, 8, half)
        first = jnp.where(low, left, pltpu.roll(right, 4, 1))
        second = jnp.where(low, pltpu.roll(left, 4, 1), right)
        both = jnp.stack([first, second], axis=1).reshape(512, half)
        slot_grad_ref[pl.ds(2 * start, 512), :] = both.astype(BF)


def settle(total):
    tail = total[PIECE:SLAB, :]
    exact = tail + pltpu.roll(tail, LAYERS, 0)
    high = exact.astype(BF).astype(F32)
    tail = jnp.where(iota((TAIL, C), 0) < LAYERS, high, exact - high)
    return jnp.concatenate([total[:PIECE, :], tail], axis=0).astype(BF)


def core_sum_kernel(keep_ref, got_ref, *out_refs):
    for at in range(16):
        total = keep_ref[at].astype(F32) + got_ref[at].astype(F32)
        out_refs[at // 4][at % 4] = settle(total)


def four_sum_kernel(a_ref, b_ref, c_ref, d_ref, *out_refs):
    for at in range(a_ref.shape[0]):
        left = a_ref[at].astype(F32) + b_ref[at].astype(F32)
        right = c_ref[at].astype(F32) + d_ref[at].astype(F32)
        out_refs[at][0] = settle(left + right)


def merge_kernel(a_ref, b_ref, rows_ref, out_ref):
    slab = settle(a_ref[0].astype(F32) + b_ref[0].astype(F32)).astype(F32)
    out_ref[...] = jnp.concatenate([rows_ref[...].astype(F32), slab], axis=0).astype(BF)


def spread_kernel(count, plan, first, place_ref, *refs):
    sources, refs = refs[:count], refs[count:]
    if not first:
        gain_before, refs = refs[1], refs[2:]
    conv_hbm, gain_ref, refs = refs[0], refs[1], refs[2:]
    held, wide_ref, in_sems, out_sems = refs[:count], *refs[count:]
    x, y, core = place_ref[1], place_ref[2], place_ref[3]
    arrivals = [
        pltpu.make_async_copy(source, slot, in_sems.at[at])
        for at, (source, slot) in enumerate(zip(sources, held))
    ]
    for arrival in arrivals:
        arrival.start()
    gain_ref[...] = jnp.zeros_like(gain_ref) if first else gain_before[...]
    leaving = []
    ready = -1
    for at, (buffer, inner, along_x, along_y, other) in enumerate(plan):
        if buffer != ready:
            arrivals[buffer].wait()
            ready = buffer
        layer = (x + along_x) % 4
        side = core if other == 0 else 1 - core
        number = layer * 8 + ((y + along_y) % 4) * 2 + side
        if inner is None:
            block = held[buffer][...].astype(F32)[C:, :]
        else:
            block = held[buffer][inner].astype(F32)
        wide_ref[at] = block[:PIECE, :]
        copy = pltpu.make_async_copy(
            wide_ref.at[at],
            conv_hbm.at[pl.ds(pl.multiple_of(number * PIECE, PIECE), PIECE)],
            out_sems.at[at],
        )
        copy.start()
        leaving.append(copy)

        @pl.when(number == 0)
        def _():
            tail = block[PIECE:, :]
            gain_ref[...] = (tail + pltpu.roll(tail, LAYERS, 0))[:LAYERS, :]

    for copy in leaving:
        copy.wait()


def spread(place, blocks, plan, before=None):
    outs = [shape((LAYERS * TAPS * C, C), F32), shape((LAYERS, C), F32)]
    count = len(blocks)
    args, specs, aliases = [place] + blocks, [SMEM] + [ANY] * count, {}
    if before is not None:
        args, specs = args + list(before), specs + [HBM, VMEM]
        aliases = {count + 1: 0}
    return pl.pallas_call(
        functools.partial(spread_kernel, count, plan, before is None),
        out_shape=outs,
        in_specs=specs,
        out_specs=[HBM, VMEM],
        input_output_aliases=aliases,
        scratch_shapes=[pltpu.VMEM(block.shape, BF) for block in blocks]
        + [
            pltpu.VMEM((len(plan), PIECE, C), F32),
            pltpu.SemaphoreType.DMA((count,)),
            pltpu.SemaphoreType.DMA((len(plan),)),
        ],
        compiler_params=pltpu.CompilerParams(vmem_limit_bytes=8 * 1024 * 1024),
        cost_estimate=pl.CostEstimate(flops=0, bytes_accessed=1 << 21, transcendentals=0),
    )(*args)


def scatter_kernel(place_ref, code_a, code_b, code_c, code_d, got_ref, out_ref):
    y, core = place_ref[2], place_ref[3]
    own = y * 2 + core
    lines = code_a.shape[1]
    total = [jnp.zeros((C, C // 2), F32)] * 2
    for along, code_ref in enumerate((code_a, code_b, code_c, code_d)):
        for other in range(2):
            side = core if other == 0 else 1 - core
            group = ((y + along) % 4) * 2 + side
            code = code_ref[pl.ds(other * 8 + own, 1), :]
            got = got_ref[pl.ds(pl.multiple_of(group * lines, lines), lines), :]
            for half in range(2):
                here = iota((C, lines), 0) + half * C == code
                here = here.astype(F32).astype(BF)
                total[half] = total[half] + jnp.dot(here, got, preferred_element_type=F32)
    out_ref[...] = jnp.concatenate(total, axis=1).astype(BF)


def adagrad_kernel(place_ref, *refs):
    sources, (codes_hbm, scales_ref, accum_ref) = refs[:8], refs[8:11]
    rows_hbm, next_ref = refs[11:13]
    held, codes_ref, rows_ref, in_sems, table_sems, out_sems = refs[13:21], *refs[21:]
    spread = spreader(scales_ref.shape[1])
    y, core = place_ref[2], place_ref[3]
    arrivals, tables, leaving = [], [], []
    for at in range(8):
        copy = pltpu.make_async_copy(sources[at], held[at], in_sems.at[at])
        copy.start()
        arrivals.append(copy)
        side = core if at < 4 else 1 - core
        number = ((y + at % 4) % 4) * 2 + side
        part = pl.ds(pl.multiple_of(number * C, C), C)
        copy = pltpu.make_async_copy(codes_hbm.at[part], codes_ref.at[at], table_sems.at[at])
        copy.start()
        tables.append((copy, number, part))
    same = iota((C, C), 0) == iota((C, C), 1)
    for at in range(8):
        copy, number, part = tables[at]
        arrivals[at].wait()
        copy.wait()
        gradient = held[at][...].astype(F32)[:C, :]
        grown = accum_ref[part, :] + jnp.mean(gradient * gradient, axis=1, keepdims=True)
        table = dequantized(codes_ref[at], scales_ref[part, :], spread)
        rows_ref[at] = table - LEARN_RATE * gradient * lax.rsqrt(grown)
        copy = pltpu.make_async_copy(rows_ref.at[at], rows_hbm.at[part], out_sems.at[at])
        copy.start()
        leaving.append(copy)
        next_ref[pl.ds(number, 1), :] = jnp.sum(
            jnp.where(same, grown, 0.0), axis=0, keepdims=True
        )
    for copy in leaving:
        copy.wait()


def shifted(values, axis, size, offset):
    return lax.ppermute(values, axis, [(i, (i + offset) % size) for i in range(size)])


def crossed(values, axis, size, bits):
    return lax.ppermute(values, axis, [(i, i ^ bits) for i in range(size)])


def body(lengths, slots, requests, counts, codes, scales, accum, conv_weight, norm_gain, upstream):
    table_axes = ("x", "z")
    owners = requests.shape[1]
    cap = requests.shape[2]
    rows = codes.shape[0]
    stride = rows // cap
    split = lengths[0, 0]
    place = jnp.stack(
        [split, lax.axis_index("x"), lax.axis_index("y"), lax.axis_index("core")]
    ).astype(jnp.int32)

    y, core = lax.axis_index("y"), lax.axis_index("core")

    entry = jnp.arange(cap, dtype=jnp.int32)[None, :]
    wanted = jnp.where(entry < counts[0][:, None], requests[0] - entry * stride, -1)
    asked = lax.all_to_all(wanted, table_axes, split_axis=0, concat_axis=0, tiled=True)

    order = jnp.arange(PACKED, dtype=jnp.int32)
    order = order + jnp.where(order >= split, LEN - split, 0)
    match = order[:, None] == jnp.arange(2 * LEN, dtype=jnp.int32)[None, :]
    packed = jnp.sum(jnp.where(match, slots.reshape(1, 2 * LEN), 0), axis=1)
    each = cap // 8
    code = (packed % cap) // each * (owners * each) + packed // cap * each + packed % each

    sending = call(
        fetch_kernel,
        shape((owners * cap, C), BF),
        [asked, codes, scales],
        specs=[VMEM, HBM, HBM],
        scratch=[
            pltpu.VMEM((rows, C), BF),
            pltpu.VMEM(scales.shape, BF),
            pltpu.SemaphoreType.DMA((rows // 512 + 1,)),
        ],
        flops=1 << 30,
        limit=16,
    )
    fetched = lax.all_to_all(
        sending.reshape(owners, cap, C), table_axes, split_axis=0, concat_axis=0, tiled=True
    ).reshape(owners * cap, C)

    lists = asked.reshape(owners, 8, each).transpose(1, 0, 2)[:, :, None, :]
    base = jnp.arange(2, dtype=jnp.int32)[:, None] * C
    base = base + jnp.arange(each, dtype=jnp.int32)[None, :] * stride
    target = jnp.where(lists >= 0, lists + base, -1).reshape(8, 2 * owners * each)
    target = jnp.concatenate([target, crossed(target, "core", 2, 1)], axis=0)
    targets = [target] + [shifted(target, "y", 4, -k) for k in (1, 2, 3)]
    fetched, *targets = lax.optimization_barrier((fetched, *targets))

    slab16 = shape((16, SLAB, C), BF)
    slot_grad, keep, send = call(
        train_kernel,
        [shape((2 * owners * cap, C // 2), BF), slab16, slab16],
        [
            place,
            slots.reshape(1, 2 * LEN),
            code.reshape(1, PACKED),
            fetched,
            conv_weight.reshape(LAYERS * TAPS * C, C),
            norm_gain,
            upstream.reshape(2 * LEN, C),
        ],
        specs=[SMEM, VMEM, VMEM, VMEM, HBM, VMEM, HBM],
        scratch=[
            pltpu.VMEM((LAYERS + 1, PACKED, C), BF),
            pltpu.VMEM((PACKED, C), F32),
            pltpu.VMEM((LAYERS, PACKED, C), F32),
            pltpu.VMEM((LAYERS, PACKED, 128), F32),
            pltpu.VMEM((PACKED, C), F32),
            pltpu.VMEM((PACKED, TAPS * C), BF),
            pltpu.VMEM((TAPS * C, C), F32),
            pltpu.VMEM((LAYERS * TAPS * C, C), BF),
            pltpu.VMEM((2 * LEN, C), BF),
            pltpu.SemaphoreType.DMA((LAYERS + 1,)),
        ],
        flops=1 << 32,
        limit=24,
    )

    got = crossed(send, "core", 2, 1)
    slab4, slab1 = shape((4, SLAB, C), BF), shape((1, SLAB, C), BF)
    parts = call(core_sum_kernel, [slab4] * 4, [keep, got])
    slot_grad, *parts = lax.optimization_barrier((slot_grad, *parts))
    returned = lax.all_to_all(
        slot_grad.reshape(8 * owners, 8, C // 2),
        ("y", "core", "x", "z"),
        split_axis=0,
        concat_axis=0,
        tiled=True,
    ).reshape(2 * owners * cap, C // 2)
    parts = [parts[0]] + [shifted(parts[k], "x", 4, k) for k in (1, 2, 3)]
    parts = call(four_sum_kernel, [slab1] * 4, parts)
    parts = [parts[0]] + [shifted(parts[k], "y", 4, k) for k in (1, 2, 3)]
    (part,) = call(four_sum_kernel, [slab1], parts)
    (part,) = call(
        four_sum_kernel, [slab1], [part] + [crossed(part, "z", 8, k) for k in (1, 2, 3)]
    )
    other = crossed(part, "z", 8, 6)
    part, returned = lax.optimization_barrier((part, returned))
    mine = call(
        scatter_kernel,
        shape((C, C), BF),
        [place] + targets + [returned],
        specs=[SMEM] + [VMEM] * 5,
        flops=1 << 30,
    )
    merged = call(merge_kernel, shape((C + SLAB, C), BF), [part, other, mine])
    merged = [merged] + [shifted(merged, "y", 4, -k) for k in (1, 2, 3)]
    across = [crossed(block, "core", 2, 1) for block in merged]
    parts = jnp.stack([block[C:] for block in merged])
    later = [shifted(parts, "x", 4, -k) for k in (1, 2, 3)]
    blocks = pltpu.VMEM((C + SLAB, C), BF)
    new_rows, next_accum = call(
        adagrad_kernel,
        [shape((rows, C), F32), shape((8, C), F32)],
        [place] + merged + across + [codes, scales, accum.reshape(rows, 1)],
        specs=[SMEM] + [ANY] * 8 + [HBM, VMEM, VMEM],
        out_specs=[HBM, VMEM],
        scratch=[blocks] * 8
        + [
            pltpu.VMEM((8, C, C), BF),
            pltpu.VMEM((8, C, C), F32),
            pltpu.SemaphoreType.DMA((8,)),
            pltpu.SemaphoreType.DMA((8,)),
            pltpu.SemaphoreType.DMA((8,)),
        ],
        limit=12,
    )
    here = [(at, None, 0, at, 0) for at in range(4)]
    here += [(4 + at, None, 0, at, 1) for at in range(4)]
    filled = spread(place, merged + across, here)
    later, next_accum, filled = lax.optimization_barrier((later, next_accum, filled))
    beyond = [crossed(part, "core", 2, 1) for part in later]
    plan = [(at, inner, at + 1, inner, 0) for at in range(3) for inner in range(4)]
    filled = spread(place, later, plan, filled)
    plan = [(at, inner, at + 1, inner, 1) for at in range(3) for inner in range(4)]
    grad_conv, grad_gain = spread(place, beyond, plan, filled)
    return (
        new_rows,
        next_accum.reshape(rows),
        grad_conv.reshape(conv_weight.shape),
        grad_gain,
    )


def solution(mesh):
    fine = Mesh(mesh.devices.reshape(4, 8, 4, 2), ("x", "z", "y", "core"))
    every = ("x", "z", "y", "core")
    table = ("x", "z")
    return jax.shard_map(
        body,
        mesh=fine,
        in_specs=(
            P(every, None),
            P(every, None),
            P(every, None, None),
            P(every, None),
            P(table, None),
            P(table, None),
            P(table),
            P(),
            P(),
            P(every, None, None),
        ),
        out_specs=(P(table, None), P(table), P(), P()),
        check_vma=False,
    )
```

time: 161 us -> 150 us (0.932)
  local copies, waits for them, and re-layouts: 18 us -> 7.12 us
  Pallas kernels: 19.7 us -> 28.5 us
  starting transfers between devices: 76.9 us -> 70.1 us
  other arithmetic: 4.7 us -> 2.66 us
    all_to_all x1, waiting for transfers between devices: 12.2 us -> 1.85 us  [body(): lax.all_to_all(sending.reshape(owners, cap, C), table_axes, split_axis=0,...]
    ppermute x18 -> x15, waiting for transfers between devices: 9.53 us -> 19.7 us  [shifted(): lax.ppermute(values, axis, [(i, (i + offset) % size) for i in range(size)])]
    unnamed x48 -> x26, local copies, waits for them, and re-layouts: 16.2 us -> 6.14 us
    pallas_call x13 -> x12, Pallas kernels: 19.7 us -> 28.5 us  [the longest x9 18.8 us: call(): pl.pallas_call(kernel, out_shape=outs, in_specs=specs, out_specs=out_spec...]
    ppermute x18 -> x15, starting transfers between devices: 26.3 us -> 19.1 us  [shifted(): lax.ppermute(values, axis, [(i, (i + offset) % size) for i in range(size)])]
    all_to_all x1, waiting for transfers between devices: 5.9 us -> 0.01 us  [body(): lax.all_to_all(slot_grad.reshape(8 * owners, 8, C // 2), ('y', 'core', 'x...]
    ppermute x14 -> x13, waiting for transfers between devices: 7.07 us -> 12.4 us  [crossed(): return lax.ppermute(values, axis, [(i, i ^ bits) for i in range(size)])]
    all_to_all x1, starting transfers between devices: 4.95 us -> 8.52 us  [body(): lax.all_to_all(slot_grad.reshape(8 * owners, 8, C // 2), ('y', 'core', 'x...]
  transfers between devices with their start and end apart: 35 -> 31, of which waited for: 13 -> 14; matrix products, arithmetic and copies ran while one was open for 2% -> 3% of each run, Pallas kernels for 5% -> 10%
where the time goes in v2:
time: 150 us
  starting transfers between devices  70.1 us (47%)
  waiting for transfers between devices  39.8 us (27%)
  Pallas kernels  28.5 us (19%)
  local copies, waits for them, and re-layouts  7.12 us (5%)
  other arithmetic  2.66 us (2%)
  between operations  1.82 us (1%)
    ppermute x13, starting transfers between devices, crossed(): return lax.ppermute(values, axis, [(i, i ^ bits) for i in range(size)])  26.7 us
    ppermute x15, waiting for transfers between devices, shifted(): lax.ppermute(values, axis, [(i, (i + offset) % size) for i in range(size)])  19.7 us
    ppermute x15, starting transfers between devices, shifted(): lax.ppermute(values, axis, [(i, (i + offset) % size) for i in range(size)])  19.1 us
    pallas_call x9, Pallas kernels, call(): pl.pallas_call(kernel, out_shape=outs, in_specs=specs, out_specs=out_spec...  18.8 us
    ppermute x13, waiting for transfers between devices, crossed(): return lax.ppermute(values, axis, [(i, i ^ bits) for i in range(size)])  12.4 us
    all_to_all x1, starting transfers between devices, body(): lax.all_to_all(wanted, table_axes, split_axis=0, concat_axis=0, tiled=True)  11.9 us
    pallas_call x3, Pallas kernels, spread(): pl.pallas_call(functools.partial(spread_kernel, count, plan, before is No...  9.67 us
    all_to_all x1, starting transfers between devices, body(): lax.all_to_all(slot_grad.reshape(8 * owners, 8, C // 2), ('y', 'core', 'x...  8.52 us
  transfers between devices with their start and end apart: 31, of which 14 were waited for; matrix products, arithmetic and copies ran while one was open for 3% of the time, Pallas kernels for 10%

profile of v2, /device:TPU:1, one launch (start us, length us, event | category | flops | bytes accessed | tf_op | source)
XLA Modules:
  0.0 150.0 jit_solution(3842279788553442437)
XLA Ops:
  0.7 1.4 compare_select_fusion
  2.1 11.9 %all-to-all-start = ((s32[32,1,32]{2,1,0:T(1,128)}), s32[32,1,32]{2,1,0:T(1,128)S(1)}, u32[]{:S(2)}, u32[]{:S(2)}) async-start(s32[32,1,32]{2,1,0:T(1,128)} %compare_select_fusion), calls=%async_computation | async-start | bytes 32768 | tf_op jit(solution)/shard_map/all_to_all | solution.py:441
  14.2 1.1 copy.44.scales_hbm.refs_9_
  15.3 0.7 copy.54
  16.6 5.9 %all-to-all-done = s32[32,1,32]{2,1,0:T(1,128)S(1)} async-done(((s32[32,1,32]{2,1,0:T(1,128)}), s32[32,1,32]{2,1,0:T(1,128)S(1)}, u32[]{:S(2)}, u32[]{:S(2)}) %all-to-all-start) | async-done | bytes 4128 | tf_op jit(solution)/shard_map/all_to_all | solution.py:441
  22.5 1.2 copy-done
  23.7 2.8 %shard_map.129 = bf16[1024,256]{1,0:T(8,128)(2,1)} custom-call(s32[32,32]{1,0:T(8,128)S(1)} %bitcast.42, bf16[2048,256]{1,0:T(8,128)(2,1)S(1)} %copy-done, bf16[2048,8]{1,0:T(8,128)(2,1)S(1)} %copy.44.scales_hbm.refs_9_), custom_call_target="tpu_custom_call" | custom-call | flops 1073741824 | bytes 1048576 | tf_op jit(solution)/shard_map/pallas_call | solution.py:36
  26.6 3.9 %all-to-all-start.1 = ((bf16[32,32,256]{2,1,0:T(8,128)(2,1)}), bf16[32,32,256]{2,1,0:T(8,128)(2,1)S(1)}, u32[]{:S(2)}, u32[]{:S(2)}) async-start(bf16[32,32,256]{2,1,0:T(8,128)(2,1)} %bitcast.8), calls=%async_computation.1 | async-start | bytes 1048576 | tf_op jit(solution)/shard_map/all_to_all | solution.py:463
  31.3 2.2 %collective-permute-start = (s32[8,256]{1,0:T(8,128)S(1)}, s32[8,256]{1,0:T(8,128)S(1)}, u32[]{:S(2)}, u32[]{:S(2)}) collective-permute-start(s32[8,256]{1,0:T(8,128)S(1)} %add_select_fusion), channel_id=1, source_target_pairs={{0,1},{1,0},{2,3},{3,2},{4,5},{5,4},{6,7},{7,6},{8,9},{9,8},{10,11... | collective-permute-start | bytes 24584 | tf_op jit(solution)/shard_map/ppermute | solution.py:423
  33.5 0.8 collective-permute-done
  34.3 2.7 %collective-permute-start.1 = (s32[16,256]{1,0:T(8,128)S(1)}, s32[16,256]{1,0:T(8,128)S(1)}, u32[]{:S(2)}, u32[]{:S(2)}) collective-permute-start(s32[16,256]{1,0:T(8,128)S(1)} %pad_add_fusion.code_a), channel_id=1, source_target_pairs={{0,6},{2,0},{4,2},{6,4},{1,7},{3,1},{5,3},{7,5},{8,14},{10,8},{12,... | collective-permute-start | bytes 49160 | tf_op jit(solution)/shard_map/ppermute | solution.py:419
  37.4 0.7 collective-permute-start.3
  38.2 3.2 %collective-permute-done.2.code_c = s32[16,256]{1,0:T(8,128)S(1)} collective-permute-done((s32[16,256]{1,0:T(8,128)S(1)}, s32[16,256]{1,0:T(8,128)S(1)}, u32[]{:S(2)}, u32[]{:S(2)}) %collective-permute-start.2) | collective-permute-done | bytes 16416 | tf_op jit(solution)/shard_map/ppermute | solution.py:419
  41.6 1.8 %all-to-all-done.1 = bf16[32,32,256]{2,1,0:T(8,128)(2,1)S(1)} async-done(((bf16[32,32,256]{2,1,0:T(8,128)(2,1)}), bf16[32,32,256]{2,1,0:T(8,128)(2,1)S(1)}, u32[]{:S(2)}, u32[]{:S(2)}) %all-to-all-start.1) | async-done | bytes 524320 | tf_op jit(solution)/shard_map/all_to_all | solution.py:463
  43.4 7.9 %shard_map.130 = (bf16[2048,128]{1,0:T(8,128)(2,1)}, bf16[16,104,256]{2,1,0:T(8,128)(2,1)S(1)}, bf16[16,104,256]{2,1,0:T(8,128)(2,1)S(1)}) custom-call(s32[4]{0:T(128)S(1)} %pad_add_fusion.1.place_ref, s32[1,512]{1,0:T(1,128)S(1)} %bitcast.44, s32[1,320]{1,0:T(1,128)S(1)} %fusion.code_ref, bf16[1024,256]{1,0:T(8,128)(2,1)S(1)} %bitcast.41, ...), custom_call_target="tpu_custom_call" | custom-call | flops 4294967296 | bytes 1048576 | tf_op jit(solution)/shard_map/pallas_call | solution.py:36
  51.4 5.3 %collective-permute-start.4 = (bf16[16,104,256]{2,1,0:T(8,128)(2,1)S(1)}, bf16[16,104,256]{2,1,0:T(8,128)(2,1)S(1)}, u32[]{:S(2)}, u32[]{:S(2)}) collective-permute-start(bf16[16,104,256]{2,1,0:T(8,128)(2,1)S(1)} %get-tuple-element.44), channel_id=1, source_target_pairs={{0,1},{1,0},{2,3},{3,2},{4,5},{5,4},{6,7},{7,6},{8,9},{9,8},{10,11... | collective-permute-start | bytes 2555912 | tf_op jit(solution)/shard_map/ppermute | solution.py:423
  56.6 2.0 %collective-permute-done.4.got_ref = bf16[16,104,256]{2,1,0:T(8,128)(2,1)S(1)} collective-permute-done((bf16[16,104,256]{2,1,0:T(8,128)(2,1)S(1)}, bf16[16,104,256]{2,1,0:T(8,128)(2,1)S(1)}, u32[]{:S(2)}, u32[]{:S(2)}) %collective-permute-start.4) | collective-permute-done | bytes 852000 | tf_op jit(solution)/shard_map/ppermute | solution.py:423
  58.9 8.5 %all-to-all-start.2 = ((bf16[256,8,128]{2,1,0:T(8,128)(2,1)}), bf16[256,8,128]{2,1,0:T(8,128)(2,1)S(1)}, u32[]{:S(2)}, u32[]{:S(2)}) async-start(bf16[256,8,128]{2,1,0:T(8,128)(2,1)} %bitcast.16), calls=%async_computation.2 | async-start | bytes 1048576 | tf_op jit(solution)/shard_map/all_to_all | solution.py:509
  67.4 1.5 collective-permute-start.5
  68.9 2.4 %collective-permute-start.6 = (bf16[4,104,256]{2,1,0:T(8,128)(2,1)S(1)}, bf16[4,104,256]{2,1,0:T(8,128)(2,1)S(1)}, u32[]{:S(2)}, u32[]{:S(2)}) collective-permute-start(bf16[4,104,256]{2,1,0:T(8,128)(2,1)S(1)} %get-tuple-element.51), channel_id=1, source_target_pairs={{0,128},{64,192},{128,0},{192,64},{1,129},{65,193},{129,1},{193,65... | collective-permute-start | bytes 638984 | tf_op jit(solution)/shard_map/ppermute | solution.py:419
  71.3 1.2 collective-permute-start.7
  72.4 3.5 %collective-permute-done.5.b_ref = bf16[4,104,256]{2,1,0:T(8,128)(2,1)S(1)} collective-permute-done((bf16[4,104,256]{2,1,0:T(8,128)(2,1)S(1)}, bf16[4,104,256]{2,1,0:T(8,128)(2,1)S(1)}, u32[]{:S(2)}, u32[]{:S(2)}) %collective-permute-start.5) | collective-permute-done | bytes 213024 | tf_op jit(solution)/shard_map/ppermute | solution.py:419
  75.9 9.7 %collective-permute-done.6.c_ref = bf16[4,104,256]{2,1,0:T(8,128)(2,1)S(1)} collective-permute-done((bf16[4,104,256]{2,1,0:T(8,128)(2,1)S(1)}, bf16[4,104,256]{2,1,0:T(8,128)(2,1)S(1)}, u32[]{:S(2)}, u32[]{:S(2)}) %collective-permute-start.6) | collective-permute-done | bytes 213024 | tf_op jit(solution)/shard_map/ppermute | solution.py:419
  85.7 2.6 %collective-permute-start.10 = (bf16[1,104,256]{2,1,0:T(8,128)(2,1)S(1)}, bf16[1,104,256]{2,1,0:T(8,128)(2,1)S(1)}, u32[]{:S(2)}, u32[]{:S(2)}) collective-permute-start(bf16[1,104,256]{2,1,0:T(8,128)(2,1)S(1)} %get-tuple-element.56), channel_id=1, source_target_pairs={{0,6},{2,0},{4,2},{6,4},{1,7},{3,1},{5,3},{7,5},{8,14},{10,8},{12,... | collective-permute-start | bytes 159752 | tf_op jit(solution)/shard_map/ppermute | solution.py:419
  88.4 1.7 %collective-permute-start.9 = (bf16[1,104,256]{2,1,0:T(8,128)(2,1)S(1)}, bf16[1,104,256]{2,1,0:T(8,128)(2,1)S(1)}, u32[]{:S(2)}, u32[]{:S(2)}) collective-permute-start(bf16[1,104,256]{2,1,0:T(8,128)(2,1)S(1)} %get-tuple-element.55), channel_id=1, source_target_pairs={{0,4},{2,6},{4,0},{6,2},{1,5},{3,7},{5,1},{7,3},{8,12},{10,14},{12... | collective-permute-start | bytes 159752 | tf_op jit(solution)/shard_map/ppermute | solution.py:419
  90.1 3.1 %collective-permute-done.8.b_ref = bf16[1,104,256]{2,1,0:T(8,128)(2,1)S(1)} collective-permute-done((bf16[1,104,256]{2,1,0:T(8,128)(2,1)S(1)}, bf16[1,104,256]{2,1,0:T(8,128)(2,1)S(1)}, u32[]{:S(2)}, u32[]{:S(2)}) %collective-permute-start.8) | collective-permute-done | bytes 53280 | tf_op jit(solution)/shard_map/ppermute | solution.py:419
  93.2 1.1 collective-permute-start.11
  94.3 2.7 %collective-permute-start.12 = (bf16[1,104,256]{2,1,0:T(8,128)(2,1)S(1)}, bf16[1,104,256]{2,1,0:T(8,128)(2,1)S(1)}, u32[]{:S(2)}, u32[]{:S(2)}) collective-permute-start(bf16[1,104,256]{2,1,0:T(8,128)(2,1)S(1)} %shard_map.133.a_ref), channel_id=1, source_target_pairs={{0,16},{8,24},{16,0},{24,8},{32,48},{40,56},{48,32},{56,40},{1,17}... | collective-permute-start | bytes 159752 | tf_op jit(solution)/shard_map/ppermute | solution.py:423
  97.1 2.2 %collective-permute-done.12.c_ref = bf16[1,104,256]{2,1,0:T(8,128)(2,1)S(1)} collective-permute-done((bf16[1,104,256]{2,1,0:T(8,128)(2,1)S(1)}, bf16[1,104,256]{2,1,0:T(8,128)(2,1)S(1)}, u32[]{:S(2)}, u32[]{:S(2)}) %collective-permute-start.12) | collective-permute-done | bytes 53280 | tf_op jit(solution)/shard_map/ppermute | solution.py:423
  99.3 3.0 %collective-permute-done.13.d_ref = bf16[1,104,256]{2,1,0:T(8,128)(2,1)S(1)} collective-permute-done((bf16[1,104,256]{2,1,0:T(8,128)(2,1)S(1)}, bf16[1,104,256]{2,1,0:T(8,128)(2,1)S(1)}, u32[]{:S(2)}, u32[]{:S(2)}) %collective-permute-start.13) | collective-permute-done | bytes 53280 | tf_op jit(solution)/shard_map/ppermute | solution.py:423
  102.3 0.7 collective-permute-start.14
  103.0 1.2 shard_map.135.rows_ref
  104.3 3.2 %collective-permute-done.14.b_ref = bf16[1,104,256]{2,1,0:T(8,128)(2,1)S(1)} collective-permute-done((bf16[1,104,256]{2,1,0:T(8,128)(2,1)S(1)}, bf16[1,104,256]{2,1,0:T(8,128)(2,1)S(1)}, u32[]{:S(2)}, u32[]{:S(2)}) %collective-permute-start.14) | collective-permute-done | bytes 53280 | tf_op jit(solution)/shard_map/ppermute | solution.py:423
  107.5 2.6 %collective-permute-start.15 = (bf16[360,256]{1,0:T(8,128)(2,1)S(1)}, bf16[360,256]{1,0:T(8,128)(2,1)S(1)}, u32[]{:S(2)}, u32[]{:S(2)}) collective-permute-start(bf16[360,256]{1,0:T(8,128)(2,1)S(1)} %shard_map.136.refs_0_), channel_id=1, source_target_pairs={{0,6},{2,0},{4,2},{6,4},{1,7},{3,1},{5,3},{7,5},{8,14},{10,8},{12,... | collective-permute-start | bytes 552968 | tf_op jit(solution)/shard_map/ppermute | solution.py:419
  110.2 0.7 collective-permute-start.17
  110.8 5.3 %collective-permute-start.18 = (bf16[360,256]{1,0:T(8,128)(2,1)S(1)}, bf16[360,256]{1,0:T(8,128)(2,1)S(1)}, u32[]{:S(2)}, u32[]{:S(2)}) collective-permute-start(bf16[360,256]{1,0:T(8,128)(2,1)S(1)} %shard_map.136.refs_0_), channel_id=1, source_target_pairs={{0,1},{1,0},{2,3},{3,2},{4,5},{5,4},{6,7},{7,6},{8,9},{9,8},{10,11... | collective-permute-start | bytes 552968 | tf_op jit(solution)/shard_map/ppermute | solution.py:423
  116.2 4.1 %collective-permute-start.19 = (bf16[360,256]{1,0:T(8,128)(2,1)S(1)}, bf16[360,256]{1,0:T(8,128)(2,1)S(1)}, u32[]{:S(2)}, u32[]{:S(2)}) collective-permute-start(bf16[360,256]{1,0:T(8,128)(2,1)S(1)} %collective-permute-done.15.refs_1_), channel_id=1, source_target_pairs={{0,1},{1,0},{2,3},{3,2},{4,5},{5,4},{6,7},{7,6},{8,9},{9,8},{10,11... | collective-permute-start | bytes 552968 | tf_op jit(solution)/shard_map/ppermute | solution.py:423
  120.3 0.7 pad_maximum_fusion
  121.0 1.4 collective-permute-start.22
  122.4 1.1 collective-permute-start.23
  123.7 4.5 %collective-permute-start.20 = (bf16[360,256]{1,0:T(8,128)(2,1)S(1)}, bf16[360,256]{1,0:T(8,128)(2,1)}, u32[]{:S(2)}, u32[]{:S(2)}) collective-permute-start(bf16[360,256]{1,0:T(8,128)(2,1)S(1)} %collective-permute-done.16.refs_2_), channel_id=1, source_target_pairs={{0,1},{1,0},{2,3},{3,2},{4,5},{5,4},{6,7},{7,6},{8,9},{9,8},{10,11... | collective-permute-start | bytes 552968 | tf_op jit(solution)/shard_map/ppermute | solution.py:423
  129.4 1.0 collective-permute-done.21.refs_7_
  130.4 0.9 copy-done.3
  131.4 4.0 %shard_map.138 = (f32[3072,256]{1,0:T(8,128)}, f32[4,256]{1,0:T(4,128)S(1)}) custom-call(s32[4]{0:T(128)S(1)} %pad_add_fusion.1.place_ref, bf16[360,256]{1,0:T(8,128)(2,1)S(1)} %shard_map.136.refs_0_, bf16[360,256]{1,0:T(8,128)(2,1)S(1)} %collective-permute-done.15.refs_1_, bf16[360,256]{1,0:T(8,128)(2,1)S(1)} %collective-permute-done.16.refs_2_, ...), custom_call_target="tpu_custom_call" | custom-call | bytes 2097152 | tf_op jit(solution)/shard_map/pallas_call | solution.py:347
  135.4 0.9 copy-done.4
  136.3 6.4 %shard_map.137 = (f32[2048,256]{1,0:T(8,128)}, f32[8,256]{1,0:T(8,128)S(1)}) custom-call(s32[4]{0:T(128)S(1)} %pad_add_fusion.1.place_ref, bf16[360,256]{1,0:T(8,128)(2,1)S(1)} %shard_map.136.refs_0_, bf16[360,256]{1,0:T(8,128)(2,1)S(1)} %collective-permute-done.15.refs_1_, bf16[360,256]{1,0:T(8,128)(2,1)S(1)} %collective-permute-done.16.refs_2_, ...), custom_call_target="tpu_custom_call" | custom-call | bytes 1048576 | tf_op jit(solution)/shard_map/pallas_call | solution.py:36
  144.0 2.6 %shard_map.139 = (f32[3072,256]{1,0:T(8,128)}, f32[4,256]{1,0:T(4,128)S(1)}) custom-call(s32[4]{0:T(128)S(1)} %pad_add_fusion.1.place_ref, bf16[4,104,256]{2,1,0:T(8,128)(2,1)} %collective-permute-done.22.refs_0_, bf16[4,104,256]{2,1,0:T(8,128)(2,1)} %collective-permute-done.23.refs_1_, ...), custom_call_target="tpu_custom_call", output_to_operand_aliasing={{0}: (4, {})} | custom-call | bytes 2097152 | tf_op jit(solution)/shard_map/pallas_call | solution.py:347
  146.7 3.1 %shard_map.140 = (f32[3072,256]{1,0:T(8,128)}, f32[4,256]{1,0:T(4,128)}) custom-call(s32[4]{0:T(128)S(1)} %pad_add_fusion.1.place_ref, bf16[4,104,256]{2,1,0:T(8,128)(2,1)S(1)} %collective-permute-done.25.refs_0_, bf16[4,104,256]{2,1,0:T(8,128)(2,1)S(1)} %collective-permute-done.26.refs_1_, ...), custom_call_target="tpu_custom_call", output_to_operand_aliasing={{0}: (4, {})} | custom-call | bytes 2097152 | tf_op jit(solution)/shard_map/pallas_call | solution.py:347
  (80 shorter events, 4.9 us)
Async XLA Ops:
  0.6 29.8 %copy-start.10 = (s32[1,2]{1,0:T(1,128)S(1)}, s32[1,2]{1,0:T(1,128)}, u32[]{:S(2)}) copy-start(s32[1,2]{1,0:T(1,128)} %param.10) | copy-start | bytes 28
  2.1 20.4 %all-to-all-start = ((s32[32,1,32]{2,1,0:T(1,128)}), s32[32,1,32]{2,1,0:T(1,128)S(1)}, u32[]{:S(2)}, u32[]{:S(2)}) async-start(s32[32,1,32]{2,1,0:T(1,128)} %compare_select_fusion), calls=%async_computation | async-start | bytes 32768 | tf_op jit(solution)/shard_map/all_to_all | solution.py:441
  14.2 24.0 %copy-start.9 = (s32[2,256]{1,0:T(2,128)S(1)}, s32[2,256]{1,0:T(2,128)}, u32[]{:S(2)}) copy-start(s32[2,256]{1,0:T(2,128)} %param.11) | copy-start | bytes 6148
  14.2 29.2 %copy-start.6 = (bf16[2,256,256]{2,1,0:T(8,128)(2,1)S(1)}, bf16[2,256,256]{2,1,0:T(8,128)(2,1)}, u32[]{:S(2)}) copy-start(bf16[2,256,256]{2,1,0:T(8,128)(2,1)} %param.19) | copy-start | bytes 786436
  14.2 29.2 %copy-start.7 = (f32[4,256]{1,0:T(4,128)S(1)}, f32[4,256]{1,0:T(4,128)}, u32[]{:S(2)}) copy-start(f32[4,256]{1,0:T(4,128)} %gain_ref.1) | copy-start | bytes 12292
  22.5 1.2 copy-start
  23.7 19.7 %copy-start.5 = (bf16[4,3,256,256]{3,2,1,0:T(8,128)(2,1)S(1)}, bf16[4,3,256,256]{3,2,1,0:T(8,128)(2,1)}, u32[]{:S(2)}) copy-start(bf16[4,3,256,256]{3,2,1,0:T(8,128)(2,1)} %param.17) | copy-start | bytes 4718596
  26.6 16.9 %all-to-all-start.1 = ((bf16[32,32,256]{2,1,0:T(8,128)(2,1)}), bf16[32,32,256]{2,1,0:T(8,128)(2,1)S(1)}, u32[]{:S(2)}, u32[]{:S(2)}) async-start(bf16[32,32,256]{2,1,0:T(8,128)(2,1)} %bitcast.8), calls=%async_computation.1 | async-start | bytes 1048576 | tf_op jit(solution)/shard_map/all_to_all | solution.py:463
  31.3 3.0 %collective-permute-start = (s32[8,256]{1,0:T(8,128)S(1)}, s32[8,256]{1,0:T(8,128)S(1)}, u32[]{:S(2)}, u32[]{:S(2)}) collective-permute-start(s32[8,256]{1,0:T(8,128)S(1)} %add_select_fusion), channel_id=1, source_target_pairs={{0,1},{1,0},{2,3},{3,2},{4,5},{5,4},{6,7},{7,6},{8,9},{9,8},{10,11... | collective-permute-start | bytes 24584 | tf_op jit(solution)/shard_map/ppermute | solution.py:423
  34.3 3.9 %collective-permute-start.1 = (s32[16,256]{1,0:T(8,128)S(1)}, s32[16,256]{1,0:T(8,128)S(1)}, u32[]{:S(2)}, u32[]{:S(2)}) collective-permute-start(s32[16,256]{1,0:T(8,128)S(1)} %pad_add_fusion.code_a), channel_id=1, source_target_pairs={{0,6},{2,0},{4,2},{6,4},{1,7},{3,1},{5,3},{7,5},{8,14},{10,8},{12,... | collective-permute-start | bytes 49160 | tf_op jit(solution)/shard_map/ppermute | solution.py:419
  37.0 4.4 %collective-permute-start.2 = (s32[16,256]{1,0:T(8,128)S(1)}, s32[16,256]{1,0:T(8,128)S(1)}, u32[]{:S(2)}, u32[]{:S(2)}) collective-permute-start(s32[16,256]{1,0:T(8,128)S(1)} %pad_add_fusion.code_a), channel_id=1, source_target_pairs={{0,4},{2,6},{4,0},{6,2},{1,5},{3,7},{5,1},{7,3},{8,12},{10,14},{12... | collective-permute-start | bytes 49160 | tf_op jit(solution)/shard_map/ppermute | solution.py:419
  37.4 4.2 %collective-permute-start.3 = (s32[16,256]{1,0:T(8,128)S(1)}, s32[16,256]{1,0:T(8,128)S(1)}, u32[]{:S(2)}, u32[]{:S(2)}) collective-permute-start(s32[16,256]{1,0:T(8,128)S(1)} %pad_add_fusion.code_a), channel_id=1, source_target_pairs={{0,2},{2,4},{4,6},{6,0},{1,3},{3,5},{5,7},{7,1},{8,10},{10,12},{12... | collective-permute-start | bytes 49160 | tf_op jit(solution)/shard_map/ppermute | solution.py:419
  51.4 7.3 %collective-permute-start.4 = (bf16[16,104,256]{2,1,0:T(8,128)(2,1)S(1)}, bf16[16,104,256]{2,1,0:T(8,128)(2,1)S(1)}, u32[]{:S(2)}, u32[]{:S(2)}) collective-permute-start(bf16[16,104,256]{2,1,0:T(8,128)(2,1)S(1)} %get-tuple-element.44), channel_id=1, source_target_pairs={{0,1},{1,0},{2,3},{3,2},{4,5},{5,4},{6,7},{7,6},{8,9},{9,8},{10,11... | collective-permute-start | bytes 2555912 | tf_op jit(solution)/shard_map/ppermute | solution.py:423
  58.9 44.2 %all-to-all-start.2 = ((bf16[256,8,128]{2,1,0:T(8,128)(2,1)}), bf16[256,8,128]{2,1,0:T(8,128)(2,1)S(1)}, u32[]{:S(2)}, u32[]{:S(2)}) async-start(bf16[256,8,128]{2,1,0:T(8,128)(2,1)} %bitcast.16), calls=%async_computation.2 | async-start | bytes 1048576 | tf_op jit(solution)/shard_map/all_to_all | solution.py:509
  67.4 61.5 %copy-start.8 = (f32[2048]{0:T(1024)S(1)}, f32[2048]{0:T(1024)}, u32[]{:S(2)}) copy-start(f32[2048]{0:T(1024)} %param.16) | copy-start | bytes 24580
  67.4 8.5 %collective-permute-start.5 = (bf16[4,104,256]{2,1,0:T(8,128)(2,1)S(1)}, bf16[4,104,256]{2,1,0:T(8,128)(2,1)S(1)}, u32[]{:S(2)}, u32[]{:S(2)}) collective-permute-start(bf16[4,104,256]{2,1,0:T(8,128)(2,1)S(1)} %get-tuple-element.50), channel_id=1, source_target_pairs={{0,64},{64,128},{128,192},{192,0},{1,65},{65,129},{129,193},{193,1... | collective-permute-start | bytes 638984 | tf_op jit(solution)/shard_map/ppermute | solution.py:419
  68.9 16.7 %collective-permute-start.6 = (bf16[4,104,256]{2,1,0:T(8,128)(2,1)S(1)}, bf16[4,104,256]{2,1,0:T(8,128)(2,1)S(1)}, u32[]{:S(2)}, u32[]{:S(2)}) collective-permute-start(bf16[4,104,256]{2,1,0:T(8,128)(2,1)S(1)} %get-tuple-element.51), channel_id=1, source_target_pairs={{0,128},{64,192},{128,0},{192,64},{1,129},{65,193},{129,1},{193,65... | collective-permute-start | bytes 638984 | tf_op jit(solution)/shard_map/ppermute | solution.py:419
  71.3 14.3 %collective-permute-start.7 = (bf16[4,104,256]{2,1,0:T(8,128)(2,1)S(1)}, bf16[4,104,256]{2,1,0:T(8,128)(2,1)S(1)}, u32[]{:S(2)}, u32[]{:S(2)}) collective-permute-start(bf16[4,104,256]{2,1,0:T(8,128)(2,1)S(1)} %get-tuple-element.52), channel_id=1, source_target_pairs={{0,192},{64,0},{128,64},{192,128},{1,193},{65,1},{129,65},{193,129... | collective-permute-start | bytes 638984 | tf_op jit(solution)/shard_map/ppermute | solution.py:419
  85.7 4.3 %collective-permute-start.10 = (bf16[1,104,256]{2,1,0:T(8,128)(2,1)S(1)}, bf16[1,104,256]{2,1,0:T(8,128)(2,1)S(1)}, u32[]{:S(2)}, u32[]{:S(2)}) collective-permute-start(bf16[1,104,256]{2,1,0:T(8,128)(2,1)S(1)} %get-tuple-element.56), channel_id=1, source_target_pairs={{0,6},{2,0},{4,2},{6,4},{1,7},{3,1},{5,3},{7,5},{8,14},{10,8},{12,... | collective-permute-start | bytes 159752 | tf_op jit(solution)/shard_map/ppermute | solution.py:419
  88.4 4.8 %collective-permute-start.8 = (bf16[1,104,256]{2,1,0:T(8,128)(2,1)S(1)}, bf16[1,104,256]{2,1,0:T(8,128)(2,1)S(1)}, u32[]{:S(2)}, u32[]{:S(2)}) collective-permute-start(bf16[1,104,256]{2,1,0:T(8,128)(2,1)S(1)} %get-tuple-element.54), channel_id=1, source_target_pairs={{0,2},{2,4},{4,6},{6,0},{1,3},{3,5},{5,7},{7,1},{8,10},{10,12},{12... | collective-permute-start | bytes 159752 | tf_op jit(solution)/shard_map/ppermute | solution.py:419
  88.4 4.8 %collective-permute-start.9 = (bf16[1,104,256]{2,1,0:T(8,128)(2,1)S(1)}, bf16[1,104,256]{2,1,0:T(8,128)(2,1)S(1)}, u32[]{:S(2)}, u32[]{:S(2)}) collective-permute-start(bf16[1,104,256]{2,1,0:T(8,128)(2,1)S(1)} %get-tuple-element.55), channel_id=1, source_target_pairs={{0,4},{2,6},{4,0},{6,2},{1,5},{3,7},{5,1},{7,3},{8,12},{10,14},{12... | collective-permute-start | bytes 159752 | tf_op jit(solution)/shard_map/ppermute | solution.py:419
  93.2 3.9 %collective-permute-start.11 = (bf16[1,104,256]{2,1,0:T(8,128)(2,1)S(1)}, bf16[1,104,256]{2,1,0:T(8,128)(2,1)S(1)}, u32[]{:S(2)}, u32[]{:S(2)}) collective-permute-start(bf16[1,104,256]{2,1,0:T(8,128)(2,1)S(1)} %shard_map.133.a_ref), channel_id=1, source_target_pairs={{0,8},{8,0},{16,24},{24,16},{32,40},{40,32},{48,56},{56,48},{1,9},... | collective-permute-start | bytes 159752 | tf_op jit(solution)/shard_map/ppermute | solution.py:423
  94.3 4.9 %collective-permute-start.12 = (bf16[1,104,256]{2,1,0:T(8,128)(2,1)S(1)}, bf16[1,104,256]{2,1,0:T(8,128)(2,1)S(1)}, u32[]{:S(2)}, u32[]{:S(2)}) collective-permute-start(bf16[1,104,256]{2,1,0:T(8,128)(2,1)S(1)} %shard_map.133.a_ref), channel_id=1, source_target_pairs={{0,16},{8,24},{16,0},{24,8},{32,48},{40,56},{48,32},{56,40},{1,17}... | collective-permute-start | bytes 159752 | tf_op jit(solution)/shard_map/ppermute | solution.py:423
  97.1 5.2 %collective-permute-start.13 = (bf16[1,104,256]{2,1,0:T(8,128)(2,1)S(1)}, bf16[1,104,256]{2,1,0:T(8,128)(2,1)S(1)}, u32[]{:S(2)}, u32[]{:S(2)}) collective-permute-start(bf16[1,104,256]{2,1,0:T(8,128)(2,1)S(1)} %shard_map.133.a_ref), channel_id=1, source_target_pairs={{0,24},{8,16},{16,8},{24,0},{32,56},{40,48},{48,40},{56,32},{1,25}... | collective-permute-start | bytes 159752 | tf_op jit(solution)/shard_map/ppermute | solution.py:423
  102.3 5.2 %collective-permute-start.14 = (bf16[1,104,256]{2,1,0:T(8,128)(2,1)S(1)}, bf16[1,104,256]{2,1,0:T(8,128)(2,1)S(1)}, u32[]{:S(2)}, u32[]{:S(2)}) collective-permute-start(bf16[1,104,256]{2,1,0:T(8,128)(2,1)S(1)} %shard_map.134.a_ref), channel_id=1, source_target_pairs={{0,48},{8,56},{16,32},{24,40},{32,16},{40,24},{48,0},{56,8},{1,49}... | collective-permute-start | bytes 159752 | tf_op jit(solution)/shard_map/ppermute | solution.py:423
  103.0 32.3 %copy-start.1 = (bf16[2048,256]{1,0:T(8,128)(2,1)S(1)}, bf16[2048,256]{1,0:T(8,128)(2,1)}, u32[]{:S(2)}) copy-start(bf16[2048,256]{1,0:T(8,128)(2,1)} %refs_8_.1) | copy-start | bytes 3145732
  107.5 8.7 %collective-permute-start.15 = (bf16[360,256]{1,0:T(8,128)(2,1)S(1)}, bf16[360,256]{1,0:T(8,128)(2,1)S(1)}, u32[]{:S(2)}, u32[]{:S(2)}) collective-permute-start(bf16[360,256]{1,0:T(8,128)(2,1)S(1)} %shard_map.136.refs_0_), channel_id=1, source_target_pairs={{0,6},{2,0},{4,2},{6,4},{1,7},{3,1},{5,3},{7,5},{8,14},{10,8},{12,... | collective-permute-start | bytes 552968 | tf_op jit(solution)/shard_map/ppermute | solution.py:419
  110.2 10.1 %collective-permute-start.16 = (bf16[360,256]{1,0:T(8,128)(2,1)S(1)}, bf16[360,256]{1,0:T(8,128)(2,1)S(1)}, u32[]{:S(2)}, u32[]{:S(2)}) collective-permute-start(bf16[360,256]{1,0:T(8,128)(2,1)S(1)} %shard_map.136.refs_0_), channel_id=1, source_target_pairs={{0,4},{2,6},{4,0},{6,2},{1,5},{3,7},{5,1},{7,3},{8,12},{10,14},{12... | collective-permute-start | bytes 552968 | tf_op jit(solution)/shard_map/ppermute | solution.py:419
  110.2 10.1 %collective-permute-start.17 = (bf16[360,256]{1,0:T(8,128)(2,1)S(1)}, bf16[360,256]{1,0:T(8,128)(2,1)S(1)}, u32[]{:S(2)}, u32[]{:S(2)}) collective-permute-start(bf16[360,256]{1,0:T(8,128)(2,1)S(1)} %shard_map.136.refs_0_), channel_id=1, source_target_pairs={{0,2},{2,4},{4,6},{6,0},{1,3},{3,5},{5,7},{7,1},{8,10},{10,12},{12... | collective-permute-start | bytes 552968 | tf_op jit(solution)/shard_map/ppermute | solution.py:419
  110.8 12.8 %collective-permute-start.18 = (bf16[360,256]{1,0:T(8,128)(2,1)S(1)}, bf16[360,256]{1,0:T(8,128)(2,1)S(1)}, u32[]{:S(2)}, u32[]{:S(2)}) collective-permute-start(bf16[360,256]{1,0:T(8,128)(2,1)S(1)} %shard_map.136.refs_0_), channel_id=1, source_target_pairs={{0,1},{1,0},{2,3},{3,2},{4,5},{5,4},{6,7},{7,6},{8,9},{9,8},{10,11... | collective-permute-start | bytes 552968 | tf_op jit(solution)/shard_map/ppermute | solution.py:423
  116.2 12.0 %collective-permute-start.19 = (bf16[360,256]{1,0:T(8,128)(2,1)S(1)}, bf16[360,256]{1,0:T(8,128)(2,1)S(1)}, u32[]{:S(2)}, u32[]{:S(2)}) collective-permute-start(bf16[360,256]{1,0:T(8,128)(2,1)S(1)} %collective-permute-done.15.refs_1_), channel_id=1, source_target_pairs={{0,1},{1,0},{2,3},{3,2},{4,5},{5,4},{6,7},{7,6},{8,9},{9,8},{10,11... | collective-permute-start | bytes 552968 | tf_op jit(solution)/shard_map/ppermute | solution.py:423
  121.0 21.6 %collective-permute-start.22 = (bf16[4,104,256]{2,1,0:T(8,128)(2,1)}, bf16[4,104,256]{2,1,0:T(8,128)(2,1)}, u32[]{:S(2)}, u32[]{:S(2)}) collective-permute-start(bf16[4,104,256]{2,1,0:T(8,128)(2,1)} %pad_maximum_fusion), channel_id=1, source_target_pairs={{0,192},{64,0},{128,64},{192,128},{1,193},{65,1},{129,65},{193,129... | collective-permute-start | bytes 638984 | tf_op jit(solution)/shard_map/ppermute | solution.py:419
  122.4 20.2 %collective-permute-start.23 = (bf16[4,104,256]{2,1,0:T(8,128)(2,1)}, bf16[4,104,256]{2,1,0:T(8,128)(2,1)}, u32[]{:S(2)}, u32[]{:S(2)}) collective-permute-start(bf16[4,104,256]{2,1,0:T(8,128)(2,1)} %pad_maximum_fusion), channel_id=1, source_target_pairs={{0,128},{64,192},{128,0},{192,64},{1,129},{65,193},{129,1},{193,65... | collective-permute-start | bytes 638984 | tf_op jit(solution)/shard_map/ppermute | solution.py:419
  123.5 19.2 %collective-permute-start.24 = (bf16[4,104,256]{2,1,0:T(8,128)(2,1)}, bf16[4,104,256]{2,1,0:T(8,128)(2,1)}, u32[]{:S(2)}, u32[]{:S(2)}) collective-permute-start(bf16[4,104,256]{2,1,0:T(8,128)(2,1)} %pad_maximum_fusion), channel_id=1, source_target_pairs={{0,64},{64,128},{128,192},{192,0},{1,65},{65,129},{129,193},{193,1... | collective-permute-start | bytes 638984 | tf_op jit(solution)/shard_map/ppermute | solution.py:419
  123.7 5.7 %collective-permute-start.20 = (bf16[360,256]{1,0:T(8,128)(2,1)S(1)}, bf16[360,256]{1,0:T(8,128)(2,1)}, u32[]{:S(2)}, u32[]{:S(2)}) collective-permute-start(bf16[360,256]{1,0:T(8,128)(2,1)S(1)} %collective-permute-done.16.refs_2_), channel_id=1, source_target_pairs={{0,1},{1,0},{2,3},{3,2},{4,5},{5,4},{6,7},{7,6},{8,9},{9,8},{10,11... | collective-permute-start | bytes 552968 | tf_op jit(solution)/shard_map/ppermute | solution.py:423
  128.2 0.7 copy-start.2
  128.9 1.6 %collective-permute-start.21 = (bf16[360,256]{1,0:T(8,128)(2,1)S(1)}, bf16[360,256]{1,0:T(8,128)(2,1)}, u32[]{:S(2)}, u32[]{:S(2)}) collective-permute-start(bf16[360,256]{1,0:T(8,128)(2,1)S(1)} %collective-permute-done.17.refs_3_), channel_id=1, source_target_pairs={{0,1},{1,0},{2,3},{3,2},{4,5},{5,4},{6,7},{7,6},{8,9},{9,8},{10,11... | collective-permute-start | bytes 552968 | tf_op jit(solution)/shard_map/ppermute | solution.py:423
  130.4 0.9 copy-start.3
  135.3 0.9 copy-start.4
  142.7 4.0 %collective-permute-start.25 = (bf16[4,104,256]{2,1,0:T(8,128)(2,1)}, bf16[4,104,256]{2,1,0:T(8,128)(2,1)S(1)}, u32[]{:S(2)}, u32[]{:S(2)}) collective-permute-start(bf16[4,104,256]{2,1,0:T(8,128)(2,1)} %collective-permute-done.22.refs_0_), channel_id=1, source_target_pairs={{0,1},{1,0},{2,3},{3,2},{4,5},{5,4},{6,7},{7,6},{8,9},{9,8},{10,11... | collective-permute-start | bytes 638984 | tf_op jit(solution)/shard_map/ppermute | solution.py:423
  142.9 3.7 %collective-permute-start.26 = (bf16[4,104,256]{2,1,0:T(8,128)(2,1)}, bf16[4,104,256]{2,1,0:T(8,128)(2,1)S(1)}, u32[]{:S(2)}, u32[]{:S(2)}) collective-permute-start(bf16[4,104,256]{2,1,0:T(8,128)(2,1)} %collective-permute-done.23.refs_1_), channel_id=1, source_target_pairs={{0,1},{1,0},{2,3},{3,2},{4,5},{5,4},{6,7},{7,6},{8,9},{9,8},{10,11... | collective-permute-start | bytes 638984 | tf_op jit(solution)/shard_map/ppermute | solution.py:423
  143.3 3.4 %collective-permute-start.27 = (bf16[4,104,256]{2,1,0:T(8,128)(2,1)}, bf16[4,104,256]{2,1,0:T(8,128)(2,1)S(1)}, u32[]{:S(2)}, u32[]{:S(2)}) collective-permute-start(bf16[4,104,256]{2,1,0:T(8,128)(2,1)} %collective-permute-done.24.refs_2_), channel_id=1, source_target_pairs={{0,1},{1,0},{2,3},{3,2},{4,5},{5,4},{6,7},{7,6},{8,9},{9,8},{10,11... | collective-permute-start | bytes 638984 | tf_op jit(solution)/shard_map/ppermute | solution.py:423

commit v3 on v1

v3 whole, which is shorter than its diff:
```python
import functools

import jax
import jax.numpy as jnp
from jax import lax
from jax.experimental import pallas as pl
from jax.experimental.pallas import tpu as pltpu
from jax.sharding import Mesh
from jax.sharding import PartitionSpec as P

DILATIONS = (1, 2, 4, 8)
LEARN_RATE = 0.5
BF = jnp.bfloat16
F32 = jnp.float32
LAYERS, TAPS, C = 4, 3, 256
GROUP = 32
LEN = 256
PACKED = 320
STEP = 64
PIECE = 96
TAIL = 8
SLAB = PIECE + TAIL
NT = (((1,), (1,)), ((), ()))
TN = (((0,), (0,)), ((), ()))
SMEM = pl.BlockSpec(memory_space=pltpu.SMEM)
VMEM = pl.BlockSpec(memory_space=pltpu.VMEM)
ANY = pl.BlockSpec(memory_space=pl.ANY)
HBM = pl.BlockSpec(memory_space=pltpu.HBM)


def call(kernel, outs, args, specs=None, out_specs=None, scratch=(), flops=0, limit=8):
    if specs is None:
        specs = [VMEM] * len(args)
    if out_specs is None:
        out_specs = jax.tree.map(lambda _: VMEM, outs)
    return pl.pallas_call(
        kernel,
        out_shape=outs,
        in_specs=specs,
        out_specs=out_specs,
        scratch_shapes=list(scratch),
        compiler_params=pltpu.CompilerParams(vmem_limit_bytes=limit * 1024 * 1024),
        cost_estimate=pl.CostEstimate(flops=flops, bytes_accessed=1 << 20, transcendentals=0),
    )(*args)


def shape(dims, dtype):
    return jax.ShapeDtypeStruct(dims, dtype)


def iota(dims, axis):
    return lax.broadcasted_iota(jnp.int32, dims, axis)


def spreader(groups):
    return (iota((groups, C), 1) // GROUP == iota((groups, C), 0)).astype(F32).astype(BF)


def dequantized(codes, scales, spread):
    return codes.astype(F32) * jnp.dot(scales, spread, preferred_element_type=F32)


def table_kernel(codes_ref, scales_ref, table_ref):
    spread = spreader(scales_ref.shape[1])
    for start in range(0, codes_ref.shape[0], 256):
        part = pl.ds(start, 256)
        table = dequantized(codes_ref[part, :], scales_ref[part, :], spread)
        table_ref[part, :] = table.astype(BF)


def fetch_kernel(asked_ref, table_ref, out_ref):
    senders, cap = asked_ref.shape
    stride = table_ref.shape[0] // cap
    asked = asked_ref[...].astype(F32).astype(BF)
    part, width = 8 * senders, 8 * stride
    pick = (iota((part, senders), 0) // 8 == iota((part, senders), 1)).astype(F32).astype(BF)
    lists = jnp.dot(pick, asked, preferred_element_type=F32)
    entry = iota((part, 1), 0) % 8
    halves = []
    for at in range(cap // 8):
        own = iota((part, cap), 1) == iota((part, cap), 0) % 8 + at * 8
        offset = jnp.sum(jnp.where(own, lists, 0.0), axis=1, keepdims=True).astype(jnp.int32)
        target = jnp.where(offset >= 0, entry * stride + offset, -1)
        chosen = (iota((part, width), 1) == target).astype(F32).astype(BF)
        got = jnp.dot(chosen, table_ref[pl.ds(at * width, width), :], preferred_element_type=F32)
        halves.append(got.reshape(senders, 8, C))
        if at % 2 == 1:
            both = jnp.concatenate(halves, axis=1)
            out_ref[:, pl.ds((at - 1) * 8, 16), :] = both.astype(BF)
            halves = []


def sigmoid(values):
    return 0.5 + 0.5 * jnp.tanh(0.5 * values)


def train_kernel(
    place_ref,
    slots_ref,
    code_ref,
    fetched_ref,
    gain_ref,
    upstream_ref,
    *refs,
):
    weight_refs, refs = refs[: LAYERS * TAPS], refs[LAYERS * TAPS :]
    slot_grad_ref, keep_ref, send_ref, held_ref, conv_ref, unit_ref = refs[:6]
    scale_ref, grad_ref, wide_ref, weight_grad_ref = refs[6:]
    split, x, y, core = place_ref[0], place_ref[1], place_ref[2], place_ref[3]
    steps = range(0, PACKED, STEP)
    line = iota((PACKED, C), 0)
    since = jnp.where(line >= split, line - split, line)
    until = jnp.where(line >= split, PACKED - line, split - line)

    source = iota((PACKED, 1), 0)
    source = jnp.where(source >= split, source + (LEN - split), source)
    match = iota((PACKED, 2 * LEN), 1) == source
    packer = match.astype(F32).astype(BF)
    slot = jnp.where(match, slots_ref[...].astype(F32), 0.0)
    slot = jnp.sum(slot, axis=1, keepdims=True).astype(jnp.int32)
    slots = fetched_ref.shape[0]
    chosen = (iota((PACKED, slots), 1) == slot).astype(F32).astype(BF)
    first = jnp.dot(chosen, fetched_ref[...], preferred_element_type=F32)
    held_ref[0] = first.astype(BF)

    for layer in range(LAYERS):
        gap = DILATIONS[layer]
        now = held_ref[layer].astype(F32)
        taps = [held_ref[layer]]
        for tap in (1, 2):
            moved = pltpu.roll(now, tap * gap, 0)
            taps.append(jnp.where(since >= tap * gap, moved, 0.0).astype(BF))
        conv_ref[...] = jnp.dot(
            jnp.concatenate(taps, axis=1),
            jnp.concatenate([ref[...] for ref in weight_refs[layer * TAPS :][:TAPS]], axis=0),
            preferred_element_type=F32,
        )
        gain = gain_ref[pl.ds(layer, 1), :]
        for start in steps:
            part = pl.ds(start, STEP)
            value = conv_ref[part, :]
            center = value - jnp.mean(value, axis=1, keepdims=True)
            spread = jnp.mean(center * center, axis=1, keepdims=True)
            scale = lax.rsqrt(spread + 1e-5)
            unit = center * scale
            unit_ref[layer, part, :] = unit
            scale_ref[layer, part, :] = jnp.broadcast_to(scale, (STEP, 128))
            if layer + 1 < LAYERS:
                gained = unit * gain
                after = gained * sigmoid(gained)
                if layer % 2 == 1:
                    after = after + held_ref[layer - 1, part, :].astype(F32)
                held_ref[layer + 1, part, :] = after.astype(BF)

    upstream = jnp.dot(packer, upstream_ref[...], preferred_element_type=F32)
    grad_ref[...] = upstream
    held_ref[5] = upstream.astype(BF)

    gain_rows = [None] * LAYERS
    for layer in reversed(range(LAYERS)):
        gap = DILATIONS[layer]
        gain = gain_ref[pl.ds(layer, 1), :]
        total = jnp.zeros((8, C), F32)
        for start in steps:
            part = pl.ds(start, STEP)
            unit = unit_ref[layer, part, :]
            scale = scale_ref[layer, part, :]
            gained = unit * gain
            gate = sigmoid(gained)
            inner = grad_ref[part, :] * (gate * (1.0 + gained * (1.0 - gate)))
            total = total + jnp.sum((inner * unit).reshape(STEP // 8, 8, C), axis=0)
            inner = inner * gain
            mean = jnp.mean(inner, axis=1, keepdims=True)
            slope = jnp.mean(inner * unit, axis=1, keepdims=True)
            outer = inner - mean - unit * slope
            conv_ref[part, :] = outer * jnp.concatenate([scale, scale], axis=1)
        gain_rows[layer] = jnp.sum(total, axis=0, keepdims=True)
        now = conv_ref[...]
        wide_ref[:, 0:C] = now.astype(BF)
        for tap in (1, 2):
            moved = pltpu.roll(now, PACKED - tap * gap, 0)
            moved = jnp.where(until > tap * gap, moved, 0.0)
            wide_ref[:, tap * C : (tap + 1) * C] = moved.astype(BF)

        below = jnp.zeros((PACKED, C), F32)
        for tap in range(TAPS):
            kernel = weight_refs[layer * TAPS + tap][...]
            below = below + lax.dot_general(
                wide_ref[:, tap * C : (tap + 1) * C], kernel, NT, preferred_element_type=F32
            )
        if layer % 2 == 0:
            if layer == 2:
                skip = held_ref[5].astype(F32)
            else:
                skip = held_ref[4].astype(F32)
            below = below + skip
        rounded = below.astype(BF)
        grad_ref[...] = rounded.astype(F32)
        if layer == 2:
            held_ref[4] = rounded

        weight_grad = lax.dot_general(
            held_ref[layer], wide_ref[...], TN, preferred_element_type=F32
        )
        for tap in range(TAPS):
            weight_grad_ref[pl.ds(tap * C, C), :] = weight_grad[:, tap * C : (tap + 1) * C]

        for pair in range(4):
            even = weight_grad_ref[pl.ds(2 * pair * PIECE, PIECE), :]
            odd = weight_grad_ref[pl.ds((2 * pair + 1) * PIECE, PIECE), :]
            tail = jnp.zeros((TAIL, C), F32)
            even_tail = tail
            if layer == 0 and pair == 0:
                exact = jnp.concatenate(gain_rows + gain_rows, axis=0)
                high = exact.astype(BF).astype(F32)
                even_tail = jnp.where(iota((TAIL, C), 0) < LAYERS, high, exact - high)
            even = jnp.concatenate([even, even_tail], axis=0)
            odd = jnp.concatenate([odd, tail], axis=0)
            place = ((pair - y + 4) % 4) * 4 + (layer - x + 4) % 4
            keep_ref[place] = jnp.where(core == 0, even, odd).astype(BF)
            send_ref[place] = jnp.where(core == 0, odd, even).astype(BF)

    mine = grad_ref[...].astype(BF)
    for start in range(0, slots, 256):
        here = iota((256, PACKED), 0) + start == code_ref[...]
        here = here.astype(F32).astype(BF)
        summed = jnp.dot(here, mine, preferred_element_type=F32)
        slot_grad_ref[pl.ds(start, 256), :] = summed.astype(BF)


def settle(total):
    tail = total[PIECE:SLAB, :]
    exact = tail + pltpu.roll(tail, LAYERS, 0)
    high = exact.astype(BF).astype(F32)
    tail = jnp.where(iota((TAIL, C), 0) < LAYERS, high, exact - high)
    return jnp.concatenate([total[:PIECE, :], tail], axis=0).astype(BF)


def core_sum_kernel(keep_ref, got_ref, *out_refs):
    for at in range(16):
        total = keep_ref[at].astype(F32) + got_ref[at].astype(F32)
        out_refs[at // 4][at % 4] = settle(total)


def four_sum_kernel(a_ref, b_ref, c_ref, d_ref, *out_refs):
    for at in range(a_ref.shape[0]):
        left = a_ref[at].astype(F32) + b_ref[at].astype(F32)
        right = c_ref[at].astype(F32) + d_ref[at].astype(F32)
        out_refs[at][0] = settle(left + right)


def last_sum_kernel(a_ref, b_ref, *refs):
    slab = settle(a_ref[0].astype(F32) + b_ref[0].astype(F32)).astype(F32)
    rows = refs[0][0].astype(F32) + refs[1][0].astype(F32)
    refs[2][...] = jnp.concatenate([rows, slab], axis=0).astype(BF)


def part_kernel(*refs):
    for at, ref in enumerate(refs[:4]):
        both = ref[...].astype(F32)
        refs[4][at] = both[:C].astype(BF)
        refs[5][at] = both[C:].astype(BF)


def spread_kernel(count, plan, first, place_ref, *refs):
    sources, refs = refs[:count], refs[count:]
    if not first:
        gain_before, refs = refs[1], refs[2:]
    conv_hbm, gain_ref, wide_ref, sems = refs
    x, y, core = place_ref[1], place_ref[2], place_ref[3]
    gain_ref[...] = jnp.zeros_like(gain_ref) if first else gain_before[...]
    leaving = []
    for at, (buffer, inner, along_x, along_y, other) in enumerate(plan):
        layer = (x + along_x) % 4
        side = core if other == 0 else 1 - core
        number = layer * 8 + ((y + along_y) % 4) * 2 + side
        block = sources[buffer][inner].astype(F32)
        wide_ref[at] = block[:PIECE, :]
        copy = pltpu.make_async_copy(
            wide_ref.at[at],
            conv_hbm.at[pl.ds(pl.multiple_of(number * PIECE, PIECE), PIECE)],
            sems.at[at],
        )
        copy.start()
        leaving.append(copy)

        @pl.when(number == 0)
        def _():
            tail = block[PIECE:, :]
            gain_ref[...] = (tail + pltpu.roll(tail, LAYERS, 0))[:LAYERS, :]

    for copy in leaving:
        copy.wait()


def spread(place, blocks, plan, before=None):
    outs = [shape((LAYERS * TAPS * C, C), F32), shape((LAYERS, C), F32)]
    count = len(blocks)
    args, specs, aliases = [place] + blocks, [SMEM] + [VMEM] * count, {}
    if before is not None:
        args, specs = args + list(before), specs + [HBM, VMEM]
        aliases = {count + 1: 0}
    return pl.pallas_call(
        functools.partial(spread_kernel, count, plan, before is None),
        out_shape=outs,
        in_specs=specs,
        out_specs=[HBM, VMEM],
        input_output_aliases=aliases,
        scratch_shapes=[
            pltpu.VMEM((len(plan), PIECE, C), F32),
            pltpu.SemaphoreType.DMA((len(plan),)),
        ],
        compiler_params=pltpu.CompilerParams(vmem_limit_bytes=8 * 1024 * 1024),
        cost_estimate=pl.CostEstimate(flops=0, bytes_accessed=1 << 21, transcendentals=0),
    )(*args)


def scatter_kernel(place_ref, code_ref, got_ref, keep_ref, send_ref):
    y, core = place_ref[2], place_ref[3]
    senders = got_ref.shape[0]
    lines = code_ref.shape[1]
    for pair in range(4):
        if pair % 2 == 0:
            both = got_ref[:, pl.ds(pair * 8, 16), :].astype(F32).reshape(senders, 2, 8, C)
        got = both[:, pair % 2].reshape(lines, C).astype(BF)
        here = iota((2 * C, lines), 0) + pair * 2 * C == code_ref[pl.ds(pair, 1), :]
        here = here.astype(F32).astype(BF)
        total = jnp.dot(here, got, preferred_element_type=F32)
        even, odd = total[:C], total[C:]
        apart = pair ^ y
        place = jnp.where(apart == 3, 1, jnp.where(apart == 0, 0, apart + 1))
        keep_ref[place] = jnp.where(core == 0, even, odd).astype(BF)
        send_ref[place] = jnp.where(core == 0, odd, even).astype(BF)


def row_sum_kernel(keep_ref, got_ref, *out_refs):
    half = keep_ref.shape[0] // 2
    total = (keep_ref[...].astype(F32) + got_ref[...].astype(F32)).astype(BF)
    out_refs[0][...] = total[:half]
    out_refs[1][...] = total[half:]


def adagrad_kernel(place_ref, *refs):
    own_ref, across_ref, codes_ref, scales_ref, accum_ref = refs[:5]
    rows_hbm, next_ref, rows_ref, sems = refs[5:]
    spread = spreader(scales_ref.shape[1])
    y, core = place_ref[2], place_ref[3]
    same = iota((C, C), 0) == iota((C, C), 1)
    half = C // 2
    leaving = []
    for at in range(8):
        side = core if at < 4 else 1 - core
        number = ((y + at % 4) % 4) * 2 + side
        part = pl.ds(pl.multiple_of(number * C, C), C)
        gradient = (own_ref[at] if at < 4 else across_ref[at - 4]).astype(F32)
        lines = [accum_ref[pl.ds(2 * number + side, 1), :] for side in range(2)]
        line = jnp.concatenate(lines, axis=1)
        grown = jnp.sum(jnp.where(same, line, 0.0), axis=1, keepdims=True)
        grown = grown + jnp.mean(gradient * gradient, axis=1, keepdims=True)
        table = dequantized(codes_ref[part, :], scales_ref[part, :], spread)
        rows_ref[at] = table - LEARN_RATE * gradient * lax.rsqrt(grown)
        copy = pltpu.make_async_copy(rows_ref.at[at], rows_hbm.at[part], sems.at[at])
        copy.start()
        leaving.append(copy)
        line = jnp.sum(jnp.where(same, grown, 0.0), axis=0, keepdims=True)
        next_ref[pl.ds(2 * number, 1), :] = line[:, :half]
        next_ref[pl.ds(2 * number + 1, 1), :] = line[:, half:]
    for copy in leaving:
        copy.wait()


def shifted(values, axis, size, offset):
    return lax.ppermute(values, axis, [(i, (i + offset) % size) for i in range(size)])


def crossed(values, axis, size, bits):
    return lax.ppermute(values, axis, [(i, i ^ bits) for i in range(size)])


def after(values, *others):
    return lax.optimization_barrier((values, *others))[0]


def body(lengths, slots, requests, counts, codes, scales, accum, conv_weight, norm_gain, upstream):
    table_axes = ("x", "z")
    owners = requests.shape[1]
    cap = requests.shape[2]
    rows = codes.shape[0]
    stride = rows // cap
    split = lengths[0, 0]
    place = jnp.stack(
        [split, lax.axis_index("x"), lax.axis_index("y"), lax.axis_index("core")]
    ).astype(jnp.int32)

    entry = jnp.arange(cap, dtype=jnp.int32)[None, :]
    wanted = jnp.where(entry < counts[0][:, None], requests[0] - entry * stride, -1)
    asked = lax.all_to_all(wanted, table_axes, split_axis=0, concat_axis=0, tiled=True)

    order = jnp.arange(PACKED, dtype=jnp.int32)
    order = order + jnp.where(order >= split, LEN - split, 0)
    match = order[:, None] == jnp.arange(2 * LEN, dtype=jnp.int32)[None, :]
    packed = jnp.sum(jnp.where(match, slots.reshape(1, 2 * LEN), 0), axis=1)

    table = call(table_kernel, shape((rows, C), BF), [codes, scales], flops=1 << 24)
    sending = call(
        fetch_kernel, shape((owners, cap, C), BF), [asked, table], flops=1 << 30
    )
    fetched = lax.all_to_all(
        sending, table_axes, split_axis=0, concat_axis=0, tiled=True
    ).reshape(owners * cap, C)

    target = jnp.where(asked >= 0, asked + entry * stride, -1)
    target = target.reshape(owners, 4, 8).transpose(1, 0, 2).reshape(4, 8 * owners)
    fetched, target = lax.optimization_barrier((fetched, target))

    slab16 = shape((16, SLAB, C), BF)
    slot_grad, keep, send = call(
        train_kernel,
        [shape((owners * cap, C), BF), slab16, slab16],
        [
            place,
            slots.reshape(1, 2 * LEN),
            packed.reshape(1, PACKED),
            fetched,
            norm_gain,
            upstream.reshape(2 * LEN, C),
            *[conv_weight[layer, tap] for layer in range(LAYERS) for tap in range(TAPS)],
        ],
        specs=[SMEM] + [VMEM] * 17,
        scratch=[
            pltpu.VMEM((LAYERS + 2, PACKED, C), BF),
            pltpu.VMEM((PACKED, C), F32),
            pltpu.VMEM((LAYERS, PACKED, C), F32),
            pltpu.VMEM((LAYERS, PACKED, 128), F32),
            pltpu.VMEM((PACKED, C), F32),
            pltpu.VMEM((PACKED, TAPS * C), BF),
            pltpu.VMEM((TAPS * C, C), F32),
        ],
        flops=1 << 32,
        limit=16,
    )

    got = crossed(send, "core", 2, 1)
    returned = lax.all_to_all(
        slot_grad.reshape(owners, cap, C), table_axes, split_axis=0, concat_axis=0, tiled=True
    )
    slab4, slab1 = shape((4, SLAB, C), BF), shape((1, SLAB, C), BF)
    block4 = shape((4, C, C), BF)

    parts = call(core_sum_kernel, [slab4] * 4, [keep, got])
    parts = [parts[0]] + [shifted(parts[k], "y", 4, k) for k in (1, 2, 3)]
    parts = call(four_sum_kernel, [slab1] * 4, parts)
    keep_rows, send_rows = call(
        scatter_kernel,
        [block4, block4],
        [place, target, after(returned, parts[0])],
        specs=[SMEM, VMEM, VMEM],
        flops=1 << 29,
    )
    parts = [parts[0]] + [shifted(parts[k], "x", 4, k) for k in (1, 2, 3)]
    sums = [keep_rows, crossed(send_rows, "core", 2, 1)]
    parts, sums = lax.optimization_barrier((parts, sums))

    (part,) = call(four_sum_kernel, [slab1], parts)
    keep_rows, send_rows = call(row_sum_kernel, [shape((2, C, C), BF)] * 2, sums)
    parts = [part] + [crossed(part, "z", 8, k) for k in (1, 2, 3)]
    sums = [keep_rows, crossed(send_rows, "y", 4, 1)]
    parts, sums = lax.optimization_barrier((parts, sums))
    (part,) = call(four_sum_kernel, [slab1], parts)
    keep_rows, send_rows = call(row_sum_kernel, [shape((1, C, C), BF)] * 2, sums)
    parts = [part, crossed(part, "z", 8, 6)]
    sums = [keep_rows, crossed(send_rows, "y", 4, 3)]
    parts, sums = lax.optimization_barrier((parts, sums))

    part = call(last_sum_kernel, shape((C + SLAB, C), BF), parts + sums)
    parts = [part] + [shifted(part, "y", 4, -k) for k in (1, 2, 3)]
    mine, parts = call(part_kernel, [block4, slab4], parts)
    later = [shifted(parts, "x", 4, -k) for k in (1, 2, 3)]
    across = crossed(mine, "core", 2, 1)
    new_rows, next_accum = call(
        adagrad_kernel,
        [shape((rows, C), F32), shape((rows // 128, 128), F32)],
        [place, mine, across, codes, scales, accum.reshape(rows // 128, 128)],
        specs=[SMEM] + [VMEM] * 5,
        out_specs=[HBM, VMEM],
        scratch=[pltpu.VMEM((8, C, C), F32), pltpu.SemaphoreType.DMA((8,))],
    )
    later = after(later, next_accum)
    held = [parts] + later
    plan = [(at, inner, at, inner, 0) for at in range(4) for inner in range(4)]
    filled = spread(place, held, plan)
    plan = [(at, inner, at, inner, 1) for at in range(4) for inner in range(4)]
    beyond = [crossed(part, "core", 2, 1) for part in held]
    grad_conv, grad_gain = spread(place, beyond, plan, filled)
    return (
        new_rows,
        next_accum.reshape(rows),
        grad_conv.reshape(conv_weight.shape),
        grad_gain,
    )


def solution(mesh):
    fine = Mesh(mesh.devices.reshape(4, 8, 4, 2), ("x", "z", "y", "core"))
    every = ("x", "z", "y", "core")
    table = ("x", "z")
    return jax.shard_map(
        body,
        mesh=fine,
        in_specs=(
            P(every, None),
            P(every, None),
            P(every, None, None),
            P(every, None),
            P(table, None),
            P(table, None),
            P(table),
            P(),
            P(),
            P(every, None, None),
        ),
        out_specs=(P(table, None), P(table), P(), P()),
        check_vma=False,
    )
```

time: 161 us -> 134 us (0.83)
  starting transfers between devices: 76.9 us -> 59.6 us
  local copies, waits for them, and re-layouts: 18 us -> 5.04 us
  waiting for transfers between devices: 39.6 us -> 48.6 us
  other arithmetic: 4.7 us -> 1.89 us
  Pallas kernels: 19.7 us -> 17.1 us
    ppermute x18 -> x12, waiting for transfers between devices: 9.53 us -> 22.8 us  [shifted(): lax.ppermute(values, axis, [(i, (i + offset) % size) for i in range(size)])]
    unnamed x48 -> x17, local copies, waits for them, and re-layouts: 16.2 us -> 3.23 us
    ppermute x18 -> x12, starting transfers between devices: 26.3 us -> 14.9 us  [shifted(): lax.ppermute(values, axis, [(i, (i + offset) % size) for i in range(size)])]
    ppermute x14 -> x13, starting transfers between devices: 29.4 us -> 23.7 us  [crossed(): return lax.ppermute(values, axis, [(i, i ^ bits) for i in range(size)])]
    all_to_all x1, waiting for transfers between devices: 5.9 us -> 0.83 us  [body(): lax.all_to_all(slot_grad.reshape(owners, cap, C), table_axes, split_axis=...]
    pallas_call x13 -> x15, Pallas kernels: 19.7 us -> 17.1 us  [the longest x13 12.9 us: call(): pl.pallas_call(kernel, out_shape=outs, in_specs=specs, out_specs=out_spec...]
    pallas_call x1 -> x0, other arithmetic: 2.17 us -> none  [call(): pl.pallas_call(kernel, out_shape=outs, in_specs=specs, out_specs=jax.tree...]
    ppermute x14 -> x13, waiting for transfers between devices: 7.07 us -> 8.51 us  [crossed(): return lax.ppermute(values, axis, [(i, i ^ bits) for i in range(size)])]
  transfers between devices with their start and end apart: 35 -> 28, of which waited for: 13 -> 15; matrix products, arithmetic and copies ran while one was open for 2% -> 2% of each run, Pallas kernels for 5% -> 4%
where the time goes in v3:
time: 134 us; the launch traced here: 133 us
  starting transfers between devices  59.6 us (44%)
  waiting for transfers between devices  48.6 us (36%)
  Pallas kernels  17.1 us (13%)
  local copies, waits for them, and re-layouts  5.04 us (4%)
  other arithmetic  1.89 us (1%)
    ppermute x13, starting transfers between devices, crossed(): return lax.ppermute(values, axis, [(i, i ^ bits) for i in range(size)])  23.7 us
    ppermute x12, waiting for transfers between devices, shifted(): lax.ppermute(values, axis, [(i, (i + offset) % size) for i in range(size)])  22.8 us
    ppermute x12, starting transfers between devices, shifted(): lax.ppermute(values, axis, [(i, (i + offset) % size) for i in range(size)])  14.9 us
    pallas_call x13, Pallas kernels, call(): pl.pallas_call(kernel, out_shape=outs, in_specs=specs, out_specs=out_spec...  12.9 us
    all_to_all x1, starting transfers between devices, body(): lax.all_to_all(wanted, table_axes, split_axis=0, concat_axis=0, tiled=True)  11.9 us
    all_to_all x1, waiting for transfers between devices, body(): lax.all_to_all(sending, table_axes, split_axis=0, concat_axis=0, tiled=True)  10.6 us
    ppermute x13, waiting for transfers between devices, crossed(): return lax.ppermute(values, axis, [(i, i ^ bits) for i in range(size)])  8.51 us
    all_to_all x1, waiting for transfers between devices, body(): lax.all_to_all(wanted, table_axes, split_axis=0, concat_axis=0, tiled=True)  5.88 us
  transfers between devices with their start and end apart: 28, of which 15 were waited for; matrix products, arithmetic and copies ran while one was open for 2% of the time, Pallas kernels for 4%

profile of v3, /device:TPU:1, one launch (start us, length us, event | category | flops | bytes accessed | tf_op | source)
XLA Modules:
  0.0 133.3 jit_solution(2085584540489145251)
XLA Ops:
  0.6 1.4 %compare_select_fusion = s32[32,1,32]{2,1,0:T(1,128)} fusion(s32[32,1,32]{2,1,0:T(1,128)} %bitcast.61, s32[32]{0:T(128)} %bitcast.68, s32[32]{0:T(128)S(1)} %iota_multiply_fusion), kind=kLoop, calls=%fused_computation.14 | loop fusion | flops 3072 | bytes 8448 | tf_op jit(solution)/shard_map/jit(_where)/select_n | solution.py:396
  2.1 11.9 %all-to-all-start = ((s32[32,1,32]{2,1,0:T(1,128)}), s32[32,1,32]{2,1,0:T(1,128)S(1)}, u32[]{:S(2)}, u32[]{:S(2)}) async-start(s32[32,1,32]{2,1,0:T(1,128)} %compare_select_fusion), calls=%async_computation | async-start | bytes 32768 | tf_op jit(solution)/shard_map/all_to_all | solution.py:397
  13.9 1.0 copy.27.scales_ref.refs_3_
  15.0 1.2 copy-done
  16.6 5.9 %all-to-all-done = s32[32,1,32]{2,1,0:T(1,128)S(1)} async-done(((s32[32,1,32]{2,1,0:T(1,128)}), s32[32,1,32]{2,1,0:T(1,128)S(1)}, u32[]{:S(2)}, u32[]{:S(2)}) %all-to-all-start) | async-done | bytes 4128 | tf_op jit(solution)/shard_map/all_to_all | solution.py:397
  22.5 1.5 %shard_map.130 = bf16[32,32,256]{2,1,0:T(8,128)(2,1)} custom-call(s32[32,32]{1,0:T(8,128)S(1)} %bitcast.56, bf16[2048,256]{1,0:T(8,128)(2,1)S(1)} %shard_map.129.table_ref), custom_call_target="tpu_custom_call" | custom-call | flops 1073741824 | bytes 1048576 | tf_op jit(solution)/shard_map/pallas_call | solution.py:36
  24.1 4.0 %all-to-all-start.1 = ((bf16[32,32,256]{2,1,0:T(8,128)(2,1)}), bf16[32,32,256]{2,1,0:T(8,128)(2,1)S(1)}, u32[]{:S(2)}, u32[]{:S(2)}) async-start(bf16[32,32,256]{2,1,0:T(8,128)(2,1)} %shard_map.130), calls=%async_computation.1 | async-start | bytes 1048576 | tf_op jit(solution)/shard_map/all_to_all | solution.py:408
  28.6 1.5 %slice_bitcast_fusion = (bf16[256,256]{1,0:T(8,128)(2,1)S(1)}, bf16[256,256]{1,0:T(8,128)(2,1)S(1)}, bf16[256,256]{1,0:T(8,128)(2,1)S(1)}, bf16[256,256]{1,0:T(8...) fusion(bf16[4,3,256,256]{3,2,1,0:T(8,128)(2,1)} %param.17), kind=kLoop, calls=%fused_computation.2 | loop fusion | bytes 3145728 | tf_op jit(solution)/shard_map/squeeze | solution.py:427
  30.5 10.6 %all-to-all-done.1 = bf16[32,32,256]{2,1,0:T(8,128)(2,1)S(1)} async-done(((bf16[32,32,256]{2,1,0:T(8,128)(2,1)}), bf16[32,32,256]{2,1,0:T(8,128)(2,1)S(1)}, u32[]{:S(2)}, u32[]{:S(2)}) %all-to-all-start.1) | async-done | bytes 524320 | tf_op jit(solution)/shard_map/all_to_all | solution.py:408
  41.1 0.9 copy-done.3
  42.0 6.4 %shard_map.131 = (bf16[1024,256]{1,0:T(8,128)(2,1)}, bf16[16,104,256]{2,1,0:T(8,128)(2,1)S(1)}, bf16[16,104,256]{2,1,0:T(8,128)(2,1)}) custom-call(s32[4]{0:T(128)S(1)} %pad_add_fusion.place_ref, s32[1,512]{1,0:T(1,128)S(1)} %bitcast.58, s32[1,320]{1,0:T(1,128)S(1)} %reshape.129.code_ref, bf16[1024,256]{1,0:T(8,128)(2,1)S(1)} %bitcast.55, ...), custom_call_target="tpu_custom_call" | custom-call | flops 4294967296 | bytes 1048576 | tf_op jit(solution)/shard_map/pallas_call | solution.py:36
  48.4 5.2 %collective-permute-start = (bf16[16,104,256]{2,1,0:T(8,128)(2,1)}, bf16[16,104,256]{2,1,0:T(8,128)(2,1)S(1)}, u32[]{:S(2)}, u32[]{:S(2)}) collective-permute-start(bf16[16,104,256]{2,1,0:T(8,128)(2,1)} %get-tuple-element.53), channel_id=1, source_target_pairs={{0,1},{1,0},{2,3},{3,2},{4,5},{5,4},{6,7},{7,6},{8,9},{9,8},{10,11... | collective-permute-start | bytes 2555912 | tf_op jit(solution)/shard_map/ppermute | solution.py:377
  53.5 5.0 %all-to-all-start.2 = ((bf16[32,32,256]{2,1,0:T(8,128)(2,1)}), bf16[32,32,256]{2,1,0:T(8,128)(2,1)S(1)}, u32[]{:S(2)}, u32[]{:S(2)}) async-start(bf16[32,32,256]{2,1,0:T(8,128)(2,1)} %bitcast.24), calls=%async_computation.2 | async-start | bytes 1048576 | tf_op jit(solution)/shard_map/all_to_all | solution.py:444
  58.8 1.4 %collective-permute-start.1 = (bf16[4,104,256]{2,1,0:T(8,128)(2,1)S(1)}, bf16[4,104,256]{2,1,0:T(8,128)(2,1)S(1)}, u32[]{:S(2)}, u32[]{:S(2)}) collective-permute-start(bf16[4,104,256]{2,1,0:T(8,128)(2,1)S(1)} %get-tuple-element.55), channel_id=1, source_target_pairs={{0,2},{2,4},{4,6},{6,0},{1,3},{3,5},{5,7},{7,1},{8,10},{10,12},{12... | collective-permute-start | bytes 638984 | tf_op jit(solution)/shard_map/ppermute | solution.py:373
  60.2 2.6 %collective-permute-start.2 = (bf16[4,104,256]{2,1,0:T(8,128)(2,1)S(1)}, bf16[4,104,256]{2,1,0:T(8,128)(2,1)S(1)}, u32[]{:S(2)}, u32[]{:S(2)}) collective-permute-start(bf16[4,104,256]{2,1,0:T(8,128)(2,1)S(1)} %get-tuple-element.56), channel_id=1, source_target_pairs={{0,4},{2,6},{4,0},{6,2},{1,5},{3,7},{5,1},{7,3},{8,12},{10,14},{12... | collective-permute-start | bytes 638984 | tf_op jit(solution)/shard_map/ppermute | solution.py:373
  62.8 1.1 collective-permute-start.3
  63.9 2.9 %collective-permute-done.1.b_ref = bf16[4,104,256]{2,1,0:T(8,128)(2,1)S(1)} collective-permute-done((bf16[4,104,256]{2,1,0:T(8,128)(2,1)S(1)}, bf16[4,104,256]{2,1,0:T(8,128)(2,1)S(1)}, u32[]{:S(2)}, u32[]{:S(2)}) %collective-permute-start.1) | collective-permute-done | bytes 213024 | tf_op jit(solution)/shard_map/ppermute | solution.py:373
  66.8 5.7 %collective-permute-done.2.c_ref = bf16[4,104,256]{2,1,0:T(8,128)(2,1)S(1)} collective-permute-done((bf16[4,104,256]{2,1,0:T(8,128)(2,1)S(1)}, bf16[4,104,256]{2,1,0:T(8,128)(2,1)S(1)}, u32[]{:S(2)}, u32[]{:S(2)}) %collective-permute-start.2) | collective-permute-done | bytes 213024 | tf_op jit(solution)/shard_map/ppermute | solution.py:373
  72.6 0.8 all-to-all-done.2.got_ref
  73.4 1.0 shard_map.134
  74.5 2.9 %collective-permute-start.7 = (bf16[4,256,256]{2,1,0:T(8,128)(2,1)S(1)}, bf16[4,256,256]{2,1,0:T(8,128)(2,1)S(1)}, u32[]{:S(2)}, u32[]{:S(2)}) collective-permute-start(bf16[4,256,256]{2,1,0:T(8,128)(2,1)S(1)} %get-tuple-element.66), channel_id=1, source_target_pairs={{0,1},{1,0},{2,3},{3,2},{4,5},{5,4},{6,7},{7,6},{8,9},{9,8},{10,11... | collective-permute-start | bytes 1572872 | tf_op jit(solution)/shard_map/ppermute | solution.py:377
  77.7 1.8 %collective-permute-start.5 = (bf16[1,104,256]{2,1,0:T(8,128)(2,1)S(1)}, bf16[1,104,256]{2,1,0:T(8,128)(2,1)S(1)}, u32[]{:S(2)}, u32[]{:S(2)}) collective-permute-start(bf16[1,104,256]{2,1,0:T(8,128)(2,1)S(1)} %get-tuple-element.60), channel_id=1, source_target_pairs={{0,128},{64,192},{128,0},{192,64},{1,129},{65,193},{129,1},{193,65... | collective-permute-start | bytes 159752 | tf_op jit(solution)/shard_map/ppermute | solution.py:373
  79.5 1.1 collective-permute-start.6
  80.6 0.9 collective-permute-done.4.b_ref
  81.6 0.8 collective-permute-done.5.c_ref
  82.4 0.7 collective-permute-done.6.d_ref
  83.3 1.4 %collective-permute-start.11 = (bf16[2,256,256]{2,1,0:T(8,128)(2,1)S(1)}, bf16[2,256,256]{2,1,0:T(8,128)(2,1)S(1)}, u32[]{:S(2)}, u32[]{:S(2)}) collective-permute-start(bf16[2,256,256]{2,1,0:T(8,128)(2,1)S(1)} %get-tuple-element.74), channel_id=1, source_target_pairs={{0,2},{2,0},{4,6},{6,4},{1,3},{3,1},{5,7},{7,5},{8,10},{10,8},{12,... | collective-permute-start | bytes 786440 | tf_op jit(solution)/shard_map/ppermute | solution.py:377
  84.7 3.0 %collective-permute-start.10 = (bf16[1,104,256]{2,1,0:T(8,128)(2,1)S(1)}, bf16[1,104,256]{2,1,0:T(8,128)(2,1)S(1)}, u32[]{:S(2)}, u32[]{:S(2)}) collective-permute-start(bf16[1,104,256]{2,1,0:T(8,128)(2,1)S(1)} %shard_map.135.a_ref), channel_id=1, source_target_pairs={{0,24},{8,16},{16,8},{24,0},{32,56},{40,48},{48,40},{56,32},{1,25}... | collective-permute-start | bytes 159752 | tf_op jit(solution)/shard_map/ppermute | solution.py:377
  87.7 0.7 collective-permute-start.9
  88.4 1.2 collective-permute-done.10.d_ref
  89.6 2.9 %collective-permute-done.9.c_ref = bf16[1,104,256]{2,1,0:T(8,128)(2,1)S(1)} collective-permute-done((bf16[1,104,256]{2,1,0:T(8,128)(2,1)S(1)}, bf16[1,104,256]{2,1,0:T(8,128)(2,1)S(1)}, u32[]{:S(2)}, u32[]{:S(2)}) %collective-permute-start.9) | collective-permute-done | bytes 53280 | tf_op jit(solution)/shard_map/ppermute | solution.py:377
  92.6 2.0 %collective-permute-start.13 = (bf16[1,256,256]{2,1,0:T(8,128)(2,1)S(1)}, bf16[1,256,256]{2,1,0:T(8,128)(2,1)S(1)}, u32[]{:S(2)}, u32[]{:S(2)}) collective-permute-start(bf16[1,256,256]{2,1,0:T(8,128)(2,1)S(1)} %get-tuple-element.82), channel_id=1, source_target_pairs={{0,6},{2,4},{4,2},{6,0},{1,7},{3,5},{5,3},{7,1},{8,14},{10,12},{12... | collective-permute-start | bytes 393224 | tf_op jit(solution)/shard_map/ppermute | solution.py:377
  94.7 0.8 collective-permute-start.12
  95.5 4.4 %collective-permute-done.12.b_ref = bf16[1,104,256]{2,1,0:T(8,128)(2,1)S(1)} collective-permute-done((bf16[1,104,256]{2,1,0:T(8,128)(2,1)S(1)}, bf16[1,104,256]{2,1,0:T(8,128)(2,1)S(1)}, u32[]{:S(2)}, u32[]{:S(2)}) %collective-permute-start.12) | collective-permute-done | bytes 53280 | tf_op jit(solution)/shard_map/ppermute | solution.py:377
  100.4 1.6 %collective-permute-start.15 = (bf16[360,256]{1,0:T(8,128)(2,1)S(1)}, bf16[360,256]{1,0:T(8,128)(2,1)S(1)}, u32[]{:S(2)}, u32[]{:S(2)}) collective-permute-start(bf16[360,256]{1,0:T(8,128)(2,1)S(1)} %shard_map.139.refs_0_), channel_id=1, source_target_pairs={{0,4},{2,6},{4,0},{6,2},{1,5},{3,7},{5,1},{7,3},{8,12},{10,14},{12... | collective-permute-start | bytes 552968 | tf_op jit(solution)/shard_map/ppermute | solution.py:373
  101.9 0.9 collective-permute-start.14
  102.9 4.7 %collective-permute-done.16.refs_3_ = bf16[360,256]{1,0:T(8,128)(2,1)S(1)} collective-permute-done((bf16[360,256]{1,0:T(8,128)(2,1)S(1)}, bf16[360,256]{1,0:T(8,128)(2,1)S(1)}, u32[]{:S(2)}, u32[]{:S(2)}) %collective-permute-start.16) | collective-permute-done | bytes 184352 | tf_op jit(solution)/shard_map/ppermute | solution.py:373
  107.6 0.6 collective-permute-done.14.refs_1_
  108.2 5.7 %collective-permute-start.17 = (bf16[4,256,256]{2,1,0:T(8,128)(2,1)S(1)}, bf16[4,256,256]{2,1,0:T(8,128)(2,1)S(1)}, u32[]{:S(2)}, u32[]{:S(2)}) collective-permute-start(bf16[4,256,256]{2,1,0:T(8,128)(2,1)S(1)} %get-tuple-element.87.refs_0_), channel_id=1, source_target_pairs={{0,1},{1,0},{2,3},{3,2},{4,5},{5,4},{6,7},{7,6},{8,9},{9,8},{10,11... | collective-permute-start | bytes 1572872 | tf_op jit(solution)/shard_map/ppermute | solution.py:377
  113.9 1.1 collective-permute-start.21
  115.1 2.5 %collective-permute-start.20 = (bf16[4,104,256]{2,1,0:T(8,128)(2,1)S(1)}, bf16[4,104,256]{2,1,0:T(8,128)(2,1)S(1)}, u32[]{:S(2)}, u32[]{:S(2)}) collective-permute-start(bf16[4,104,256]{2,1,0:T(8,128)(2,1)S(1)} %get-tuple-element.90.refs_0_), channel_id=1, source_target_pairs={{0,128},{64,192},{128,0},{192,64},{1,129},{65,193},{129,1},{193,65... | collective-permute-start | bytes 638984 | tf_op jit(solution)/shard_map/ppermute | solution.py:373
  117.6 0.6 collective-permute-start.18
  118.2 2.9 %shard_map.141 = (f32[2048,256]{1,0:T(8,128)}, f32[16,128]{1,0:T(8,128)}) custom-call(s32[4]{0:T(128)S(1)} %pad_add_fusion.place_ref, bf16[4,256,256]{2,1,0:T(8,128)(2,1)S(1)} %get-tuple-element.87.refs_0_, bf16[4,256,256]{2,1,0:T(8,128)(2,1)S(1)} %collective-permute-done.17.refs_1_, bf16[2048,256]{1,0:T(8,128)(2,1)S(1)} %copy-done.1, ...), custom_call_target="tpu_custom_call" | custom-call | bytes 1048576 | tf_op jit(solution)/shard_map/pallas_call | solution.py:36
  121.1 0.8 collective-permute-done.21.refs_3_
  122.0 5.5 %collective-permute-done.20.refs_2_ = bf16[4,104,256]{2,1,0:T(8,128)(2,1)S(1)} collective-permute-done((bf16[4,104,256]{2,1,0:T(8,128)(2,1)S(1)}, bf16[4,104,256]{2,1,0:T(8,128)(2,1)S(1)}, u32[]{:S(2)}, u32[]{:S(2)}) %collective-permute-start.20) | collective-permute-done | bytes 213024 | tf_op jit(solution)/shard_map/ppermute | solution.py:373
  127.5 0.9 collective-permute-start.22
  128.9 1.8 %shard_map.142 = (f32[3072,256]{1,0:T(8,128)}, f32[4,256]{1,0:T(4,128)S(1)}) custom-call(s32[4]{0:T(128)S(1)} %pad_add_fusion.place_ref, bf16[4,104,256]{2,1,0:T(8,128)(2,1)S(1)} %get-tuple-element.90.refs_0_, bf16[4,104,256]{2,1,0:T(8,128)(2,1)S(1)} %collective-permute-done.19.refs_1_, bf16[4,104,256]{2,1,0:T(8,128)(2,1)S(1)} %collective-permute-done.20.refs_2_, ...), custom_call_target="tpu_custom_call" | custom-call | bytes 2097152 | tf_op jit(solution)/shard_map/pallas_call | solution.py:303
  130.7 2.4 %shard_map.143 = (f32[3072,256]{1,0:T(8,128)}, f32[4,256]{1,0:T(4,128)}) custom-call(s32[4]{0:T(128)S(1)} %pad_add_fusion.place_ref, bf16[4,104,256]{2,1,0:T(8,128)(2,1)S(1)} %collective-permute-done.18.refs_0_, bf16[4,104,256]{2,1,0:T(8,128)(2,1)S(1)} %collective-permute-done.22.refs_1_, ...), custom_call_target="tpu_custom_call", output_to_operand_aliasing={{0}: (5, {})} | custom-call | bytes 2097152 | tf_op jit(solution)/shard_map/pallas_call | solution.py:303
  (52 shorter events, 3.3 us)
Async XLA Ops:
  2.1 20.4 %all-to-all-start = ((s32[32,1,32]{2,1,0:T(1,128)}), s32[32,1,32]{2,1,0:T(1,128)S(1)}, u32[]{:S(2)}, u32[]{:S(2)}) async-start(s32[32,1,32]{2,1,0:T(1,128)} %compare_select_fusion), calls=%async_computation | async-start | bytes 32768 | tf_op jit(solution)/shard_map/all_to_all | solution.py:397
  15.0 1.2 copy-start
  22.5 5.6 %copy-start.5 = (s32[2,256]{1,0:T(2,128)S(1)}, s32[2,256]{1,0:T(2,128)}, u32[]{:S(2)}) copy-start(s32[2,256]{1,0:T(2,128)} %param.11) | copy-start | bytes 6148
  22.5 5.6 %copy-start.6 = (s32[1,2]{1,0:T(1,128)S(1)}, s32[1,2]{1,0:T(1,128)}, u32[]{:S(2)}) copy-start(s32[1,2]{1,0:T(1,128)} %param.10) | copy-start | bytes 28
  24.1 17.0 %copy-start.4 = (f32[4,256]{1,0:T(4,128)S(1)}, f32[4,256]{1,0:T(4,128)}, u32[]{:S(2)}) copy-start(f32[4,256]{1,0:T(4,128)} %gain_ref.1) | copy-start | bytes 12292
  24.1 17.0 %all-to-all-start.1 = ((bf16[32,32,256]{2,1,0:T(8,128)(2,1)}), bf16[32,32,256]{2,1,0:T(8,128)(2,1)S(1)}, u32[]{:S(2)}, u32[]{:S(2)}) async-start(bf16[32,32,256]{2,1,0:T(8,128)(2,1)} %shard_map.130), calls=%async_computation.1 | async-start | bytes 1048576 | tf_op jit(solution)/shard_map/all_to_all | solution.py:408
  41.1 1.0 copy-start.3
  48.4 10.2 %collective-permute-start = (bf16[16,104,256]{2,1,0:T(8,128)(2,1)}, bf16[16,104,256]{2,1,0:T(8,128)(2,1)S(1)}, u32[]{:S(2)}, u32[]{:S(2)}) collective-permute-start(bf16[16,104,256]{2,1,0:T(8,128)(2,1)} %get-tuple-element.53), channel_id=1, source_target_pairs={{0,1},{1,0},{2,3},{3,2},{4,5},{5,4},{6,7},{7,6},{8,9},{9,8},{10,11... | collective-permute-start | bytes 2555912 | tf_op jit(solution)/shard_map/ppermute | solution.py:377
  53.5 19.9 %all-to-all-start.2 = ((bf16[32,32,256]{2,1,0:T(8,128)(2,1)}), bf16[32,32,256]{2,1,0:T(8,128)(2,1)S(1)}, u32[]{:S(2)}, u32[]{:S(2)}) async-start(bf16[32,32,256]{2,1,0:T(8,128)(2,1)} %bitcast.24), calls=%async_computation.2 | async-start | bytes 1048576 | tf_op jit(solution)/shard_map/all_to_all | solution.py:444
  58.8 8.0 %collective-permute-start.1 = (bf16[4,104,256]{2,1,0:T(8,128)(2,1)S(1)}, bf16[4,104,256]{2,1,0:T(8,128)(2,1)S(1)}, u32[]{:S(2)}, u32[]{:S(2)}) collective-permute-start(bf16[4,104,256]{2,1,0:T(8,128)(2,1)S(1)} %get-tuple-element.55), channel_id=1, source_target_pairs={{0,2},{2,4},{4,6},{6,0},{1,3},{3,5},{5,7},{7,1},{8,10},{10,12},{12... | collective-permute-start | bytes 638984 | tf_op jit(solution)/shard_map/ppermute | solution.py:373
  60.2 12.3 %collective-permute-start.2 = (bf16[4,104,256]{2,1,0:T(8,128)(2,1)S(1)}, bf16[4,104,256]{2,1,0:T(8,128)(2,1)S(1)}, u32[]{:S(2)}, u32[]{:S(2)}) collective-permute-start(bf16[4,104,256]{2,1,0:T(8,128)(2,1)S(1)} %get-tuple-element.56), channel_id=1, source_target_pairs={{0,4},{2,6},{4,0},{6,2},{1,5},{3,7},{5,1},{7,3},{8,12},{10,14},{12... | collective-permute-start | bytes 638984 | tf_op jit(solution)/shard_map/ppermute | solution.py:373
  62.8 9.7 %collective-permute-start.3 = (bf16[4,104,256]{2,1,0:T(8,128)(2,1)S(1)}, bf16[4,104,256]{2,1,0:T(8,128)(2,1)S(1)}, u32[]{:S(2)}, u32[]{:S(2)}) collective-permute-start(bf16[4,104,256]{2,1,0:T(8,128)(2,1)S(1)} %get-tuple-element.57), channel_id=1, source_target_pairs={{0,6},{2,0},{4,2},{6,4},{1,7},{3,1},{5,3},{7,5},{8,14},{10,8},{12,... | collective-permute-start | bytes 638984 | tf_op jit(solution)/shard_map/ppermute | solution.py:373
  74.4 43.8 %copy-start.1 = (bf16[2048,256]{1,0:T(8,128)(2,1)S(1)}, bf16[2048,256]{1,0:T(8,128)(2,1)}, u32[]{:S(2)}) copy-start(bf16[2048,256]{1,0:T(8,128)(2,1)} %refs_2_.1) | copy-start | bytes 3145732
  74.5 43.8 %copy-start.2 = (f32[2048]{0:T(1024)S(1)}, f32[2048]{0:T(1024)}, u32[]{:S(2)}) copy-start(f32[2048]{0:T(1024)} %param.16) | copy-start | bytes 24580
  74.5 8.7 %collective-permute-start.7 = (bf16[4,256,256]{2,1,0:T(8,128)(2,1)S(1)}, bf16[4,256,256]{2,1,0:T(8,128)(2,1)S(1)}, u32[]{:S(2)}, u32[]{:S(2)}) collective-permute-start(bf16[4,256,256]{2,1,0:T(8,128)(2,1)S(1)} %get-tuple-element.66), channel_id=1, source_target_pairs={{0,1},{1,0},{2,3},{3,2},{4,5},{5,4},{6,7},{7,6},{8,9},{9,8},{10,11... | collective-permute-start | bytes 1572872 | tf_op jit(solution)/shard_map/ppermute | solution.py:377
  77.4 4.2 %collective-permute-start.4 = (bf16[1,104,256]{2,1,0:T(8,128)(2,1)S(1)}, bf16[1,104,256]{2,1,0:T(8,128)(2,1)S(1)}, u32[]{:S(2)}, u32[]{:S(2)}) collective-permute-start(bf16[1,104,256]{2,1,0:T(8,128)(2,1)S(1)} %get-tuple-element.59), channel_id=1, source_target_pairs={{0,64},{64,128},{128,192},{192,0},{1,65},{65,129},{129,193},{193,1... | collective-permute-start | bytes 159752 | tf_op jit(solution)/shard_map/ppermute | solution.py:373
  77.7 4.7 %collective-permute-start.5 = (bf16[1,104,256]{2,1,0:T(8,128)(2,1)S(1)}, bf16[1,104,256]{2,1,0:T(8,128)(2,1)S(1)}, u32[]{:S(2)}, u32[]{:S(2)}) collective-permute-start(bf16[1,104,256]{2,1,0:T(8,128)(2,1)S(1)} %get-tuple-element.60), channel_id=1, source_target_pairs={{0,128},{64,192},{128,0},{192,64},{1,129},{65,193},{129,1},{193,65... | collective-permute-start | bytes 159752 | tf_op jit(solution)/shard_map/ppermute | solution.py:373
  79.5 3.7 %collective-permute-start.6 = (bf16[1,104,256]{2,1,0:T(8,128)(2,1)S(1)}, bf16[1,104,256]{2,1,0:T(8,128)(2,1)S(1)}, u32[]{:S(2)}, u32[]{:S(2)}) collective-permute-start(bf16[1,104,256]{2,1,0:T(8,128)(2,1)S(1)} %get-tuple-element.61), channel_id=1, source_target_pairs={{0,192},{64,0},{128,64},{192,128},{1,193},{65,1},{129,65},{193,129... | collective-permute-start | bytes 159752 | tf_op jit(solution)/shard_map/ppermute | solution.py:373
  83.3 9.3 %collective-permute-start.11 = (bf16[2,256,256]{2,1,0:T(8,128)(2,1)S(1)}, bf16[2,256,256]{2,1,0:T(8,128)(2,1)S(1)}, u32[]{:S(2)}, u32[]{:S(2)}) collective-permute-start(bf16[2,256,256]{2,1,0:T(8,128)(2,1)S(1)} %get-tuple-element.74), channel_id=1, source_target_pairs={{0,2},{2,0},{4,6},{6,4},{1,3},{3,1},{5,7},{7,5},{8,10},{10,8},{12,... | collective-permute-start | bytes 786440 | tf_op jit(solution)/shard_map/ppermute | solution.py:377
  84.7 4.9 %collective-permute-start.10 = (bf16[1,104,256]{2,1,0:T(8,128)(2,1)S(1)}, bf16[1,104,256]{2,1,0:T(8,128)(2,1)S(1)}, u32[]{:S(2)}, u32[]{:S(2)}) collective-permute-start(bf16[1,104,256]{2,1,0:T(8,128)(2,1)S(1)} %shard_map.135.a_ref), channel_id=1, source_target_pairs={{0,24},{8,16},{16,8},{24,0},{32,56},{40,48},{48,40},{56,32},{1,25}... | collective-permute-start | bytes 159752 | tf_op jit(solution)/shard_map/ppermute | solution.py:377
  87.7 4.8 %collective-permute-start.9 = (bf16[1,104,256]{2,1,0:T(8,128)(2,1)S(1)}, bf16[1,104,256]{2,1,0:T(8,128)(2,1)S(1)}, u32[]{:S(2)}, u32[]{:S(2)}) collective-permute-start(bf16[1,104,256]{2,1,0:T(8,128)(2,1)S(1)} %shard_map.135.a_ref), channel_id=1, source_target_pairs={{0,16},{8,24},{16,0},{24,8},{32,48},{40,56},{48,32},{56,40},{1,17}... | collective-permute-start | bytes 159752 | tf_op jit(solution)/shard_map/ppermute | solution.py:377
  88.4 4.1 %collective-permute-start.8 = (bf16[1,104,256]{2,1,0:T(8,128)(2,1)S(1)}, bf16[1,104,256]{2,1,0:T(8,128)(2,1)S(1)}, u32[]{:S(2)}, u32[]{:S(2)}) collective-permute-start(bf16[1,104,256]{2,1,0:T(8,128)(2,1)S(1)} %shard_map.135.a_ref), channel_id=1, source_target_pairs={{0,8},{8,0},{16,24},{24,16},{32,40},{40,32},{48,56},{56,48},{1,9},... | collective-permute-start | bytes 159752 | tf_op jit(solution)/shard_map/ppermute | solution.py:377
  92.6 7.2 %collective-permute-start.13 = (bf16[1,256,256]{2,1,0:T(8,128)(2,1)S(1)}, bf16[1,256,256]{2,1,0:T(8,128)(2,1)S(1)}, u32[]{:S(2)}, u32[]{:S(2)}) collective-permute-start(bf16[1,256,256]{2,1,0:T(8,128)(2,1)S(1)} %get-tuple-element.82), channel_id=1, source_target_pairs={{0,6},{2,4},{4,2},{6,0},{1,7},{3,5},{5,3},{7,1},{8,14},{10,12},{12... | collective-permute-start | bytes 393224 | tf_op jit(solution)/shard_map/ppermute | solution.py:377
  94.7 5.2 %collective-permute-start.12 = (bf16[1,104,256]{2,1,0:T(8,128)(2,1)S(1)}, bf16[1,104,256]{2,1,0:T(8,128)(2,1)S(1)}, u32[]{:S(2)}, u32[]{:S(2)}) collective-permute-start(bf16[1,104,256]{2,1,0:T(8,128)(2,1)S(1)} %shard_map.137.a_ref), channel_id=1, source_target_pairs={{0,48},{8,56},{16,32},{24,40},{32,16},{40,24},{48,0},{56,8},{1,49}... | collective-permute-start | bytes 159752 | tf_op jit(solution)/shard_map/ppermute | solution.py:377
  99.9 7.7 %collective-permute-start.16 = (bf16[360,256]{1,0:T(8,128)(2,1)S(1)}, bf16[360,256]{1,0:T(8,128)(2,1)S(1)}, u32[]{:S(2)}, u32[]{:S(2)}) collective-permute-start(bf16[360,256]{1,0:T(8,128)(2,1)S(1)} %shard_map.139.refs_0_), channel_id=1, source_target_pairs={{0,2},{2,4},{4,6},{6,0},{1,3},{3,5},{5,7},{7,1},{8,10},{10,12},{12... | collective-permute-start | bytes 552968 | tf_op jit(solution)/shard_map/ppermute | solution.py:373
  100.4 7.2 %collective-permute-start.15 = (bf16[360,256]{1,0:T(8,128)(2,1)S(1)}, bf16[360,256]{1,0:T(8,128)(2,1)S(1)}, u32[]{:S(2)}, u32[]{:S(2)}) collective-permute-start(bf16[360,256]{1,0:T(8,128)(2,1)S(1)} %shard_map.139.refs_0_), channel_id=1, source_target_pairs={{0,4},{2,6},{4,0},{6,2},{1,5},{3,7},{5,1},{7,3},{8,12},{10,14},{12... | collective-permute-start | bytes 552968 | tf_op jit(solution)/shard_map/ppermute | solution.py:373
  101.9 6.2 %collective-permute-start.14 = (bf16[360,256]{1,0:T(8,128)(2,1)S(1)}, bf16[360,256]{1,0:T(8,128)(2,1)S(1)}, u32[]{:S(2)}, u32[]{:S(2)}) collective-permute-start(bf16[360,256]{1,0:T(8,128)(2,1)S(1)} %shard_map.139.refs_0_), channel_id=1, source_target_pairs={{0,6},{2,0},{4,2},{6,4},{1,7},{3,1},{5,3},{7,5},{8,14},{10,8},{12,... | collective-permute-start | bytes 552968 | tf_op jit(solution)/shard_map/ppermute | solution.py:373
  108.2 10.0 %collective-permute-start.17 = (bf16[4,256,256]{2,1,0:T(8,128)(2,1)S(1)}, bf16[4,256,256]{2,1,0:T(8,128)(2,1)S(1)}, u32[]{:S(2)}, u32[]{:S(2)}) collective-permute-start(bf16[4,256,256]{2,1,0:T(8,128)(2,1)S(1)} %get-tuple-element.87.refs_0_), channel_id=1, source_target_pairs={{0,1},{1,0},{2,3},{3,2},{4,5},{5,4},{6,7},{7,6},{8,9},{9,8},{10,11... | collective-permute-start | bytes 1572872 | tf_op jit(solution)/shard_map/ppermute | solution.py:377
  113.9 8.0 %collective-permute-start.21 = (bf16[4,104,256]{2,1,0:T(8,128)(2,1)S(1)}, bf16[4,104,256]{2,1,0:T(8,128)(2,1)S(1)}, u32[]{:S(2)}, u32[]{:S(2)}) collective-permute-start(bf16[4,104,256]{2,1,0:T(8,128)(2,1)S(1)} %get-tuple-element.90.refs_0_), channel_id=1, source_target_pairs={{0,64},{64,128},{128,192},{192,0},{1,65},{65,129},{129,193},{193,1... | collective-permute-start | bytes 638984 | tf_op jit(solution)/shard_map/ppermute | solution.py:373
  115.1 12.4 %collective-permute-start.20 = (bf16[4,104,256]{2,1,0:T(8,128)(2,1)S(1)}, bf16[4,104,256]{2,1,0:T(8,128)(2,1)S(1)}, u32[]{:S(2)}, u32[]{:S(2)}) collective-permute-start(bf16[4,104,256]{2,1,0:T(8,128)(2,1)S(1)} %get-tuple-element.90.refs_0_), channel_id=1, source_target_pairs={{0,128},{64,192},{128,0},{192,64},{1,129},{65,193},{129,1},{193,65... | collective-permute-start | bytes 638984 | tf_op jit(solution)/shard_map/ppermute | solution.py:373
  117.6 9.9 %collective-permute-start.19 = (bf16[4,104,256]{2,1,0:T(8,128)(2,1)S(1)}, bf16[4,104,256]{2,1,0:T(8,128)(2,1)S(1)}, u32[]{:S(2)}, u32[]{:S(2)}) collective-permute-start(bf16[4,104,256]{2,1,0:T(8,128)(2,1)S(1)} %get-tuple-element.90.refs_0_), channel_id=1, source_target_pairs={{0,192},{64,0},{128,64},{192,128},{1,193},{65,1},{129,65},{193,129... | collective-permute-start | bytes 638984 | tf_op jit(solution)/shard_map/ppermute | solution.py:373
  117.6 13.1 %collective-permute-start.18 = (bf16[4,104,256]{2,1,0:T(8,128)(2,1)S(1)}, bf16[4,104,256]{2,1,0:T(8,128)(2,1)S(1)}, u32[]{:S(2)}, u32[]{:S(2)}) collective-permute-start(bf16[4,104,256]{2,1,0:T(8,128)(2,1)S(1)} %get-tuple-element.90.refs_0_), channel_id=1, source_target_pairs={{0,1},{1,0},{2,3},{3,2},{4,5},{5,4},{6,7},{7,6},{8,9},{9,8},{10,11... | collective-permute-start | bytes 638984 | tf_op jit(solution)/shard_map/ppermute | solution.py:377
  127.5 3.2 %collective-permute-start.22 = (bf16[4,104,256]{2,1,0:T(8,128)(2,1)S(1)}, bf16[4,104,256]{2,1,0:T(8,128)(2,1)S(1)}, u32[]{:S(2)}, u32[]{:S(2)}) collective-permute-start(bf16[4,104,256]{2,1,0:T(8,128)(2,1)S(1)} %collective-permute-done.19.refs_1_), channel_id=1, source_target_pairs={{0,1},{1,0},{2,3},{3,2},{4,5},{5,4},{6,7},{7,6},{8,9},{9,8},{10,11... | collective-permute-start | bytes 638984 | tf_op jit(solution)/shard_map/ppermute | solution.py:377
  128.4 2.4 %collective-permute-start.23 = (bf16[4,104,256]{2,1,0:T(8,128)(2,1)S(1)}, bf16[4,104,256]{2,1,0:T(8,128)(2,1)S(1)}, u32[]{:S(2)}, u32[]{:S(2)}) collective-permute-start(bf16[4,104,256]{2,1,0:T(8,128)(2,1)S(1)} %collective-permute-done.20.refs_2_), channel_id=1, source_target_pairs={{0,1},{1,0},{2,3},{3,2},{4,5},{5,4},{6,7},{7,6},{8,9},{9,8},{10,11... | collective-permute-start | bytes 638984 | tf_op jit(solution)/shard_map/ppermute | solution.py:377
  128.4 2.4 %collective-permute-start.24 = (bf16[4,104,256]{2,1,0:T(8,128)(2,1)S(1)}, bf16[4,104,256]{2,1,0:T(8,128)(2,1)S(1)}, u32[]{:S(2)}, u32[]{:S(2)}) collective-permute-start(bf16[4,104,256]{2,1,0:T(8,128)(2,1)S(1)} %collective-permute-done.21.refs_3_), channel_id=1, source_target_pairs={{0,1},{1,0},{2,3},{3,2},{4,5},{5,4},{6,7},{7,6},{8,9},{9,8},{10,11... | collective-permute-start | bytes 638984 | tf_op jit(solution)/shard_map/ppermute | solution.py:377

commit v4 on v3

--- a/solution.py
+++ b/solution.py
@@ -256,7 +256,7 @@
 
 
 def part_kernel(*refs):
-    for at, ref in enumerate(refs[:4]):
+    for at, ref in zip((0, 1, 3, 2), refs[:4]):
         both = ref[...].astype(F32)
         refs[4][at] = both[:C].astype(BF)
         refs[5][at] = both[C:].astype(BF)
@@ -448,7 +448,7 @@
     block4 = shape((4, C, C), BF)
 
     parts = call(core_sum_kernel, [slab4] * 4, [keep, got])
-    parts = [parts[0]] + [shifted(parts[k], "y", 4, k) for k in (1, 2, 3)]
+    parts = [parts[0]] + [shifted(parts[k], "y", 4, k) for k in (2, 1, 3)]
     parts = call(four_sum_kernel, [slab1] * 4, parts)
     keep_rows, send_rows = call(
         scatter_kernel,
@@ -457,7 +457,7 @@
         specs=[SMEM, VMEM, VMEM],
         flops=1 << 29,
     )
-    parts = [parts[0]] + [shifted(parts[k], "x", 4, k) for k in (1, 2, 3)]
+    parts = [parts[0]] + [shifted(parts[k], "x", 4, k) for k in (2, 1, 3)]
     sums = [keep_rows, crossed(send_rows, "core", 2, 1)]
     parts, sums = lax.optimization_barrier((parts, sums))
 
@@ -473,9 +473,9 @@
     parts, sums = lax.optimization_barrier((parts, sums))
 
     part = call(last_sum_kernel, shape((C + SLAB, C), BF), parts + sums)
-    parts = [part] + [shifted(part, "y", 4, -k) for k in (1, 2, 3)]
+    parts = [part] + [shifted(part, "y", 4, -k) for k in (1, 3, 2)]
     mine, parts = call(part_kernel, [block4, slab4], parts)
-    later = [shifted(parts, "x", 4, -k) for k in (1, 2, 3)]
+    later = [shifted(parts, "x", 4, -k) for k in (1, 3, 2)]
     across = crossed(mine, "core", 2, 1)
     new_rows, next_accum = call(
         adagrad_kernel,
@@ -487,9 +487,10 @@
     )
     later = after(later, next_accum)
     held = [parts] + later
-    plan = [(at, inner, at, inner, 0) for at in range(4) for inner in range(4)]
+    order = (0, 1, 3, 2)
+    plan = [(at, inner, order[at], inner, 0) for at in range(4) for inner in range(4)]
     filled = spread(place, held, plan)
-    plan = [(at, inner, at, inner, 1) for at in range(4) for inner in range(4)]
+    plan = [(at, inner, order[at], inner, 1) for at in range(4) for inner in range(4)]
     beyond = [crossed(part, "core", 2, 1) for part in held]
     grad_conv, grad_gain = spread(place, beyond, plan, filled)
     return (

time: 134 us -> 133 us (level)
  waiting for transfers between devices: 48.6 us -> 46.3 us
    ppermute x12, waiting for transfers between devices: 22.8 us -> 19.4 us  [shifted(): lax.ppermute(values, axis, [(i, (i + offset) % size) for i in range(size)])]
    ppermute x12, starting transfers between devices: 14.9 us -> 17.4 us  [shifted(): lax.ppermute(values, axis, [(i, (i + offset) % size) for i in range(size)])]
  transfers between devices with their start and end apart: 28 -> 28, of which waited for: 15 -> 15; matrix products, arithmetic and copies ran while one was open for 2% -> 3% of each run, Pallas kernels for 4% -> 4%
where the time goes in v4:
time: 133 us; the launch traced here: 132 us
  starting transfers between devices  60.8 us (46%)
  waiting for transfers between devices  46.3 us (35%)
  Pallas kernels  17.1 us (13%)
  local copies, waits for them, and re-layouts  5.04 us (4%)
  other arithmetic  1.89 us (1%)
    ppermute x13, starting transfers between devices, crossed(): return lax.ppermute(values, axis, [(i, i ^ bits) for i in range(size)])  22.5 us
    ppermute x12, waiting for transfers between devices, shifted(): lax.ppermute(values, axis, [(i, (i + offset) % size) for i in range(size)])  19.4 us
    ppermute x12, starting transfers between devices, shifted(): lax.ppermute(values, axis, [(i, (i + offset) % size) for i in range(size)])  17.4 us
    pallas_call x13, Pallas kernels, call(): pl.pallas_call(kernel, out_shape=outs, in_specs=specs, out_specs=out_spec...  12.9 us
    all_to_all x1, starting transfers between devices, body(): lax.all_to_all(wanted, table_axes, split_axis=0, concat_axis=0, tiled=True)  11.9 us
    all_to_all x1, waiting for transfers between devices, body(): lax.all_to_all(sending, table_axes, split_axis=0, concat_axis=0, tiled=True)  10.6 us
    ppermute x13, waiting for transfers between devices, crossed(): return lax.ppermute(values, axis, [(i, i ^ bits) for i in range(size)])  9.28 us
    all_to_all x1, waiting for transfers between devices, body(): lax.all_to_all(wanted, table_axes, split_axis=0, concat_axis=0, tiled=True)  5.88 us
  transfers between devices with their start and end apart: 28, of which 15 were waited for; matrix products, arithmetic and copies ran while one was open for 3% of the time, Pallas kernels for 4%

profile of v4, /device:TPU:1, one launch (start us, length us, event | category | flops | bytes accessed | tf_op | source)
XLA Modules:
  0.0 132.3 jit_solution(2294266196362470291)
XLA Ops:
  0.6 1.4 %compare_select_fusion = s32[32,1,32]{2,1,0:T(1,128)} fusion(s32[32,1,32]{2,1,0:T(1,128)} %bitcast.61, s32[32]{0:T(128)} %bitcast.68, s32[32]{0:T(128)S(1)} %iota_multiply_fusion), kind=kLoop, calls=%fused_computation.14 | loop fusion | flops 3072 | bytes 8448 | tf_op jit(solution)/shard_map/jit(_where)/select_n | solution.py:396
  2.1 11.9 %all-to-all-start = ((s32[32,1,32]{2,1,0:T(1,128)}), s32[32,1,32]{2,1,0:T(1,128)S(1)}, u32[]{:S(2)}, u32[]{:S(2)}) async-start(s32[32,1,32]{2,1,0:T(1,128)} %compare_select_fusion), calls=%async_computation | async-start | bytes 32768 | tf_op jit(solution)/shard_map/all_to_all | solution.py:397
  13.9 1.0 copy.27.scales_ref.refs_3_
  15.0 1.2 copy-done
  16.2 0.4 shard_map.129.table_ref
  16.6 5.9 %all-to-all-done = s32[32,1,32]{2,1,0:T(1,128)S(1)} async-done(((s32[32,1,32]{2,1,0:T(1,128)}), s32[32,1,32]{2,1,0:T(1,128)S(1)}, u32[]{:S(2)}, u32[]{:S(2)}) %all-to-all-start) | async-done | bytes 4128 | tf_op jit(solution)/shard_map/all_to_all | solution.py:397
  22.5 1.5 %shard_map.130 = bf16[32,32,256]{2,1,0:T(8,128)(2,1)} custom-call(s32[32,32]{1,0:T(8,128)S(1)} %bitcast.56, bf16[2048,256]{1,0:T(8,128)(2,1)S(1)} %shard_map.129.table_ref), custom_call_target="tpu_custom_call" | custom-call | flops 1073741824 | bytes 1048576 | tf_op jit(solution)/shard_map/pallas_call | solution.py:36
  24.1 4.0 %all-to-all-start.1 = ((bf16[32,32,256]{2,1,0:T(8,128)(2,1)}), bf16[32,32,256]{2,1,0:T(8,128)(2,1)S(1)}, u32[]{:S(2)}, u32[]{:S(2)}) async-start(bf16[32,32,256]{2,1,0:T(8,128)(2,1)} %shard_map.130), calls=%async_computation.1 | async-start | bytes 1048576 | tf_op jit(solution)/shard_map/all_to_all | solution.py:408
  28.6 1.5 %slice_bitcast_fusion = (bf16[256,256]{1,0:T(8,128)(2,1)S(1)}, bf16[256,256]{1,0:T(8,128)(2,1)S(1)}, bf16[256,256]{1,0:T(8,128)(2,1)S(1)}, bf16[256,256]{1,0:T(8...) fusion(bf16[4,3,256,256]{3,2,1,0:T(8,128)(2,1)} %param.17), kind=kLoop, calls=%fused_computation.2 | loop fusion | bytes 3145728 | tf_op jit(solution)/shard_map/squeeze | solution.py:427
  30.5 10.6 %all-to-all-done.1 = bf16[32,32,256]{2,1,0:T(8,128)(2,1)S(1)} async-done(((bf16[32,32,256]{2,1,0:T(8,128)(2,1)}), bf16[32,32,256]{2,1,0:T(8,128)(2,1)S(1)}, u32[]{:S(2)}, u32[]{:S(2)}) %all-to-all-start.1) | async-done | bytes 524320 | tf_op jit(solution)/shard_map/all_to_all | solution.py:408
  41.1 0.9 copy-done.3
  42.0 6.4 %shard_map.131 = (bf16[1024,256]{1,0:T(8,128)(2,1)}, bf16[16,104,256]{2,1,0:T(8,128)(2,1)S(1)}, bf16[16,104,256]{2,1,0:T(8,128)(2,1)}) custom-call(s32[4]{0:T(128)S(1)} %pad_add_fusion.place_ref, s32[1,512]{1,0:T(1,128)S(1)} %bitcast.58, s32[1,320]{1,0:T(1,128)S(1)} %reshape.129.code_ref, bf16[1024,256]{1,0:T(8,128)(2,1)S(1)} %bitcast.55, ...), custom_call_target="tpu_custom_call" | custom-call | flops 4294967296 | bytes 1048576 | tf_op jit(solution)/shard_map/pallas_call | solution.py:36
  48.4 5.2 %collective-permute-start = (bf16[16,104,256]{2,1,0:T(8,128)(2,1)}, bf16[16,104,256]{2,1,0:T(8,128)(2,1)S(1)}, u32[]{:S(2)}, u32[]{:S(2)}) collective-permute-start(bf16[16,104,256]{2,1,0:T(8,128)(2,1)} %get-tuple-element.53), channel_id=1, source_target_pairs={{0,1},{1,0},{2,3},{3,2},{4,5},{5,4},{6,7},{7,6},{8,9},{9,8},{10,11... | collective-permute-start | bytes 2555912 | tf_op jit(solution)/shard_map/ppermute | solution.py:377
  53.5 5.0 %all-to-all-start.2 = ((bf16[32,32,256]{2,1,0:T(8,128)(2,1)}), bf16[32,32,256]{2,1,0:T(8,128)(2,1)S(1)}, u32[]{:S(2)}, u32[]{:S(2)}) async-start(bf16[32,32,256]{2,1,0:T(8,128)(2,1)} %bitcast.24), calls=%async_computation.2 | async-start | bytes 1048576 | tf_op jit(solution)/shard_map/all_to_all | solution.py:444
  58.8 3.0 %collective-permute-start.1 = (bf16[4,104,256]{2,1,0:T(8,128)(2,1)S(1)}, bf16[4,104,256]{2,1,0:T(8,128)(2,1)S(1)}, u32[]{:S(2)}, u32[]{:S(2)}) collective-permute-start(bf16[4,104,256]{2,1,0:T(8,128)(2,1)S(1)} %get-tuple-element.55), channel_id=1, source_target_pairs={{0,4},{2,6},{4,0},{6,2},{1,5},{3,7},{5,1},{7,3},{8,12},{10,14},{12... | collective-permute-start | bytes 638984 | tf_op jit(solution)/shard_map/ppermute | solution.py:373
  62.2 2.3 %collective-permute-start.3 = (bf16[4,104,256]{2,1,0:T(8,128)(2,1)S(1)}, bf16[4,104,256]{2,1,0:T(8,128)(2,1)S(1)}, u32[]{:S(2)}, u32[]{:S(2)}) collective-permute-start(bf16[4,104,256]{2,1,0:T(8,128)(2,1)S(1)} %get-tuple-element.57), channel_id=1, source_target_pairs={{0,6},{2,0},{4,2},{6,4},{1,7},{3,1},{5,3},{7,5},{8,14},{10,8},{12,... | collective-permute-start | bytes 638984 | tf_op jit(solution)/shard_map/ppermute | solution.py:373
  64.5 2.5 %collective-permute-done.1.b_ref = bf16[4,104,256]{2,1,0:T(8,128)(2,1)S(1)} collective-permute-done((bf16[4,104,256]{2,1,0:T(8,128)(2,1)S(1)}, bf16[4,104,256]{2,1,0:T(8,128)(2,1)S(1)}, u32[]{:S(2)}, u32[]{:S(2)}) %collective-permute-start.1) | collective-permute-done | bytes 213024 | tf_op jit(solution)/shard_map/ppermute | solution.py:373
  67.0 5.2 %collective-permute-done.2.c_ref = bf16[4,104,256]{2,1,0:T(8,128)(2,1)S(1)} collective-permute-done((bf16[4,104,256]{2,1,0:T(8,128)(2,1)S(1)}, bf16[4,104,256]{2,1,0:T(8,128)(2,1)S(1)}, u32[]{:S(2)}, u32[]{:S(2)}) %collective-permute-start.2) | collective-permute-done | bytes 213024 | tf_op jit(solution)/shard_map/ppermute | solution.py:373
  72.3 1.2 all-to-all-done.2.got_ref
  73.4 1.0 shard_map.134
  74.5 2.9 %collective-permute-start.7 = (bf16[4,256,256]{2,1,0:T(8,128)(2,1)S(1)}, bf16[4,256,256]{2,1,0:T(8,128)(2,1)S(1)}, u32[]{:S(2)}, u32[]{:S(2)}) collective-permute-start(bf16[4,256,256]{2,1,0:T(8,128)(2,1)S(1)} %get-tuple-element.66), channel_id=1, source_target_pairs={{0,1},{1,0},{2,3},{3,2},{4,5},{5,4},{6,7},{7,6},{8,9},{9,8},{10,11... | collective-permute-start | bytes 1572872 | tf_op jit(solution)/shard_map/ppermute | solution.py:377
  77.4 1.2 collective-permute-start.4
  78.9 2.4 %collective-permute-start.6 = (bf16[1,104,256]{2,1,0:T(8,128)(2,1)S(1)}, bf16[1,104,256]{2,1,0:T(8,128)(2,1)S(1)}, u32[]{:S(2)}, u32[]{:S(2)}) collective-permute-start(bf16[1,104,256]{2,1,0:T(8,128)(2,1)S(1)} %get-tuple-element.61), channel_id=1, source_target_pairs={{0,192},{64,0},{128,64},{192,128},{1,193},{65,1},{129,65},{193,129... | collective-permute-start | bytes 159752 | tf_op jit(solution)/shard_map/ppermute | solution.py:373
  81.3 1.0 collective-permute-done.4.b_ref
  82.3 1.1 collective-permute-done.5.c_ref
  83.5 1.4 %collective-permute-start.11 = (bf16[2,256,256]{2,1,0:T(8,128)(2,1)S(1)}, bf16[2,256,256]{2,1,0:T(8,128)(2,1)S(1)}, u32[]{:S(2)}, u32[]{:S(2)}) collective-permute-start(bf16[2,256,256]{2,1,0:T(8,128)(2,1)S(1)} %get-tuple-element.74), channel_id=1, source_target_pairs={{0,2},{2,0},{4,6},{6,4},{1,3},{3,1},{5,7},{7,5},{8,10},{10,8},{12,... | collective-permute-start | bytes 786440 | tf_op jit(solution)/shard_map/ppermute | solution.py:377
  84.9 3.1 %collective-permute-start.10 = (bf16[1,104,256]{2,1,0:T(8,128)(2,1)S(1)}, bf16[1,104,256]{2,1,0:T(8,128)(2,1)S(1)}, u32[]{:S(2)}, u32[]{:S(2)}) collective-permute-start(bf16[1,104,256]{2,1,0:T(8,128)(2,1)S(1)} %shard_map.135.a_ref), channel_id=1, source_target_pairs={{0,24},{8,16},{16,8},{24,0},{32,56},{40,48},{48,40},{56,32},{1,25}... | collective-permute-start | bytes 159752 | tf_op jit(solution)/shard_map/ppermute | solution.py:377
  88.0 0.6 collective-permute-start.9
  88.7 1.1 collective-permute-done.10.d_ref
  89.8 3.1 %collective-permute-done.9.c_ref = bf16[1,104,256]{2,1,0:T(8,128)(2,1)S(1)} collective-permute-done((bf16[1,104,256]{2,1,0:T(8,128)(2,1)S(1)}, bf16[1,104,256]{2,1,0:T(8,128)(2,1)S(1)}, u32[]{:S(2)}, u32[]{:S(2)}) %collective-permute-start.9) | collective-permute-done | bytes 53280 | tf_op jit(solution)/shard_map/ppermute | solution.py:377
  93.0 2.0 %collective-permute-start.13 = (bf16[1,256,256]{2,1,0:T(8,128)(2,1)S(1)}, bf16[1,256,256]{2,1,0:T(8,128)(2,1)S(1)}, u32[]{:S(2)}, u32[]{:S(2)}) collective-permute-start(bf16[1,256,256]{2,1,0:T(8,128)(2,1)S(1)} %get-tuple-element.82), channel_id=1, source_target_pairs={{0,6},{2,4},{4,2},{6,0},{1,7},{3,5},{5,3},{7,1},{8,14},{10,12},{12... | collective-permute-start | bytes 393224 | tf_op jit(solution)/shard_map/ppermute | solution.py:377
  95.3 5.0 %collective-permute-done.12.b_ref = bf16[1,104,256]{2,1,0:T(8,128)(2,1)S(1)} collective-permute-done((bf16[1,104,256]{2,1,0:T(8,128)(2,1)S(1)}, bf16[1,104,256]{2,1,0:T(8,128)(2,1)S(1)}, u32[]{:S(2)}, u32[]{:S(2)}) %collective-permute-start.12) | collective-permute-done | bytes 53280 | tf_op jit(solution)/shard_map/ppermute | solution.py:377
  100.4 0.7 collective-permute-start.16
  101.1 0.6 collective-permute-start.15
  101.7 2.1 %collective-permute-start.14 = (bf16[360,256]{1,0:T(8,128)(2,1)S(1)}, bf16[360,256]{1,0:T(8,128)(2,1)S(1)}, u32[]{:S(2)}, u32[]{:S(2)}) collective-permute-start(bf16[360,256]{1,0:T(8,128)(2,1)S(1)} %shard_map.139.refs_0_), channel_id=1, source_target_pairs={{0,6},{2,0},{4,2},{6,4},{1,7},{3,1},{5,3},{7,5},{8,14},{10,8},{12,... | collective-permute-start | bytes 552968 | tf_op jit(solution)/shard_map/ppermute | solution.py:373
  103.8 2.7 %collective-permute-done.16.refs_3_ = bf16[360,256]{1,0:T(8,128)(2,1)S(1)} collective-permute-done((bf16[360,256]{1,0:T(8,128)(2,1)S(1)}, bf16[360,256]{1,0:T(8,128)(2,1)S(1)}, u32[]{:S(2)}, u32[]{:S(2)}) %collective-permute-start.16) | collective-permute-done | bytes 184352 | tf_op jit(solution)/shard_map/ppermute | solution.py:373
  106.5 1.9 %collective-permute-done.15.refs_2_ = bf16[360,256]{1,0:T(8,128)(2,1)S(1)} collective-permute-done((bf16[360,256]{1,0:T(8,128)(2,1)S(1)}, bf16[360,256]{1,0:T(8,128)(2,1)S(1)}, u32[]{:S(2)}, u32[]{:S(2)}) %collective-permute-start.15) | collective-permute-done | bytes 184352 | tf_op jit(solution)/shard_map/ppermute | solution.py:373
  108.4 4.8 %collective-permute-start.17 = (bf16[4,256,256]{2,1,0:T(8,128)(2,1)S(1)}, bf16[4,256,256]{2,1,0:T(8,128)(2,1)S(1)}, u32[]{:S(2)}, u32[]{:S(2)}) collective-permute-start(bf16[4,256,256]{2,1,0:T(8,128)(2,1)S(1)} %get-tuple-element.87.refs_0_), channel_id=1, source_target_pairs={{0,1},{1,0},{2,3},{3,2},{4,5},{5,4},{6,7},{7,6},{8,9},{9,8},{10,11... | collective-permute-start | bytes 1572872 | tf_op jit(solution)/shard_map/ppermute | solution.py:377
  113.1 1.8 %collective-permute-start.21 = (bf16[4,104,256]{2,1,0:T(8,128)(2,1)S(1)}, bf16[4,104,256]{2,1,0:T(8,128)(2,1)S(1)}, u32[]{:S(2)}, u32[]{:S(2)}) collective-permute-start(bf16[4,104,256]{2,1,0:T(8,128)(2,1)S(1)} %get-tuple-element.90.refs_0_), channel_id=1, source_target_pairs={{0,128},{64,192},{128,0},{192,64},{1,129},{65,193},{129,1},{193,65... | collective-permute-start | bytes 638984 | tf_op jit(solution)/shard_map/ppermute | solution.py:373
  114.9 1.6 %collective-permute-start.20 = (bf16[4,104,256]{2,1,0:T(8,128)(2,1)S(1)}, bf16[4,104,256]{2,1,0:T(8,128)(2,1)S(1)}, u32[]{:S(2)}, u32[]{:S(2)}) collective-permute-start(bf16[4,104,256]{2,1,0:T(8,128)(2,1)S(1)} %get-tuple-element.90.refs_0_), channel_id=1, source_target_pairs={{0,64},{64,128},{128,192},{192,0},{1,65},{65,129},{129,193},{193,1... | collective-permute-start | bytes 638984 | tf_op jit(solution)/shard_map/ppermute | solution.py:373
  116.6 1.0 collective-permute-start.19
  117.6 0.9 collective-permute-start.18
  118.5 2.9 %shard_map.141 = (f32[2048,256]{1,0:T(8,128)}, f32[16,128]{1,0:T(8,128)}) custom-call(s32[4]{0:T(128)S(1)} %pad_add_fusion.place_ref, bf16[4,256,256]{2,1,0:T(8,128)(2,1)S(1)} %get-tuple-element.87.refs_0_, bf16[4,256,256]{2,1,0:T(8,128)(2,1)S(1)} %collective-permute-done.17.refs_1_, bf16[2048,256]{1,0:T(8,128)(2,1)S(1)} %copy-done.1, ...), custom_call_target="tpu_custom_call" | custom-call | bytes 1048576 | tf_op jit(solution)/shard_map/pallas_call | solution.py:36
  121.5 4.9 %collective-permute-done.20.refs_2_ = bf16[4,104,256]{2,1,0:T(8,128)(2,1)S(1)} collective-permute-done((bf16[4,104,256]{2,1,0:T(8,128)(2,1)S(1)}, bf16[4,104,256]{2,1,0:T(8,128)(2,1)S(1)}, u32[]{:S(2)}, u32[]{:S(2)}) %collective-permute-start.20) | collective-permute-done | bytes 213024 | tf_op jit(solution)/shard_map/ppermute | solution.py:373
  126.5 0.9 collective-permute-start.22
  127.4 0.5 collective-permute-start.24
  127.9 1.8 %shard_map.142 = (f32[3072,256]{1,0:T(8,128)}, f32[4,256]{1,0:T(4,128)S(1)}) custom-call(s32[4]{0:T(128)S(1)} %pad_add_fusion.place_ref, bf16[4,104,256]{2,1,0:T(8,128)(2,1)S(1)} %get-tuple-element.90.refs_0_, bf16[4,104,256]{2,1,0:T(8,128)(2,1)S(1)} %collective-permute-done.19.refs_1_, bf16[4,104,256]{2,1,0:T(8,128)(2,1)S(1)} %collective-permute-done.20.refs_2_, ...), custom_call_target="tpu_custom_call" | custom-call | bytes 2097152 | tf_op jit(solution)/shard_map/pallas_call | solution.py:303
  129.7 2.4 %shard_map.143 = (f32[3072,256]{1,0:T(8,128)}, f32[4,256]{1,0:T(4,128)}) custom-call(s32[4]{0:T(128)S(1)} %pad_add_fusion.place_ref, bf16[4,104,256]{2,1,0:T(8,128)(2,1)S(1)} %collective-permute-done.18.refs_0_, bf16[4,104,256]{2,1,0:T(8,128)(2,1)S(1)} %collective-permute-done.22.refs_1_, ...), custom_call_target="tpu_custom_call", output_to_operand_aliasing={{0}: (5, {})} | custom-call | bytes 2097152 | tf_op jit(solution)/shard_map/pallas_call | solution.py:303
  (52 shorter events, 2.7 us)
Async XLA Ops:
  2.1 20.4 %all-to-all-start = ((s32[32,1,32]{2,1,0:T(1,128)}), s32[32,1,32]{2,1,0:T(1,128)S(1)}, u32[]{:S(2)}, u32[]{:S(2)}) async-start(s32[32,1,32]{2,1,0:T(1,128)} %compare_select_fusion), calls=%async_computation | async-start | bytes 32768 | tf_op jit(solution)/shard_map/all_to_all | solution.py:397
  15.0 1.2 copy-start
  22.5 5.6 %copy-start.5 = (s32[2,256]{1,0:T(2,128)S(1)}, s32[2,256]{1,0:T(2,128)}, u32[]{:S(2)}) copy-start(s32[2,256]{1,0:T(2,128)} %param.11) | copy-start | bytes 6148
  22.5 5.6 %copy-start.6 = (s32[1,2]{1,0:T(1,128)S(1)}, s32[1,2]{1,0:T(1,128)}, u32[]{:S(2)}) copy-start(s32[1,2]{1,0:T(1,128)} %param.10) | copy-start | bytes 28
  24.1 17.0 %copy-start.4 = (f32[4,256]{1,0:T(4,128)S(1)}, f32[4,256]{1,0:T(4,128)}, u32[]{:S(2)}) copy-start(f32[4,256]{1,0:T(4,128)} %gain_ref.1) | copy-start | bytes 12292
  24.1 17.0 %all-to-all-start.1 = ((bf16[32,32,256]{2,1,0:T(8,128)(2,1)}), bf16[32,32,256]{2,1,0:T(8,128)(2,1)S(1)}, u32[]{:S(2)}, u32[]{:S(2)}) async-start(bf16[32,32,256]{2,1,0:T(8,128)(2,1)} %shard_map.130), calls=%async_computation.1 | async-start | bytes 1048576 | tf_op jit(solution)/shard_map/all_to_all | solution.py:408
  41.1 1.0 copy-start.3
  48.4 10.2 %collective-permute-start = (bf16[16,104,256]{2,1,0:T(8,128)(2,1)}, bf16[16,104,256]{2,1,0:T(8,128)(2,1)S(1)}, u32[]{:S(2)}, u32[]{:S(2)}) collective-permute-start(bf16[16,104,256]{2,1,0:T(8,128)(2,1)} %get-tuple-element.53), channel_id=1, source_target_pairs={{0,1},{1,0},{2,3},{3,2},{4,5},{5,4},{6,7},{7,6},{8,9},{9,8},{10,11... | collective-permute-start | bytes 2555912 | tf_op jit(solution)/shard_map/ppermute | solution.py:377
  53.5 19.9 %all-to-all-start.2 = ((bf16[32,32,256]{2,1,0:T(8,128)(2,1)}), bf16[32,32,256]{2,1,0:T(8,128)(2,1)S(1)}, u32[]{:S(2)}, u32[]{:S(2)}) async-start(bf16[32,32,256]{2,1,0:T(8,128)(2,1)} %bitcast.24), calls=%async_computation.2 | async-start | bytes 1048576 | tf_op jit(solution)/shard_map/all_to_all | solution.py:444
  58.8 8.2 %collective-permute-start.1 = (bf16[4,104,256]{2,1,0:T(8,128)(2,1)S(1)}, bf16[4,104,256]{2,1,0:T(8,128)(2,1)S(1)}, u32[]{:S(2)}, u32[]{:S(2)}) collective-permute-start(bf16[4,104,256]{2,1,0:T(8,128)(2,1)S(1)} %get-tuple-element.55), channel_id=1, source_target_pairs={{0,4},{2,6},{4,0},{6,2},{1,5},{3,7},{5,1},{7,3},{8,12},{10,14},{12... | collective-permute-start | bytes 638984 | tf_op jit(solution)/shard_map/ppermute | solution.py:373
  61.8 10.3 %collective-permute-start.2 = (bf16[4,104,256]{2,1,0:T(8,128)(2,1)S(1)}, bf16[4,104,256]{2,1,0:T(8,128)(2,1)S(1)}, u32[]{:S(2)}, u32[]{:S(2)}) collective-permute-start(bf16[4,104,256]{2,1,0:T(8,128)(2,1)S(1)} %get-tuple-element.56), channel_id=1, source_target_pairs={{0,2},{2,4},{4,6},{6,0},{1,3},{3,5},{5,7},{7,1},{8,10},{10,12},{12... | collective-permute-start | bytes 638984 | tf_op jit(solution)/shard_map/ppermute | solution.py:373
  62.2 9.9 %collective-permute-start.3 = (bf16[4,104,256]{2,1,0:T(8,128)(2,1)S(1)}, bf16[4,104,256]{2,1,0:T(8,128)(2,1)S(1)}, u32[]{:S(2)}, u32[]{:S(2)}) collective-permute-start(bf16[4,104,256]{2,1,0:T(8,128)(2,1)S(1)} %get-tuple-element.57), channel_id=1, source_target_pairs={{0,6},{2,0},{4,2},{6,4},{1,7},{3,1},{5,3},{7,5},{8,14},{10,8},{12,... | collective-permute-start | bytes 638984 | tf_op jit(solution)/shard_map/ppermute | solution.py:373
  74.4 44.1 %copy-start.1 = (bf16[2048,256]{1,0:T(8,128)(2,1)S(1)}, bf16[2048,256]{1,0:T(8,128)(2,1)}, u32[]{:S(2)}) copy-start(bf16[2048,256]{1,0:T(8,128)(2,1)} %refs_2_.1) | copy-start | bytes 3145732
  74.5 44.1 %copy-start.2 = (f32[2048]{0:T(1024)S(1)}, f32[2048]{0:T(1024)}, u32[]{:S(2)}) copy-start(f32[2048]{0:T(1024)} %param.16) | copy-start | bytes 24580
  74.5 8.9 %collective-permute-start.7 = (bf16[4,256,256]{2,1,0:T(8,128)(2,1)S(1)}, bf16[4,256,256]{2,1,0:T(8,128)(2,1)S(1)}, u32[]{:S(2)}, u32[]{:S(2)}) collective-permute-start(bf16[4,256,256]{2,1,0:T(8,128)(2,1)S(1)} %get-tuple-element.66), channel_id=1, source_target_pairs={{0,1},{1,0},{2,3},{3,2},{4,5},{5,4},{6,7},{7,6},{8,9},{9,8},{10,11... | collective-permute-start | bytes 1572872 | tf_op jit(solution)/shard_map/ppermute | solution.py:377
  77.4 4.9 %collective-permute-start.4 = (bf16[1,104,256]{2,1,0:T(8,128)(2,1)S(1)}, bf16[1,104,256]{2,1,0:T(8,128)(2,1)S(1)}, u32[]{:S(2)}, u32[]{:S(2)}) collective-permute-start(bf16[1,104,256]{2,1,0:T(8,128)(2,1)S(1)} %get-tuple-element.59), channel_id=1, source_target_pairs={{0,128},{64,192},{128,0},{192,64},{1,129},{65,193},{129,1},{193,65... | collective-permute-start | bytes 159752 | tf_op jit(solution)/shard_map/ppermute | solution.py:373
  78.6 4.8 %collective-permute-start.5 = (bf16[1,104,256]{2,1,0:T(8,128)(2,1)S(1)}, bf16[1,104,256]{2,1,0:T(8,128)(2,1)S(1)}, u32[]{:S(2)}, u32[]{:S(2)}) collective-permute-start(bf16[1,104,256]{2,1,0:T(8,128)(2,1)S(1)} %get-tuple-element.60), channel_id=1, source_target_pairs={{0,64},{64,128},{128,192},{192,0},{1,65},{65,129},{129,193},{193,1... | collective-permute-start | bytes 159752 | tf_op jit(solution)/shard_map/ppermute | solution.py:373
  78.9 4.5 %collective-permute-start.6 = (bf16[1,104,256]{2,1,0:T(8,128)(2,1)S(1)}, bf16[1,104,256]{2,1,0:T(8,128)(2,1)S(1)}, u32[]{:S(2)}, u32[]{:S(2)}) collective-permute-start(bf16[1,104,256]{2,1,0:T(8,128)(2,1)S(1)} %get-tuple-element.61), channel_id=1, source_target_pairs={{0,192},{64,0},{128,64},{192,128},{1,193},{65,1},{129,65},{193,129... | collective-permute-start | bytes 159752 | tf_op jit(solution)/shard_map/ppermute | solution.py:373
  83.5 9.4 %collective-permute-start.11 = (bf16[2,256,256]{2,1,0:T(8,128)(2,1)S(1)}, bf16[2,256,256]{2,1,0:T(8,128)(2,1)S(1)}, u32[]{:S(2)}, u32[]{:S(2)}) collective-permute-start(bf16[2,256,256]{2,1,0:T(8,128)(2,1)S(1)} %get-tuple-element.74), channel_id=1, source_target_pairs={{0,2},{2,0},{4,6},{6,4},{1,3},{3,1},{5,7},{7,5},{8,10},{10,8},{12,... | collective-permute-start | bytes 786440 | tf_op jit(solution)/shard_map/ppermute | solution.py:377
  84.9 4.9 %collective-permute-start.10 = (bf16[1,104,256]{2,1,0:T(8,128)(2,1)S(1)}, bf16[1,104,256]{2,1,0:T(8,128)(2,1)S(1)}, u32[]{:S(2)}, u32[]{:S(2)}) collective-permute-start(bf16[1,104,256]{2,1,0:T(8,128)(2,1)S(1)} %shard_map.135.a_ref), channel_id=1, source_target_pairs={{0,24},{8,16},{16,8},{24,0},{32,56},{40,48},{48,40},{56,32},{1,25}... | collective-permute-start | bytes 159752 | tf_op jit(solution)/shard_map/ppermute | solution.py:377
  88.0 4.9 %collective-permute-start.9 = (bf16[1,104,256]{2,1,0:T(8,128)(2,1)S(1)}, bf16[1,104,256]{2,1,0:T(8,128)(2,1)S(1)}, u32[]{:S(2)}, u32[]{:S(2)}) collective-permute-start(bf16[1,104,256]{2,1,0:T(8,128)(2,1)S(1)} %shard_map.135.a_ref), channel_id=1, source_target_pairs={{0,16},{8,24},{16,0},{24,8},{32,48},{40,56},{48,32},{56,40},{1,17}... | collective-permute-start | bytes 159752 | tf_op jit(solution)/shard_map/ppermute | solution.py:377
  88.7 4.3 %collective-permute-start.8 = (bf16[1,104,256]{2,1,0:T(8,128)(2,1)S(1)}, bf16[1,104,256]{2,1,0:T(8,128)(2,1)S(1)}, u32[]{:S(2)}, u32[]{:S(2)}) collective-permute-start(bf16[1,104,256]{2,1,0:T(8,128)(2,1)S(1)} %shard_map.135.a_ref), channel_id=1, source_target_pairs={{0,8},{8,0},{16,24},{24,16},{32,40},{40,32},{48,56},{56,48},{1,9},... | collective-permute-start | bytes 159752 | tf_op jit(solution)/shard_map/ppermute | solution.py:377
  93.0 7.3 %collective-permute-start.13 = (bf16[1,256,256]{2,1,0:T(8,128)(2,1)S(1)}, bf16[1,256,256]{2,1,0:T(8,128)(2,1)S(1)}, u32[]{:S(2)}, u32[]{:S(2)}) collective-permute-start(bf16[1,256,256]{2,1,0:T(8,128)(2,1)S(1)} %get-tuple-element.82), channel_id=1, source_target_pairs={{0,6},{2,4},{4,2},{6,0},{1,7},{3,5},{5,3},{7,1},{8,14},{10,12},{12... | collective-permute-start | bytes 393224 | tf_op jit(solution)/shard_map/ppermute | solution.py:377
  95.0 5.3 %collective-permute-start.12 = (bf16[1,104,256]{2,1,0:T(8,128)(2,1)S(1)}, bf16[1,104,256]{2,1,0:T(8,128)(2,1)S(1)}, u32[]{:S(2)}, u32[]{:S(2)}) collective-permute-start(bf16[1,104,256]{2,1,0:T(8,128)(2,1)S(1)} %shard_map.137.a_ref), channel_id=1, source_target_pairs={{0,48},{8,56},{16,32},{24,40},{32,16},{40,24},{48,0},{56,8},{1,49}... | collective-permute-start | bytes 159752 | tf_op jit(solution)/shard_map/ppermute | solution.py:377
  100.4 6.1 %collective-permute-start.16 = (bf16[360,256]{1,0:T(8,128)(2,1)S(1)}, bf16[360,256]{1,0:T(8,128)(2,1)S(1)}, u32[]{:S(2)}, u32[]{:S(2)}) collective-permute-start(bf16[360,256]{1,0:T(8,128)(2,1)S(1)} %shard_map.139.refs_0_), channel_id=1, source_target_pairs={{0,4},{2,6},{4,0},{6,2},{1,5},{3,7},{5,1},{7,3},{8,12},{10,14},{12... | collective-permute-start | bytes 552968 | tf_op jit(solution)/shard_map/ppermute | solution.py:373
  101.1 7.2 %collective-permute-start.15 = (bf16[360,256]{1,0:T(8,128)(2,1)S(1)}, bf16[360,256]{1,0:T(8,128)(2,1)S(1)}, u32[]{:S(2)}, u32[]{:S(2)}) collective-permute-start(bf16[360,256]{1,0:T(8,128)(2,1)S(1)} %shard_map.139.refs_0_), channel_id=1, source_target_pairs={{0,2},{2,4},{4,6},{6,0},{1,3},{3,5},{5,7},{7,1},{8,10},{10,12},{12... | collective-permute-start | bytes 552968 | tf_op jit(solution)/shard_map/ppermute | solution.py:373
  101.7 6.6 %collective-permute-start.14 = (bf16[360,256]{1,0:T(8,128)(2,1)S(1)}, bf16[360,256]{1,0:T(8,128)(2,1)S(1)}, u32[]{:S(2)}, u32[]{:S(2)}) collective-permute-start(bf16[360,256]{1,0:T(8,128)(2,1)S(1)} %shard_map.139.refs_0_), channel_id=1, source_target_pairs={{0,6},{2,0},{4,2},{6,4},{1,7},{3,1},{5,3},{7,5},{8,14},{10,8},{12,... | collective-permute-start | bytes 552968 | tf_op jit(solution)/shard_map/ppermute | solution.py:373
  108.4 10.1 %collective-permute-start.17 = (bf16[4,256,256]{2,1,0:T(8,128)(2,1)S(1)}, bf16[4,256,256]{2,1,0:T(8,128)(2,1)S(1)}, u32[]{:S(2)}, u32[]{:S(2)}) collective-permute-start(bf16[4,256,256]{2,1,0:T(8,128)(2,1)S(1)} %get-tuple-element.87.refs_0_), channel_id=1, source_target_pairs={{0,1},{1,0},{2,3},{3,2},{4,5},{5,4},{6,7},{7,6},{8,9},{9,8},{10,11... | collective-permute-start | bytes 1572872 | tf_op jit(solution)/shard_map/ppermute | solution.py:377
  113.1 8.4 %collective-permute-start.21 = (bf16[4,104,256]{2,1,0:T(8,128)(2,1)S(1)}, bf16[4,104,256]{2,1,0:T(8,128)(2,1)S(1)}, u32[]{:S(2)}, u32[]{:S(2)}) collective-permute-start(bf16[4,104,256]{2,1,0:T(8,128)(2,1)S(1)} %get-tuple-element.90.refs_0_), channel_id=1, source_target_pairs={{0,128},{64,192},{128,0},{192,64},{1,129},{65,193},{129,1},{193,65... | collective-permute-start | bytes 638984 | tf_op jit(solution)/shard_map/ppermute | solution.py:373
  114.9 11.5 %collective-permute-start.20 = (bf16[4,104,256]{2,1,0:T(8,128)(2,1)S(1)}, bf16[4,104,256]{2,1,0:T(8,128)(2,1)S(1)}, u32[]{:S(2)}, u32[]{:S(2)}) collective-permute-start(bf16[4,104,256]{2,1,0:T(8,128)(2,1)S(1)} %get-tuple-element.90.refs_0_), channel_id=1, source_target_pairs={{0,64},{64,128},{128,192},{192,0},{1,65},{65,129},{129,193},{193,1... | collective-permute-start | bytes 638984 | tf_op jit(solution)/shard_map/ppermute | solution.py:373
  116.6 9.9 %collective-permute-start.19 = (bf16[4,104,256]{2,1,0:T(8,128)(2,1)S(1)}, bf16[4,104,256]{2,1,0:T(8,128)(2,1)S(1)}, u32[]{:S(2)}, u32[]{:S(2)}) collective-permute-start(bf16[4,104,256]{2,1,0:T(8,128)(2,1)S(1)} %get-tuple-element.90.refs_0_), channel_id=1, source_target_pairs={{0,192},{64,0},{128,64},{192,128},{1,193},{65,1},{129,65},{193,129... | collective-permute-start | bytes 638984 | tf_op jit(solution)/shard_map/ppermute | solution.py:373
  117.6 12.1 %collective-permute-start.18 = (bf16[4,104,256]{2,1,0:T(8,128)(2,1)S(1)}, bf16[4,104,256]{2,1,0:T(8,128)(2,1)S(1)}, u32[]{:S(2)}, u32[]{:S(2)}) collective-permute-start(bf16[4,104,256]{2,1,0:T(8,128)(2,1)S(1)} %get-tuple-element.90.refs_0_), channel_id=1, source_target_pairs={{0,1},{1,0},{2,3},{3,2},{4,5},{5,4},{6,7},{7,6},{8,9},{9,8},{10,11... | collective-permute-start | bytes 638984 | tf_op jit(solution)/shard_map/ppermute | solution.py:377
  126.5 3.2 %collective-permute-start.22 = (bf16[4,104,256]{2,1,0:T(8,128)(2,1)S(1)}, bf16[4,104,256]{2,1,0:T(8,128)(2,1)S(1)}, u32[]{:S(2)}, u32[]{:S(2)}) collective-permute-start(bf16[4,104,256]{2,1,0:T(8,128)(2,1)S(1)} %collective-permute-done.19.refs_1_), channel_id=1, source_target_pairs={{0,1},{1,0},{2,3},{3,2},{4,5},{5,4},{6,7},{7,6},{8,9},{9,8},{10,11... | collective-permute-start | bytes 638984 | tf_op jit(solution)/shard_map/ppermute | solution.py:377
  127.4 2.4 %collective-permute-start.23 = (bf16[4,104,256]{2,1,0:T(8,128)(2,1)S(1)}, bf16[4,104,256]{2,1,0:T(8,128)(2,1)S(1)}, u32[]{:S(2)}, u32[]{:S(2)}) collective-permute-start(bf16[4,104,256]{2,1,0:T(8,128)(2,1)S(1)} %collective-permute-done.20.refs_2_), channel_id=1, source_target_pairs={{0,1},{1,0},{2,3},{3,2},{4,5},{5,4},{6,7},{7,6},{8,9},{9,8},{10,11... | collective-permute-start | bytes 638984 | tf_op jit(solution)/shard_map/ppermute | solution.py:377
  127.4 2.4 %collective-permute-start.24 = (bf16[4,104,256]{2,1,0:T(8,128)(2,1)S(1)}, bf16[4,104,256]{2,1,0:T(8,128)(2,1)S(1)}, u32[]{:S(2)}, u32[]{:S(2)}) collective-permute-start(bf16[4,104,256]{2,1,0:T(8,128)(2,1)S(1)} %collective-permute-done.21.refs_3_), channel_id=1, source_target_pairs={{0,1},{1,0},{2,3},{3,2},{4,5},{5,4},{6,7},{7,6},{8,9},{9,8},{10,11... | collective-permute-start | bytes 638984 | tf_op jit(solution)/shard_map/ppermute | solution.py:377

commit v5 on v4

--- a/solution.py
+++ b/solution.py
@@ -485,13 +485,14 @@
         out_specs=[HBM, VMEM],
         scratch=[pltpu.VMEM((8, C, C), F32), pltpu.SemaphoreType.DMA((8,))],
     )
-    later = after(later, next_accum)
-    held = [parts] + later
-    order = (0, 1, 3, 2)
-    plan = [(at, inner, order[at], inner, 0) for at in range(4) for inner in range(4)]
-    filled = spread(place, held, plan)
-    plan = [(at, inner, order[at], inner, 1) for at in range(4) for inner in range(4)]
-    beyond = [crossed(part, "core", 2, 1) for part in held]
+    plan = [(at, inner, 0, inner, at) for at in range(2) for inner in range(4)]
+    filled = spread(place, [parts, crossed(parts, "core", 2, 1)], plan)
+    later = after(later, next_accum, filled)
+    order = (1, 3, 2)
+    plan = [(at, inner, order[at], inner, 0) for at in range(3) for inner in range(4)]
+    beyond = [crossed(part, "core", 2, 1) for part in later]
+    filled = spread(place, later, plan, filled)
+    plan = [(at, inner, order[at], inner, 1) for at in range(3) for inner in range(4)]
     grad_conv, grad_gain = spread(place, beyond, plan, filled)
     return (
         new_rows,

time: 133 us -> 133 us (level)
    pallas_call x2 -> x3, Pallas kernels: 4.23 us -> 5.39 us  [spread(): pl.pallas_call(functools.partial(spread_kernel, count, plan, before is No...]
  transfers between devices with their start and end apart: 28 -> 28, of which waited for: 15 -> 13; matrix products, arithmetic and copies ran while one was open for 3% -> 3% of each run, Pallas kernels for 4% -> 5%
where the time goes in v5:
time: 133 us; the launch traced here: 132 us
  starting transfers between devices  60.4 us (45%)
  waiting for transfers between devices  45.3 us (34%)
  Pallas kernels  18.2 us (14%)
  local copies, waits for them, and re-layouts  5.04 us (4%)
  other arithmetic  1.89 us (1%)
    ppermute x13, starting transfers between devices, crossed(): return lax.ppermute(values, axis, [(i, i ^ bits) for i in range(size)])  22.1 us
    ppermute x12, waiting for transfers between devices, shifted(): lax.ppermute(values, axis, [(i, (i + offset) % size) for i in range(size)])  18.4 us
    ppermute x12, starting transfers between devices, shifted(): lax.ppermute(values, axis, [(i, (i + offset) % size) for i in range(size)])  17.4 us
    pallas_call x13, Pallas kernels, call(): pl.pallas_call(kernel, out_shape=outs, in_specs=specs, out_specs=out_spec...  12.8 us
    all_to_all x1, starting transfers between devices, body(): lax.all_to_all(wanted, table_axes, split_axis=0, concat_axis=0, tiled=True)  11.9 us
    all_to_all x1, waiting for transfers between devices, body(): lax.all_to_all(sending, table_axes, split_axis=0, concat_axis=0, tiled=True)  10.6 us
    ppermute x13, waiting for transfers between devices, crossed(): return lax.ppermute(values, axis, [(i, i ^ bits) for i in range(size)])  9.28 us
    all_to_all x1, waiting for transfers between devices, body(): lax.all_to_all(wanted, table_axes, split_axis=0, concat_axis=0, tiled=True)  5.86 us
  transfers between devices with their start and end apart: 28, of which 13 were waited for; matrix products, arithmetic and copies ran while one was open for 3% of the time, Pallas kernels for 5%

profile of v5, /device:TPU:1, one launch (start us, length us, event | category | flops | bytes accessed | tf_op | source)
XLA Modules:
  0.0 132.0 jit_solution(14329470020999381695)
XLA Ops:
  0.6 1.4 %compare_select_fusion = s32[32,1,32]{2,1,0:T(1,128)} fusion(s32[32,1,32]{2,1,0:T(1,128)} %bitcast.61, s32[32]{0:T(128)} %bitcast.68, s32[32]{0:T(128)S(1)} %iota_multiply_fusion), kind=kLoop, calls=%fused_computation.14 | loop fusion | flops 3072 | bytes 8448 | tf_op jit(solution)/shard_map/jit(_where)/select_n | solution.py:396
  2.1 11.9 %all-to-all-start = ((s32[32,1,32]{2,1,0:T(1,128)}), s32[32,1,32]{2,1,0:T(1,128)S(1)}, u32[]{:S(2)}, u32[]{:S(2)}) async-start(s32[32,1,32]{2,1,0:T(1,128)} %compare_select_fusion), calls=%async_computation | async-start | bytes 32768 | tf_op jit(solution)/shard_map/all_to_all | solution.py:397
  13.9 1.0 copy.28.scales_ref.refs_3_
  15.0 1.2 copy-done
  16.2 0.4 shard_map.129.table_ref
  16.6 5.9 %all-to-all-done = s32[32,1,32]{2,1,0:T(1,128)S(1)} async-done(((s32[32,1,32]{2,1,0:T(1,128)}), s32[32,1,32]{2,1,0:T(1,128)S(1)}, u32[]{:S(2)}, u32[]{:S(2)}) %all-to-all-start) | async-done | bytes 4128 | tf_op jit(solution)/shard_map/all_to_all | solution.py:397
  22.5 1.6 %shard_map.130 = bf16[32,32,256]{2,1,0:T(8,128)(2,1)} custom-call(s32[32,32]{1,0:T(8,128)S(1)} %bitcast.56, bf16[2048,256]{1,0:T(8,128)(2,1)S(1)} %shard_map.129.table_ref), custom_call_target="tpu_custom_call" | custom-call | flops 1073741824 | bytes 1048576 | tf_op jit(solution)/shard_map/pallas_call | solution.py:36
  24.1 4.0 %all-to-all-start.1 = ((bf16[32,32,256]{2,1,0:T(8,128)(2,1)}), bf16[32,32,256]{2,1,0:T(8,128)(2,1)S(1)}, u32[]{:S(2)}, u32[]{:S(2)}) async-start(bf16[32,32,256]{2,1,0:T(8,128)(2,1)} %shard_map.130), calls=%async_computation.1 | async-start | bytes 1048576 | tf_op jit(solution)/shard_map/all_to_all | solution.py:408
  28.6 1.5 %slice_bitcast_fusion = (bf16[256,256]{1,0:T(8,128)(2,1)S(1)}, bf16[256,256]{1,0:T(8,128)(2,1)S(1)}, bf16[256,256]{1,0:T(8,128)(2,1)S(1)}, bf16[256,256]{1,0:T(8...) fusion(bf16[4,3,256,256]{3,2,1,0:T(8,128)(2,1)} %param.17), kind=kLoop, calls=%fused_computation.2 | loop fusion | bytes 3145728 | tf_op jit(solution)/shard_map/squeeze | solution.py:427
  30.5 10.6 %all-to-all-done.1 = bf16[32,32,256]{2,1,0:T(8,128)(2,1)S(1)} async-done(((bf16[32,32,256]{2,1,0:T(8,128)(2,1)}), bf16[32,32,256]{2,1,0:T(8,128)(2,1)S(1)}, u32[]{:S(2)}, u32[]{:S(2)}) %all-to-all-start.1) | async-done | bytes 524320 | tf_op jit(solution)/shard_map/all_to_all | solution.py:408
  41.1 0.9 copy-done.3
  42.0 6.3 %shard_map.131 = (bf16[1024,256]{1,0:T(8,128)(2,1)}, bf16[16,104,256]{2,1,0:T(8,128)(2,1)S(1)}, bf16[16,104,256]{2,1,0:T(8,128)(2,1)}) custom-call(s32[4]{0:T(128)S(1)} %pad_add_fusion.place_ref, s32[1,512]{1,0:T(1,128)S(1)} %bitcast.58, s32[1,320]{1,0:T(1,128)S(1)} %reshape.129.code_ref, bf16[1024,256]{1,0:T(8,128)(2,1)S(1)} %bitcast.55, ...), custom_call_target="tpu_custom_call" | custom-call | flops 4294967296 | bytes 1048576 | tf_op jit(solution)/shard_map/pallas_call | solution.py:36
  48.3 5.2 %collective-permute-start = (bf16[16,104,256]{2,1,0:T(8,128)(2,1)}, bf16[16,104,256]{2,1,0:T(8,128)(2,1)S(1)}, u32[]{:S(2)}, u32[]{:S(2)}) collective-permute-start(bf16[16,104,256]{2,1,0:T(8,128)(2,1)} %get-tuple-element.55), channel_id=1, source_target_pairs={{0,1},{1,0},{2,3},{3,2},{4,5},{5,4},{6,7},{7,6},{8,9},{9,8},{10,11... | collective-permute-start | bytes 2555912 | tf_op jit(solution)/shard_map/ppermute | solution.py:377
  53.5 5.0 %all-to-all-start.2 = ((bf16[32,32,256]{2,1,0:T(8,128)(2,1)}), bf16[32,32,256]{2,1,0:T(8,128)(2,1)S(1)}, u32[]{:S(2)}, u32[]{:S(2)}) async-start(bf16[32,32,256]{2,1,0:T(8,128)(2,1)} %bitcast.24), calls=%async_computation.2 | async-start | bytes 1048576 | tf_op jit(solution)/shard_map/all_to_all | solution.py:444
  58.7 3.0 %collective-permute-start.1 = (bf16[4,104,256]{2,1,0:T(8,128)(2,1)S(1)}, bf16[4,104,256]{2,1,0:T(8,128)(2,1)S(1)}, u32[]{:S(2)}, u32[]{:S(2)}) collective-permute-start(bf16[4,104,256]{2,1,0:T(8,128)(2,1)S(1)} %get-tuple-element.57), channel_id=1, source_target_pairs={{0,4},{2,6},{4,0},{6,2},{1,5},{3,7},{5,1},{7,3},{8,12},{10,14},{12... | collective-permute-start | bytes 638984 | tf_op jit(solution)/shard_map/ppermute | solution.py:373
  62.1 2.3 %collective-permute-start.3 = (bf16[4,104,256]{2,1,0:T(8,128)(2,1)S(1)}, bf16[4,104,256]{2,1,0:T(8,128)(2,1)S(1)}, u32[]{:S(2)}, u32[]{:S(2)}) collective-permute-start(bf16[4,104,256]{2,1,0:T(8,128)(2,1)S(1)} %get-tuple-element.59), channel_id=1, source_target_pairs={{0,6},{2,0},{4,2},{6,4},{1,7},{3,1},{5,3},{7,5},{8,14},{10,8},{12,... | collective-permute-start | bytes 638984 | tf_op jit(solution)/shard_map/ppermute | solution.py:373
  64.4 2.5 %collective-permute-done.1.b_ref = bf16[4,104,256]{2,1,0:T(8,128)(2,1)S(1)} collective-permute-done((bf16[4,104,256]{2,1,0:T(8,128)(2,1)S(1)}, bf16[4,104,256]{2,1,0:T(8,128)(2,1)S(1)}, u32[]{:S(2)}, u32[]{:S(2)}) %collective-permute-start.1) | collective-permute-done | bytes 213024 | tf_op jit(solution)/shard_map/ppermute | solution.py:373
  66.9 5.2 %collective-permute-done.2.c_ref = bf16[4,104,256]{2,1,0:T(8,128)(2,1)S(1)} collective-permute-done((bf16[4,104,256]{2,1,0:T(8,128)(2,1)S(1)}, bf16[4,104,256]{2,1,0:T(8,128)(2,1)S(1)}, u32[]{:S(2)}, u32[]{:S(2)}) %collective-permute-start.2) | collective-permute-done | bytes 213024 | tf_op jit(solution)/shard_map/ppermute | solution.py:373
  72.2 1.2 all-to-all-done.2.got_ref
  73.4 1.0 shard_map.134
  74.4 2.9 %collective-permute-start.7 = (bf16[4,256,256]{2,1,0:T(8,128)(2,1)S(1)}, bf16[4,256,256]{2,1,0:T(8,128)(2,1)S(1)}, u32[]{:S(2)}, u32[]{:S(2)}) collective-permute-start(bf16[4,256,256]{2,1,0:T(8,128)(2,1)S(1)} %get-tuple-element.68), channel_id=1, source_target_pairs={{0,1},{1,0},{2,3},{3,2},{4,5},{5,4},{6,7},{7,6},{8,9},{9,8},{10,11... | collective-permute-start | bytes 1572872 | tf_op jit(solution)/shard_map/ppermute | solution.py:377
  77.3 1.2 collective-permute-start.4
  78.8 2.4 %collective-permute-start.6 = (bf16[1,104,256]{2,1,0:T(8,128)(2,1)S(1)}, bf16[1,104,256]{2,1,0:T(8,128)(2,1)S(1)}, u32[]{:S(2)}, u32[]{:S(2)}) collective-permute-start(bf16[1,104,256]{2,1,0:T(8,128)(2,1)S(1)} %get-tuple-element.63), channel_id=1, source_target_pairs={{0,192},{64,0},{128,64},{192,128},{1,193},{65,1},{129,65},{193,129... | collective-permute-start | bytes 159752 | tf_op jit(solution)/shard_map/ppermute | solution.py:373
  81.2 1.0 collective-permute-done.4.b_ref
  82.2 0.8 collective-permute-done.5.c_ref
  83.1 1.4 %collective-permute-start.11 = (bf16[2,256,256]{2,1,0:T(8,128)(2,1)S(1)}, bf16[2,256,256]{2,1,0:T(8,128)(2,1)S(1)}, u32[]{:S(2)}, u32[]{:S(2)}) collective-permute-start(bf16[2,256,256]{2,1,0:T(8,128)(2,1)S(1)} %get-tuple-element.76), channel_id=1, source_target_pairs={{0,2},{2,0},{4,6},{6,4},{1,3},{3,1},{5,7},{7,5},{8,10},{10,8},{12,... | collective-permute-start | bytes 786440 | tf_op jit(solution)/shard_map/ppermute | solution.py:377
  84.5 3.4 %collective-permute-start.10 = (bf16[1,104,256]{2,1,0:T(8,128)(2,1)S(1)}, bf16[1,104,256]{2,1,0:T(8,128)(2,1)S(1)}, u32[]{:S(2)}, u32[]{:S(2)}) collective-permute-start(bf16[1,104,256]{2,1,0:T(8,128)(2,1)S(1)} %shard_map.135.a_ref), channel_id=1, source_target_pairs={{0,24},{8,16},{16,8},{24,0},{32,56},{40,48},{48,40},{56,32},{1,25}... | collective-permute-start | bytes 159752 | tf_op jit(solution)/shard_map/ppermute | solution.py:377
  87.9 0.7 collective-permute-start.9
  88.6 0.9 collective-permute-done.10.d_ref
  89.4 3.4 %collective-permute-done.9.c_ref = bf16[1,104,256]{2,1,0:T(8,128)(2,1)S(1)} collective-permute-done((bf16[1,104,256]{2,1,0:T(8,128)(2,1)S(1)}, bf16[1,104,256]{2,1,0:T(8,128)(2,1)S(1)}, u32[]{:S(2)}, u32[]{:S(2)}) %collective-permute-start.9) | collective-permute-done | bytes 53280 | tf_op jit(solution)/shard_map/ppermute | solution.py:377
  92.9 2.0 %collective-permute-start.13 = (bf16[1,256,256]{2,1,0:T(8,128)(2,1)S(1)}, bf16[1,256,256]{2,1,0:T(8,128)(2,1)S(1)}, u32[]{:S(2)}, u32[]{:S(2)}) collective-permute-start(bf16[1,256,256]{2,1,0:T(8,128)(2,1)S(1)} %get-tuple-element.84), channel_id=1, source_target_pairs={{0,6},{2,4},{4,2},{6,0},{1,7},{3,5},{5,3},{7,1},{8,14},{10,12},{12... | collective-permute-start | bytes 393224 | tf_op jit(solution)/shard_map/ppermute | solution.py:377
  95.2 5.0 %collective-permute-done.12.b_ref = bf16[1,104,256]{2,1,0:T(8,128)(2,1)S(1)} collective-permute-done((bf16[1,104,256]{2,1,0:T(8,128)(2,1)S(1)}, bf16[1,104,256]{2,1,0:T(8,128)(2,1)S(1)}, u32[]{:S(2)}, u32[]{:S(2)}) %collective-permute-start.12) | collective-permute-done | bytes 53280 | tf_op jit(solution)/shard_map/ppermute | solution.py:377
  100.3 0.7 collective-permute-start.16
  101.0 0.6 collective-permute-start.15
  101.6 2.1 %collective-permute-start.14 = (bf16[360,256]{1,0:T(8,128)(2,1)S(1)}, bf16[360,256]{1,0:T(8,128)(2,1)S(1)}, u32[]{:S(2)}, u32[]{:S(2)}) collective-permute-start(bf16[360,256]{1,0:T(8,128)(2,1)S(1)} %shard_map.139.refs_0_), channel_id=1, source_target_pairs={{0,6},{2,0},{4,2},{6,4},{1,7},{3,1},{5,3},{7,5},{8,14},{10,8},{12,... | collective-permute-start | bytes 552968 | tf_op jit(solution)/shard_map/ppermute | solution.py:373
  103.7 2.7 %collective-permute-done.16.refs_3_ = bf16[360,256]{1,0:T(8,128)(2,1)S(1)} collective-permute-done((bf16[360,256]{1,0:T(8,128)(2,1)S(1)}, bf16[360,256]{1,0:T(8,128)(2,1)S(1)}, u32[]{:S(2)}, u32[]{:S(2)}) %collective-permute-start.16) | collective-permute-done | bytes 184352 | tf_op jit(solution)/shard_map/ppermute | solution.py:373
  106.4 1.9 %collective-permute-done.15.refs_2_ = bf16[360,256]{1,0:T(8,128)(2,1)S(1)} collective-permute-done((bf16[360,256]{1,0:T(8,128)(2,1)S(1)}, bf16[360,256]{1,0:T(8,128)(2,1)S(1)}, u32[]{:S(2)}, u32[]{:S(2)}) %collective-permute-start.15) | collective-permute-done | bytes 184352 | tf_op jit(solution)/shard_map/ppermute | solution.py:373
  108.3 4.8 %collective-permute-start.17 = (bf16[4,256,256]{2,1,0:T(8,128)(2,1)S(1)}, bf16[4,256,256]{2,1,0:T(8,128)(2,1)S(1)}, u32[]{:S(2)}, u32[]{:S(2)}) collective-permute-start(bf16[4,256,256]{2,1,0:T(8,128)(2,1)S(1)} %get-tuple-element.89.refs_0_), channel_id=1, source_target_pairs={{0,1},{1,0},{2,3},{3,2},{4,5},{5,4},{6,7},{7,6},{8,9},{9,8},{10,11... | collective-permute-start | bytes 1572872 | tf_op jit(solution)/shard_map/ppermute | solution.py:377
  113.1 1.8 %collective-permute-start.20 = (bf16[4,104,256]{2,1,0:T(8,128)(2,1)S(1)}, bf16[4,104,256]{2,1,0:T(8,128)(2,1)S(1)}, u32[]{:S(2)}, u32[]{:S(2)}) collective-permute-start(bf16[4,104,256]{2,1,0:T(8,128)(2,1)S(1)} %get-tuple-element.92.refs_0_), channel_id=1, source_target_pairs={{0,128},{64,192},{128,0},{192,64},{1,129},{65,193},{129,1},{193,65... | collective-permute-start | bytes 638984 | tf_op jit(solution)/shard_map/ppermute | solution.py:373
  114.9 1.6 %collective-permute-start.19 = (bf16[4,104,256]{2,1,0:T(8,128)(2,1)S(1)}, bf16[4,104,256]{2,1,0:T(8,128)(2,1)S(1)}, u32[]{:S(2)}, u32[]{:S(2)}) collective-permute-start(bf16[4,104,256]{2,1,0:T(8,128)(2,1)S(1)} %get-tuple-element.92.refs_0_), channel_id=1, source_target_pairs={{0,64},{64,128},{128,192},{192,0},{1,65},{65,129},{129,193},{193,1... | collective-permute-start | bytes 638984 | tf_op jit(solution)/shard_map/ppermute | solution.py:373
  116.5 1.0 collective-permute-start.18
  117.6 1.5 %shard_map.142 = (f32[3072,256]{1,0:T(8,128)}, f32[4,256]{1,0:T(4,128)S(1)}) custom-call(s32[4]{0:T(128)S(1)} %pad_add_fusion.place_ref, bf16[4,104,256]{2,1,0:T(8,128)(2,1)S(1)} %get-tuple-element.92.refs_0_, bf16[4,104,256]{2,1,0:T(8,128)(2,1)S(1)} %collective-permute-done.21.refs_1_), custom_call_target="tpu_custom_call" | custom-call | bytes 2097152 | tf_op jit(solution)/shard_map/pallas_call | solution.py:303
  119.1 2.8 %shard_map.141 = (f32[2048,256]{1,0:T(8,128)}, f32[16,128]{1,0:T(8,128)}) custom-call(s32[4]{0:T(128)S(1)} %pad_add_fusion.place_ref, bf16[4,256,256]{2,1,0:T(8,128)(2,1)S(1)} %get-tuple-element.89.refs_0_, bf16[4,256,256]{2,1,0:T(8,128)(2,1)S(1)} %collective-permute-done.17.refs_1_, bf16[2048,256]{1,0:T(8,128)(2,1)S(1)} %copy-done.1, ...), custom_call_target="tpu_custom_call" | custom-call | bytes 1048576 | tf_op jit(solution)/shard_map/pallas_call | solution.py:36
  122.0 4.4 %collective-permute-done.19.refs_1_ = bf16[4,104,256]{2,1,0:T(8,128)(2,1)S(1)} collective-permute-done((bf16[4,104,256]{2,1,0:T(8,128)(2,1)S(1)}, bf16[4,104,256]{2,1,0:T(8,128)(2,1)S(1)}, u32[]{:S(2)}, u32[]{:S(2)}) %collective-permute-start.19) | collective-permute-done | bytes 213024 | tf_op jit(solution)/shard_map/ppermute | solution.py:373
  126.4 1.0 collective-permute-start.22
  127.3 0.5 collective-permute-start.24
  127.9 1.7 %shard_map.143 = (f32[3072,256]{1,0:T(8,128)}, f32[4,256]{1,0:T(4,128)S(1)}) custom-call(s32[4]{0:T(128)S(1)} %pad_add_fusion.place_ref, bf16[4,104,256]{2,1,0:T(8,128)(2,1)S(1)} %collective-permute-done.18.refs_0_, bf16[4,104,256]{2,1,0:T(8,128)(2,1)S(1)} %collective-permute-done.19.refs_1_, ...), custom_call_target="tpu_custom_call", output_to_operand_aliasing={{0}: (4, {})} | custom-call | bytes 2097152 | tf_op jit(solution)/shard_map/pallas_call | solution.py:303
  129.5 2.2 %shard_map.144 = (f32[3072,256]{1,0:T(8,128)}, f32[4,256]{1,0:T(4,128)}) custom-call(s32[4]{0:T(128)S(1)} %pad_add_fusion.place_ref, bf16[4,104,256]{2,1,0:T(8,128)(2,1)S(1)} %collective-permute-done.22.refs_0_, bf16[4,104,256]{2,1,0:T(8,128)(2,1)S(1)} %collective-permute-done.23.refs_1_, ...), custom_call_target="tpu_custom_call", output_to_operand_aliasing={{0}: (4, {})} | custom-call | bytes 2097152 | tf_op jit(solution)/shard_map/pallas_call | solution.py:303
  (53 shorter events, 2.6 us)
Async XLA Ops:
  2.1 20.4 %all-to-all-start = ((s32[32,1,32]{2,1,0:T(1,128)}), s32[32,1,32]{2,1,0:T(1,128)S(1)}, u32[]{:S(2)}, u32[]{:S(2)}) async-start(s32[32,1,32]{2,1,0:T(1,128)} %compare_select_fusion), calls=%async_computation | async-start | bytes 32768 | tf_op jit(solution)/shard_map/all_to_all | solution.py:397
  15.0 1.2 copy-start
  16.6 11.5 %copy-start.5 = (s32[2,256]{1,0:T(2,128)S(1)}, s32[2,256]{1,0:T(2,128)}, u32[]{:S(2)}) copy-start(s32[2,256]{1,0:T(2,128)} %param.11) | copy-start | bytes 6148
  16.6 11.5 %copy-start.6 = (s32[1,2]{1,0:T(1,128)S(1)}, s32[1,2]{1,0:T(1,128)}, u32[]{:S(2)}) copy-start(s32[1,2]{1,0:T(1,128)} %param.10) | copy-start | bytes 28
  24.1 17.0 %copy-start.4 = (f32[4,256]{1,0:T(4,128)S(1)}, f32[4,256]{1,0:T(4,128)}, u32[]{:S(2)}) copy-start(f32[4,256]{1,0:T(4,128)} %gain_ref.1) | copy-start | bytes 12292
  24.1 17.0 %all-to-all-start.1 = ((bf16[32,32,256]{2,1,0:T(8,128)(2,1)}), bf16[32,32,256]{2,1,0:T(8,128)(2,1)S(1)}, u32[]{:S(2)}, u32[]{:S(2)}) async-start(bf16[32,32,256]{2,1,0:T(8,128)(2,1)} %shard_map.130), calls=%async_computation.1 | async-start | bytes 1048576 | tf_op jit(solution)/shard_map/all_to_all | solution.py:408
  41.1 1.0 copy-start.3
  48.3 10.2 %collective-permute-start = (bf16[16,104,256]{2,1,0:T(8,128)(2,1)}, bf16[16,104,256]{2,1,0:T(8,128)(2,1)S(1)}, u32[]{:S(2)}, u32[]{:S(2)}) collective-permute-start(bf16[16,104,256]{2,1,0:T(8,128)(2,1)} %get-tuple-element.55), channel_id=1, source_target_pairs={{0,1},{1,0},{2,3},{3,2},{4,5},{5,4},{6,7},{7,6},{8,9},{9,8},{10,11... | collective-permute-start | bytes 2555912 | tf_op jit(solution)/shard_map/ppermute | solution.py:377
  53.5 19.9 %all-to-all-start.2 = ((bf16[32,32,256]{2,1,0:T(8,128)(2,1)}), bf16[32,32,256]{2,1,0:T(8,128)(2,1)S(1)}, u32[]{:S(2)}, u32[]{:S(2)}) async-start(bf16[32,32,256]{2,1,0:T(8,128)(2,1)} %bitcast.24), calls=%async_computation.2 | async-start | bytes 1048576 | tf_op jit(solution)/shard_map/all_to_all | solution.py:444
  58.7 8.2 %collective-permute-start.1 = (bf16[4,104,256]{2,1,0:T(8,128)(2,1)S(1)}, bf16[4,104,256]{2,1,0:T(8,128)(2,1)S(1)}, u32[]{:S(2)}, u32[]{:S(2)}) collective-permute-start(bf16[4,104,256]{2,1,0:T(8,128)(2,1)S(1)} %get-tuple-element.57), channel_id=1, source_target_pairs={{0,4},{2,6},{4,0},{6,2},{1,5},{3,7},{5,1},{7,3},{8,12},{10,14},{12... | collective-permute-start | bytes 638984 | tf_op jit(solution)/shard_map/ppermute | solution.py:373
  61.7 10.3 %collective-permute-start.2 = (bf16[4,104,256]{2,1,0:T(8,128)(2,1)S(1)}, bf16[4,104,256]{2,1,0:T(8,128)(2,1)S(1)}, u32[]{:S(2)}, u32[]{:S(2)}) collective-permute-start(bf16[4,104,256]{2,1,0:T(8,128)(2,1)S(1)} %get-tuple-element.58), channel_id=1, source_target_pairs={{0,2},{2,4},{4,6},{6,0},{1,3},{3,5},{5,7},{7,1},{8,10},{10,12},{12... | collective-permute-start | bytes 638984 | tf_op jit(solution)/shard_map/ppermute | solution.py:373
  62.1 9.9 %collective-permute-start.3 = (bf16[4,104,256]{2,1,0:T(8,128)(2,1)S(1)}, bf16[4,104,256]{2,1,0:T(8,128)(2,1)S(1)}, u32[]{:S(2)}, u32[]{:S(2)}) collective-permute-start(bf16[4,104,256]{2,1,0:T(8,128)(2,1)S(1)} %get-tuple-element.59), channel_id=1, source_target_pairs={{0,6},{2,0},{4,2},{6,4},{1,7},{3,1},{5,3},{7,5},{8,14},{10,8},{12,... | collective-permute-start | bytes 638984 | tf_op jit(solution)/shard_map/ppermute | solution.py:373
  72.1 47.0 %copy-start.1 = (bf16[2048,256]{1,0:T(8,128)(2,1)S(1)}, bf16[2048,256]{1,0:T(8,128)(2,1)}, u32[]{:S(2)}) copy-start(bf16[2048,256]{1,0:T(8,128)(2,1)} %refs_2_.1) | copy-start | bytes 3145732
  72.1 47.0 %copy-start.2 = (f32[2048]{0:T(1024)S(1)}, f32[2048]{0:T(1024)}, u32[]{:S(2)}) copy-start(f32[2048]{0:T(1024)} %param.16) | copy-start | bytes 24580
  74.4 8.6 %collective-permute-start.7 = (bf16[4,256,256]{2,1,0:T(8,128)(2,1)S(1)}, bf16[4,256,256]{2,1,0:T(8,128)(2,1)S(1)}, u32[]{:S(2)}, u32[]{:S(2)}) collective-permute-start(bf16[4,256,256]{2,1,0:T(8,128)(2,1)S(1)} %get-tuple-element.68), channel_id=1, source_target_pairs={{0,1},{1,0},{2,3},{3,2},{4,5},{5,4},{6,7},{7,6},{8,9},{9,8},{10,11... | collective-permute-start | bytes 1572872 | tf_op jit(solution)/shard_map/ppermute | solution.py:377
  77.3 4.9 %collective-permute-start.4 = (bf16[1,104,256]{2,1,0:T(8,128)(2,1)S(1)}, bf16[1,104,256]{2,1,0:T(8,128)(2,1)S(1)}, u32[]{:S(2)}, u32[]{:S(2)}) collective-permute-start(bf16[1,104,256]{2,1,0:T(8,128)(2,1)S(1)} %get-tuple-element.61), channel_id=1, source_target_pairs={{0,128},{64,192},{128,0},{192,64},{1,129},{65,193},{129,1},{193,65... | collective-permute-start | bytes 159752 | tf_op jit(solution)/shard_map/ppermute | solution.py:373
  78.5 4.5 %collective-permute-start.5 = (bf16[1,104,256]{2,1,0:T(8,128)(2,1)S(1)}, bf16[1,104,256]{2,1,0:T(8,128)(2,1)S(1)}, u32[]{:S(2)}, u32[]{:S(2)}) collective-permute-start(bf16[1,104,256]{2,1,0:T(8,128)(2,1)S(1)} %get-tuple-element.62), channel_id=1, source_target_pairs={{0,64},{64,128},{128,192},{192,0},{1,65},{65,129},{129,193},{193,1... | collective-permute-start | bytes 159752 | tf_op jit(solution)/shard_map/ppermute | solution.py:373
  78.8 4.1 %collective-permute-start.6 = (bf16[1,104,256]{2,1,0:T(8,128)(2,1)S(1)}, bf16[1,104,256]{2,1,0:T(8,128)(2,1)S(1)}, u32[]{:S(2)}, u32[]{:S(2)}) collective-permute-start(bf16[1,104,256]{2,1,0:T(8,128)(2,1)S(1)} %get-tuple-element.63), channel_id=1, source_target_pairs={{0,192},{64,0},{128,64},{192,128},{1,193},{65,1},{129,65},{193,129... | collective-permute-start | bytes 159752 | tf_op jit(solution)/shard_map/ppermute | solution.py:373
  83.1 9.7 %collective-permute-start.11 = (bf16[2,256,256]{2,1,0:T(8,128)(2,1)S(1)}, bf16[2,256,256]{2,1,0:T(8,128)(2,1)S(1)}, u32[]{:S(2)}, u32[]{:S(2)}) collective-permute-start(bf16[2,256,256]{2,1,0:T(8,128)(2,1)S(1)} %get-tuple-element.76), channel_id=1, source_target_pairs={{0,2},{2,0},{4,6},{6,4},{1,3},{3,1},{5,7},{7,5},{8,10},{10,8},{12,... | collective-permute-start | bytes 786440 | tf_op jit(solution)/shard_map/ppermute | solution.py:377
  84.5 4.9 %collective-permute-start.10 = (bf16[1,104,256]{2,1,0:T(8,128)(2,1)S(1)}, bf16[1,104,256]{2,1,0:T(8,128)(2,1)S(1)}, u32[]{:S(2)}, u32[]{:S(2)}) collective-permute-start(bf16[1,104,256]{2,1,0:T(8,128)(2,1)S(1)} %shard_map.135.a_ref), channel_id=1, source_target_pairs={{0,24},{8,16},{16,8},{24,0},{32,56},{40,48},{48,40},{56,32},{1,25}... | collective-permute-start | bytes 159752 | tf_op jit(solution)/shard_map/ppermute | solution.py:377
  87.9 4.9 %collective-permute-start.9 = (bf16[1,104,256]{2,1,0:T(8,128)(2,1)S(1)}, bf16[1,104,256]{2,1,0:T(8,128)(2,1)S(1)}, u32[]{:S(2)}, u32[]{:S(2)}) collective-permute-start(bf16[1,104,256]{2,1,0:T(8,128)(2,1)S(1)} %shard_map.135.a_ref), channel_id=1, source_target_pairs={{0,16},{8,24},{16,0},{24,8},{32,48},{40,56},{48,32},{56,40},{1,17}... | collective-permute-start | bytes 159752 | tf_op jit(solution)/shard_map/ppermute | solution.py:377
  88.6 4.2 %collective-permute-start.8 = (bf16[1,104,256]{2,1,0:T(8,128)(2,1)S(1)}, bf16[1,104,256]{2,1,0:T(8,128)(2,1)S(1)}, u32[]{:S(2)}, u32[]{:S(2)}) collective-permute-start(bf16[1,104,256]{2,1,0:T(8,128)(2,1)S(1)} %shard_map.135.a_ref), channel_id=1, source_target_pairs={{0,8},{8,0},{16,24},{24,16},{32,40},{40,32},{48,56},{56,48},{1,9},... | collective-permute-start | bytes 159752 | tf_op jit(solution)/shard_map/ppermute | solution.py:377
  92.9 7.3 %collective-permute-start.13 = (bf16[1,256,256]{2,1,0:T(8,128)(2,1)S(1)}, bf16[1,256,256]{2,1,0:T(8,128)(2,1)S(1)}, u32[]{:S(2)}, u32[]{:S(2)}) collective-permute-start(bf16[1,256,256]{2,1,0:T(8,128)(2,1)S(1)} %get-tuple-element.84), channel_id=1, source_target_pairs={{0,6},{2,4},{4,2},{6,0},{1,7},{3,5},{5,3},{7,1},{8,14},{10,12},{12... | collective-permute-start | bytes 393224 | tf_op jit(solution)/shard_map/ppermute | solution.py:377
  94.9 5.3 %collective-permute-start.12 = (bf16[1,104,256]{2,1,0:T(8,128)(2,1)S(1)}, bf16[1,104,256]{2,1,0:T(8,128)(2,1)S(1)}, u32[]{:S(2)}, u32[]{:S(2)}) collective-permute-start(bf16[1,104,256]{2,1,0:T(8,128)(2,1)S(1)} %shard_map.137.a_ref), channel_id=1, source_target_pairs={{0,48},{8,56},{16,32},{24,40},{32,16},{40,24},{48,0},{56,8},{1,49}... | collective-permute-start | bytes 159752 | tf_op jit(solution)/shard_map/ppermute | solution.py:377
  100.3 6.1 %collective-permute-start.16 = (bf16[360,256]{1,0:T(8,128)(2,1)S(1)}, bf16[360,256]{1,0:T(8,128)(2,1)S(1)}, u32[]{:S(2)}, u32[]{:S(2)}) collective-permute-start(bf16[360,256]{1,0:T(8,128)(2,1)S(1)} %shard_map.139.refs_0_), channel_id=1, source_target_pairs={{0,4},{2,6},{4,0},{6,2},{1,5},{3,7},{5,1},{7,3},{8,12},{10,14},{12... | collective-permute-start | bytes 552968 | tf_op jit(solution)/shard_map/ppermute | solution.py:373
  101.0 7.2 %collective-permute-start.15 = (bf16[360,256]{1,0:T(8,128)(2,1)S(1)}, bf16[360,256]{1,0:T(8,128)(2,1)S(1)}, u32[]{:S(2)}, u32[]{:S(2)}) collective-permute-start(bf16[360,256]{1,0:T(8,128)(2,1)S(1)} %shard_map.139.refs_0_), channel_id=1, source_target_pairs={{0,2},{2,4},{4,6},{6,0},{1,3},{3,5},{5,7},{7,1},{8,10},{10,12},{12... | collective-permute-start | bytes 552968 | tf_op jit(solution)/shard_map/ppermute | solution.py:373
  101.6 6.6 %collective-permute-start.14 = (bf16[360,256]{1,0:T(8,128)(2,1)S(1)}, bf16[360,256]{1,0:T(8,128)(2,1)S(1)}, u32[]{:S(2)}, u32[]{:S(2)}) collective-permute-start(bf16[360,256]{1,0:T(8,128)(2,1)S(1)} %shard_map.139.refs_0_), channel_id=1, source_target_pairs={{0,6},{2,0},{4,2},{6,4},{1,7},{3,1},{5,3},{7,5},{8,14},{10,8},{12,... | collective-permute-start | bytes 552968 | tf_op jit(solution)/shard_map/ppermute | solution.py:373
  108.3 10.8 %collective-permute-start.17 = (bf16[4,256,256]{2,1,0:T(8,128)(2,1)S(1)}, bf16[4,256,256]{2,1,0:T(8,128)(2,1)S(1)}, u32[]{:S(2)}, u32[]{:S(2)}) collective-permute-start(bf16[4,256,256]{2,1,0:T(8,128)(2,1)S(1)} %get-tuple-element.89.refs_0_), channel_id=1, source_target_pairs={{0,1},{1,0},{2,3},{3,2},{4,5},{5,4},{6,7},{7,6},{8,9},{9,8},{10,11... | collective-permute-start | bytes 1572872 | tf_op jit(solution)/shard_map/ppermute | solution.py:377
  113.0 4.5 %collective-permute-start.21 = (bf16[4,104,256]{2,1,0:T(8,128)(2,1)S(1)}, bf16[4,104,256]{2,1,0:T(8,128)(2,1)S(1)}, u32[]{:S(2)}, u32[]{:S(2)}) collective-permute-start(bf16[4,104,256]{2,1,0:T(8,128)(2,1)S(1)} %get-tuple-element.92.refs_0_), channel_id=1, source_target_pairs={{0,1},{1,0},{2,3},{3,2},{4,5},{5,4},{6,7},{7,6},{8,9},{9,8},{10,11... | collective-permute-start | bytes 638984 | tf_op jit(solution)/shard_map/ppermute | solution.py:377
  113.1 8.8 %collective-permute-start.20 = (bf16[4,104,256]{2,1,0:T(8,128)(2,1)S(1)}, bf16[4,104,256]{2,1,0:T(8,128)(2,1)S(1)}, u32[]{:S(2)}, u32[]{:S(2)}) collective-permute-start(bf16[4,104,256]{2,1,0:T(8,128)(2,1)S(1)} %get-tuple-element.92.refs_0_), channel_id=1, source_target_pairs={{0,128},{64,192},{128,0},{192,64},{1,129},{65,193},{129,1},{193,65... | collective-permute-start | bytes 638984 | tf_op jit(solution)/shard_map/ppermute | solution.py:373
  114.9 11.5 %collective-permute-start.19 = (bf16[4,104,256]{2,1,0:T(8,128)(2,1)S(1)}, bf16[4,104,256]{2,1,0:T(8,128)(2,1)S(1)}, u32[]{:S(2)}, u32[]{:S(2)}) collective-permute-start(bf16[4,104,256]{2,1,0:T(8,128)(2,1)S(1)} %get-tuple-element.92.refs_0_), channel_id=1, source_target_pairs={{0,64},{64,128},{128,192},{192,0},{1,65},{65,129},{129,193},{193,1... | collective-permute-start | bytes 638984 | tf_op jit(solution)/shard_map/ppermute | solution.py:373
  116.5 9.9 %collective-permute-start.18 = (bf16[4,104,256]{2,1,0:T(8,128)(2,1)S(1)}, bf16[4,104,256]{2,1,0:T(8,128)(2,1)S(1)}, u32[]{:S(2)}, u32[]{:S(2)}) collective-permute-start(bf16[4,104,256]{2,1,0:T(8,128)(2,1)S(1)} %get-tuple-element.92.refs_0_), channel_id=1, source_target_pairs={{0,192},{64,0},{128,64},{192,128},{1,193},{65,1},{129,65},{193,129... | collective-permute-start | bytes 638984 | tf_op jit(solution)/shard_map/ppermute | solution.py:373
  126.4 3.1 %collective-permute-start.22 = (bf16[4,104,256]{2,1,0:T(8,128)(2,1)S(1)}, bf16[4,104,256]{2,1,0:T(8,128)(2,1)S(1)}, u32[]{:S(2)}, u32[]{:S(2)}) collective-permute-start(bf16[4,104,256]{2,1,0:T(8,128)(2,1)S(1)} %collective-permute-done.18.refs_0_), channel_id=1, source_target_pairs={{0,1},{1,0},{2,3},{3,2},{4,5},{5,4},{6,7},{7,6},{8,9},{9,8},{10,11... | collective-permute-start | bytes 638984 | tf_op jit(solution)/shard_map/ppermute | solution.py:377
  127.3 2.2 %collective-permute-start.23 = (bf16[4,104,256]{2,1,0:T(8,128)(2,1)S(1)}, bf16[4,104,256]{2,1,0:T(8,128)(2,1)S(1)}, u32[]{:S(2)}, u32[]{:S(2)}) collective-permute-start(bf16[4,104,256]{2,1,0:T(8,128)(2,1)S(1)} %collective-permute-done.19.refs_1_), channel_id=1, source_target_pairs={{0,1},{1,0},{2,3},{3,2},{4,5},{5,4},{6,7},{7,6},{8,9},{9,8},{10,11... | collective-permute-start | bytes 638984 | tf_op jit(solution)/shard_map/ppermute | solution.py:377
  127.3 2.2 %collective-permute-start.24 = (bf16[4,104,256]{2,1,0:T(8,128)(2,1)S(1)}, bf16[4,104,256]{2,1,0:T(8,128)(2,1)S(1)}, u32[]{:S(2)}, u32[]{:S(2)}) collective-permute-start(bf16[4,104,256]{2,1,0:T(8,128)(2,1)S(1)} %collective-permute-done.20.refs_2_), channel_id=1, source_target_pairs={{0,1},{1,0},{2,3},{3,2},{4,5},{5,4},{6,7},{7,6},{8,9},{9,8},{10,11... | collective-permute-start | bytes 638984 | tf_op jit(solution)/shard_map/ppermute | solution.py:377

commit v6 on v5

--- a/solution.py
+++ b/solution.py
@@ -450,14 +450,14 @@
     parts = call(core_sum_kernel, [slab4] * 4, [keep, got])
     parts = [parts[0]] + [shifted(parts[k], "y", 4, k) for k in (2, 1, 3)]
     parts = call(four_sum_kernel, [slab1] * 4, parts)
+    parts = [parts[0]] + [shifted(parts[k], "x", 4, k) for k in (2, 1, 3)]
     keep_rows, send_rows = call(
         scatter_kernel,
         [block4, block4],
-        [place, target, after(returned, parts[0])],
+        [place, target, after(returned, *parts[1:])],
         specs=[SMEM, VMEM, VMEM],
         flops=1 << 29,
     )
-    parts = [parts[0]] + [shifted(parts[k], "x", 4, k) for k in (2, 1, 3)]
     sums = [keep_rows, crossed(send_rows, "core", 2, 1)]
     parts, sums = lax.optimization_barrier((parts, sums))
 

time: 133 us -> 133 us (level)
    ppermute x12, waiting for transfers between devices: 18.4 us -> 21.4 us  [shifted(): lax.ppermute(values, axis, [(i, (i + offset) % size) for i in range(size)])]
    ppermute x13, starting transfers between devices: 22.1 us -> 20.5 us  [crossed(): return lax.ppermute(values, axis, [(i, i ^ bits) for i in range(size)])]
  transfers between devices with their start and end apart: 28 -> 28, of which waited for: 13 -> 12; matrix products, arithmetic and copies ran while one was open for 3% -> 3% of each run, Pallas kernels for 5% -> 5%
where the time goes in v6:
time: 133 us; the launch traced here: 132 us
  starting transfers between devices  59.9 us (45%)
  waiting for transfers between devices  45.9 us (35%)
  Pallas kernels  18.2 us (14%)
  local copies, waits for them, and re-layouts  5.04 us (4%)
  other arithmetic  1.89 us (1%)
    ppermute x12, waiting for transfers between devices, shifted(): lax.ppermute(values, axis, [(i, (i + offset) % size) for i in range(size)])  21.4 us
    ppermute x13, starting transfers between devices, crossed(): return lax.ppermute(values, axis, [(i, i ^ bits) for i in range(size)])  20.5 us
    ppermute x12, starting transfers between devices, shifted(): lax.ppermute(values, axis, [(i, (i + offset) % size) for i in range(size)])  18.5 us
    pallas_call x13, Pallas kernels, call(): pl.pallas_call(kernel, out_shape=outs, in_specs=specs, out_specs=out_spec...  12.8 us
    all_to_all x1, starting transfers between devices, body(): lax.all_to_all(wanted, table_axes, split_axis=0, concat_axis=0, tiled=True)  11.9 us
    all_to_all x1, waiting for transfers between devices, body(): lax.all_to_all(sending, table_axes, split_axis=0, concat_axis=0, tiled=True)  10.6 us
    ppermute x13, waiting for transfers between devices, crossed(): return lax.ppermute(values, axis, [(i, i ^ bits) for i in range(size)])  8.08 us
    all_to_all x1, waiting for transfers between devices, body(): lax.all_to_all(wanted, table_axes, split_axis=0, concat_axis=0, tiled=True)  5.86 us
  transfers between devices with their start and end apart: 28, of which 12 were waited for; matrix products, arithmetic and copies ran while one was open for 3% of the time, Pallas kernels for 5%

profile of v6, /device:TPU:1, one launch (start us, length us, event | category | flops | bytes accessed | tf_op | source)
XLA Modules:
  0.0 132.1 jit_solution(14679393364856868832)
XLA Ops:
  0.6 1.4 %compare_select_fusion = s32[32,1,32]{2,1,0:T(1,128)} fusion(s32[32,1,32]{2,1,0:T(1,128)} %bitcast.61, s32[32]{0:T(128)} %bitcast.68, s32[32]{0:T(128)S(1)} %iota_multiply_fusion), kind=kLoop, calls=%fused_computation.14 | loop fusion | flops 3072 | bytes 8448 | tf_op jit(solution)/shard_map/jit(_where)/select_n | solution.py:396
  2.1 11.9 %all-to-all-start = ((s32[32,1,32]{2,1,0:T(1,128)}), s32[32,1,32]{2,1,0:T(1,128)S(1)}, u32[]{:S(2)}, u32[]{:S(2)}) async-start(s32[32,1,32]{2,1,0:T(1,128)} %compare_select_fusion), calls=%async_computation | async-start | bytes 32768 | tf_op jit(solution)/shard_map/all_to_all | solution.py:397
  13.9 1.0 copy.28.scales_ref.refs_3_
  15.0 1.2 copy-done
  16.2 0.4 shard_map.129.table_ref
  16.6 5.9 %all-to-all-done = s32[32,1,32]{2,1,0:T(1,128)S(1)} async-done(((s32[32,1,32]{2,1,0:T(1,128)}), s32[32,1,32]{2,1,0:T(1,128)S(1)}, u32[]{:S(2)}, u32[]{:S(2)}) %all-to-all-start) | async-done | bytes 4128 | tf_op jit(solution)/shard_map/all_to_all | solution.py:397
  22.5 1.6 %shard_map.130 = bf16[32,32,256]{2,1,0:T(8,128)(2,1)} custom-call(s32[32,32]{1,0:T(8,128)S(1)} %bitcast.56, bf16[2048,256]{1,0:T(8,128)(2,1)S(1)} %shard_map.129.table_ref), custom_call_target="tpu_custom_call" | custom-call | flops 1073741824 | bytes 1048576 | tf_op jit(solution)/shard_map/pallas_call | solution.py:36
  24.1 4.0 %all-to-all-start.1 = ((bf16[32,32,256]{2,1,0:T(8,128)(2,1)}), bf16[32,32,256]{2,1,0:T(8,128)(2,1)S(1)}, u32[]{:S(2)}, u32[]{:S(2)}) async-start(bf16[32,32,256]{2,1,0:T(8,128)(2,1)} %shard_map.130), calls=%async_computation.1 | async-start | bytes 1048576 | tf_op jit(solution)/shard_map/all_to_all | solution.py:408
  28.6 1.5 %slice_bitcast_fusion = (bf16[256,256]{1,0:T(8,128)(2,1)S(1)}, bf16[256,256]{1,0:T(8,128)(2,1)S(1)}, bf16[256,256]{1,0:T(8,128)(2,1)S(1)}, bf16[256,256]{1,0:T(8...) fusion(bf16[4,3,256,256]{3,2,1,0:T(8,128)(2,1)} %param.17), kind=kLoop, calls=%fused_computation.2 | loop fusion | bytes 3145728 | tf_op jit(solution)/shard_map/squeeze | solution.py:427
  30.5 10.6 %all-to-all-done.1 = bf16[32,32,256]{2,1,0:T(8,128)(2,1)S(1)} async-done(((bf16[32,32,256]{2,1,0:T(8,128)(2,1)}), bf16[32,32,256]{2,1,0:T(8,128)(2,1)S(1)}, u32[]{:S(2)}, u32[]{:S(2)}) %all-to-all-start.1) | async-done | bytes 524320 | tf_op jit(solution)/shard_map/all_to_all | solution.py:408
  41.1 0.9 copy-done.3
  42.0 6.3 %shard_map.131 = (bf16[1024,256]{1,0:T(8,128)(2,1)}, bf16[16,104,256]{2,1,0:T(8,128)(2,1)S(1)}, bf16[16,104,256]{2,1,0:T(8,128)(2,1)}) custom-call(s32[4]{0:T(128)S(1)} %pad_add_fusion.place_ref, s32[1,512]{1,0:T(1,128)S(1)} %bitcast.58, s32[1,320]{1,0:T(1,128)S(1)} %reshape.129.code_ref, bf16[1024,256]{1,0:T(8,128)(2,1)S(1)} %bitcast.55, ...), custom_call_target="tpu_custom_call" | custom-call | flops 4294967296 | bytes 1048576 | tf_op jit(solution)/shard_map/pallas_call | solution.py:36
  48.3 5.2 %collective-permute-start = (bf16[16,104,256]{2,1,0:T(8,128)(2,1)}, bf16[16,104,256]{2,1,0:T(8,128)(2,1)S(1)}, u32[]{:S(2)}, u32[]{:S(2)}) collective-permute-start(bf16[16,104,256]{2,1,0:T(8,128)(2,1)} %get-tuple-element.55), channel_id=1, source_target_pairs={{0,1},{1,0},{2,3},{3,2},{4,5},{5,4},{6,7},{7,6},{8,9},{9,8},{10,11... | collective-permute-start | bytes 2555912 | tf_op jit(solution)/shard_map/ppermute | solution.py:377
  53.5 5.0 %all-to-all-start.2 = ((bf16[32,32,256]{2,1,0:T(8,128)(2,1)}), bf16[32,32,256]{2,1,0:T(8,128)(2,1)S(1)}, u32[]{:S(2)}, u32[]{:S(2)}) async-start(bf16[32,32,256]{2,1,0:T(8,128)(2,1)} %bitcast.24), calls=%async_computation.2 | async-start | bytes 1048576 | tf_op jit(solution)/shard_map/all_to_all | solution.py:444
  58.7 3.0 %collective-permute-start.1 = (bf16[4,104,256]{2,1,0:T(8,128)(2,1)S(1)}, bf16[4,104,256]{2,1,0:T(8,128)(2,1)S(1)}, u32[]{:S(2)}, u32[]{:S(2)}) collective-permute-start(bf16[4,104,256]{2,1,0:T(8,128)(2,1)S(1)} %get-tuple-element.57), channel_id=1, source_target_pairs={{0,4},{2,6},{4,0},{6,2},{1,5},{3,7},{5,1},{7,3},{8,12},{10,14},{12... | collective-permute-start | bytes 638984 | tf_op jit(solution)/shard_map/ppermute | solution.py:373
  61.7 0.4 collective-permute-start.2
  62.1 2.3 %collective-permute-start.3 = (bf16[4,104,256]{2,1,0:T(8,128)(2,1)S(1)}, bf16[4,104,256]{2,1,0:T(8,128)(2,1)S(1)}, u32[]{:S(2)}, u32[]{:S(2)}) collective-permute-start(bf16[4,104,256]{2,1,0:T(8,128)(2,1)S(1)} %get-tuple-element.59), channel_id=1, source_target_pairs={{0,6},{2,0},{4,2},{6,4},{1,7},{3,1},{5,3},{7,5},{8,14},{10,8},{12,... | collective-permute-start | bytes 638984 | tf_op jit(solution)/shard_map/ppermute | solution.py:373
  64.4 2.5 %collective-permute-done.1.b_ref = bf16[4,104,256]{2,1,0:T(8,128)(2,1)S(1)} collective-permute-done((bf16[4,104,256]{2,1,0:T(8,128)(2,1)S(1)}, bf16[4,104,256]{2,1,0:T(8,128)(2,1)S(1)}, u32[]{:S(2)}, u32[]{:S(2)}) %collective-permute-start.1) | collective-permute-done | bytes 213024 | tf_op jit(solution)/shard_map/ppermute | solution.py:373
  66.9 5.2 %collective-permute-done.2.c_ref = bf16[4,104,256]{2,1,0:T(8,128)(2,1)S(1)} collective-permute-done((bf16[4,104,256]{2,1,0:T(8,128)(2,1)S(1)}, bf16[4,104,256]{2,1,0:T(8,128)(2,1)S(1)}, u32[]{:S(2)}, u32[]{:S(2)}) %collective-permute-start.2) | collective-permute-done | bytes 213024 | tf_op jit(solution)/shard_map/ppermute | solution.py:373
  72.2 2.7 %collective-permute-start.4 = (bf16[1,104,256]{2,1,0:T(8,128)(2,1)S(1)}, bf16[1,104,256]{2,1,0:T(8,128)(2,1)S(1)}, u32[]{:S(2)}, u32[]{:S(2)}) collective-permute-start(bf16[1,104,256]{2,1,0:T(8,128)(2,1)S(1)} %get-tuple-element.61), channel_id=1, source_target_pairs={{0,128},{64,192},{128,0},{192,64},{1,129},{65,193},{129,1},{193,65... | collective-permute-start | bytes 159752 | tf_op jit(solution)/shard_map/ppermute | solution.py:373
  75.3 2.4 %collective-permute-start.6 = (bf16[1,104,256]{2,1,0:T(8,128)(2,1)S(1)}, bf16[1,104,256]{2,1,0:T(8,128)(2,1)S(1)}, u32[]{:S(2)}, u32[]{:S(2)}) collective-permute-start(bf16[1,104,256]{2,1,0:T(8,128)(2,1)S(1)} %get-tuple-element.63), channel_id=1, source_target_pairs={{0,192},{64,0},{128,64},{192,128},{1,193},{65,1},{129,65},{193,129... | collective-permute-start | bytes 159752 | tf_op jit(solution)/shard_map/ppermute | solution.py:373
  77.6 1.5 %collective-permute-done.5.c_ref = bf16[1,104,256]{2,1,0:T(8,128)(2,1)S(1)} collective-permute-done((bf16[1,104,256]{2,1,0:T(8,128)(2,1)S(1)}, bf16[1,104,256]{2,1,0:T(8,128)(2,1)S(1)}, u32[]{:S(2)}, u32[]{:S(2)}) %collective-permute-start.5) | collective-permute-done | bytes 53280 | tf_op jit(solution)/shard_map/ppermute | solution.py:373
  79.1 1.0 shard_map.134
  80.2 2.4 %collective-permute-start.7 = (bf16[4,256,256]{2,1,0:T(8,128)(2,1)S(1)}, bf16[4,256,256]{2,1,0:T(8,128)(2,1)S(1)}, u32[]{:S(2)}, u32[]{:S(2)}) collective-permute-start(bf16[4,256,256]{2,1,0:T(8,128)(2,1)S(1)} %get-tuple-element.68), channel_id=1, source_target_pairs={{0,1},{1,0},{2,3},{3,2},{4,5},{5,4},{6,7},{7,6},{8,9},{9,8},{10,11... | collective-permute-start | bytes 1572872 | tf_op jit(solution)/shard_map/ppermute | solution.py:377
  82.6 1.5 %collective-permute-done.7.got_ref = bf16[4,256,256]{2,1,0:T(8,128)(2,1)S(1)} collective-permute-done((bf16[4,256,256]{2,1,0:T(8,128)(2,1)S(1)}, bf16[4,256,256]{2,1,0:T(8,128)(2,1)S(1)}, u32[]{:S(2)}, u32[]{:S(2)}) %collective-permute-start.7) | collective-permute-done | bytes 524320 | tf_op jit(solution)/shard_map/ppermute | solution.py:377
  84.3 1.2 collective-permute-start.11
  85.5 3.1 %collective-permute-start.10 = (bf16[1,104,256]{2,1,0:T(8,128)(2,1)S(1)}, bf16[1,104,256]{2,1,0:T(8,128)(2,1)S(1)}, u32[]{:S(2)}, u32[]{:S(2)}) collective-permute-start(bf16[1,104,256]{2,1,0:T(8,128)(2,1)S(1)} %shard_map.135.a_ref), channel_id=1, source_target_pairs={{0,24},{8,16},{16,8},{24,0},{32,56},{40,48},{48,40},{56,32},{1,25}... | collective-permute-start | bytes 159752 | tf_op jit(solution)/shard_map/ppermute | solution.py:377
  88.6 0.6 collective-permute-start.8
  89.1 1.3 collective-permute-done.10.d_ref
  90.4 2.8 %collective-permute-done.9.c_ref = bf16[1,104,256]{2,1,0:T(8,128)(2,1)S(1)} collective-permute-done((bf16[1,104,256]{2,1,0:T(8,128)(2,1)S(1)}, bf16[1,104,256]{2,1,0:T(8,128)(2,1)S(1)}, u32[]{:S(2)}, u32[]{:S(2)}) %collective-permute-start.9) | collective-permute-done | bytes 53280 | tf_op jit(solution)/shard_map/ppermute | solution.py:377
  93.3 1.7 %collective-permute-start.13 = (bf16[1,256,256]{2,1,0:T(8,128)(2,1)S(1)}, bf16[1,256,256]{2,1,0:T(8,128)(2,1)S(1)}, u32[]{:S(2)}, u32[]{:S(2)}) collective-permute-start(bf16[1,256,256]{2,1,0:T(8,128)(2,1)S(1)} %get-tuple-element.84), channel_id=1, source_target_pairs={{0,6},{2,4},{4,2},{6,0},{1,7},{3,5},{5,3},{7,1},{8,14},{10,12},{12... | collective-permute-start | bytes 393224 | tf_op jit(solution)/shard_map/ppermute | solution.py:377
  95.1 2.8 %collective-permute-start.12 = (bf16[1,104,256]{2,1,0:T(8,128)(2,1)S(1)}, bf16[1,104,256]{2,1,0:T(8,128)(2,1)S(1)}, u32[]{:S(2)}, u32[]{:S(2)}) collective-permute-start(bf16[1,104,256]{2,1,0:T(8,128)(2,1)S(1)} %shard_map.137.a_ref), channel_id=1, source_target_pairs={{0,48},{8,56},{16,32},{24,40},{32,16},{40,24},{48,0},{56,8},{1,49}... | collective-permute-start | bytes 159752 | tf_op jit(solution)/shard_map/ppermute | solution.py:377
  97.9 2.4 %collective-permute-done.12.b_ref = bf16[1,104,256]{2,1,0:T(8,128)(2,1)S(1)} collective-permute-done((bf16[1,104,256]{2,1,0:T(8,128)(2,1)S(1)}, bf16[1,104,256]{2,1,0:T(8,128)(2,1)S(1)}, u32[]{:S(2)}, u32[]{:S(2)}) %collective-permute-start.12) | collective-permute-done | bytes 53280 | tf_op jit(solution)/shard_map/ppermute | solution.py:377
  100.3 0.9 collective-permute-start.16
  101.2 0.8 collective-permute-start.15
  102.0 1.9 %collective-permute-start.14 = (bf16[360,256]{1,0:T(8,128)(2,1)S(1)}, bf16[360,256]{1,0:T(8,128)(2,1)S(1)}, u32[]{:S(2)}, u32[]{:S(2)}) collective-permute-start(bf16[360,256]{1,0:T(8,128)(2,1)S(1)} %shard_map.139.refs_0_), channel_id=1, source_target_pairs={{0,6},{2,0},{4,2},{6,4},{1,7},{3,1},{5,3},{7,5},{8,14},{10,8},{12,... | collective-permute-start | bytes 552968 | tf_op jit(solution)/shard_map/ppermute | solution.py:373
  103.9 2.5 %collective-permute-done.16.refs_3_ = bf16[360,256]{1,0:T(8,128)(2,1)S(1)} collective-permute-done((bf16[360,256]{1,0:T(8,128)(2,1)S(1)}, bf16[360,256]{1,0:T(8,128)(2,1)S(1)}, u32[]{:S(2)}, u32[]{:S(2)}) %collective-permute-start.16) | collective-permute-done | bytes 184352 | tf_op jit(solution)/shard_map/ppermute | solution.py:373
  106.4 4.7 %collective-permute-done.15.refs_2_ = bf16[360,256]{1,0:T(8,128)(2,1)S(1)} collective-permute-done((bf16[360,256]{1,0:T(8,128)(2,1)S(1)}, bf16[360,256]{1,0:T(8,128)(2,1)S(1)}, u32[]{:S(2)}, u32[]{:S(2)}) %collective-permute-start.15) | collective-permute-done | bytes 184352 | tf_op jit(solution)/shard_map/ppermute | solution.py:373
  111.2 1.9 %collective-permute-start.17 = (bf16[4,256,256]{2,1,0:T(8,128)(2,1)S(1)}, bf16[4,256,256]{2,1,0:T(8,128)(2,1)S(1)}, u32[]{:S(2)}, u32[]{:S(2)}) collective-permute-start(bf16[4,256,256]{2,1,0:T(8,128)(2,1)S(1)} %get-tuple-element.89.refs_0_), channel_id=1, source_target_pairs={{0,1},{1,0},{2,3},{3,2},{4,5},{5,4},{6,7},{7,6},{8,9},{9,8},{10,11... | collective-permute-start | bytes 1572872 | tf_op jit(solution)/shard_map/ppermute | solution.py:377
  113.2 1.2 collective-permute-start.20
  114.4 2.3 %collective-permute-start.19 = (bf16[4,104,256]{2,1,0:T(8,128)(2,1)S(1)}, bf16[4,104,256]{2,1,0:T(8,128)(2,1)S(1)}, u32[]{:S(2)}, u32[]{:S(2)}) collective-permute-start(bf16[4,104,256]{2,1,0:T(8,128)(2,1)S(1)} %get-tuple-element.92.refs_0_), channel_id=1, source_target_pairs={{0,64},{64,128},{128,192},{192,0},{1,65},{65,129},{129,193},{193,1... | collective-permute-start | bytes 638984 | tf_op jit(solution)/shard_map/ppermute | solution.py:373
  117.0 1.5 %shard_map.142 = (f32[3072,256]{1,0:T(8,128)}, f32[4,256]{1,0:T(4,128)S(1)}) custom-call(s32[4]{0:T(128)S(1)} %pad_add_fusion.place_ref, bf16[4,104,256]{2,1,0:T(8,128)(2,1)S(1)} %get-tuple-element.92.refs_0_, bf16[4,104,256]{2,1,0:T(8,128)(2,1)S(1)} %collective-permute-done.21.refs_1_), custom_call_target="tpu_custom_call" | custom-call | bytes 2097152 | tf_op jit(solution)/shard_map/pallas_call | solution.py:303
  118.6 2.8 %shard_map.141 = (f32[2048,256]{1,0:T(8,128)}, f32[16,128]{1,0:T(8,128)}) custom-call(s32[4]{0:T(128)S(1)} %pad_add_fusion.place_ref, bf16[4,256,256]{2,1,0:T(8,128)(2,1)S(1)} %get-tuple-element.89.refs_0_, bf16[4,256,256]{2,1,0:T(8,128)(2,1)S(1)} %collective-permute-done.17.refs_1_, bf16[2048,256]{1,0:T(8,128)(2,1)S(1)} %copy-done.1, ...), custom_call_target="tpu_custom_call" | custom-call | bytes 1048576 | tf_op jit(solution)/shard_map/pallas_call | solution.py:36
  121.4 5.0 %collective-permute-done.19.refs_1_ = bf16[4,104,256]{2,1,0:T(8,128)(2,1)S(1)} collective-permute-done((bf16[4,104,256]{2,1,0:T(8,128)(2,1)S(1)}, bf16[4,104,256]{2,1,0:T(8,128)(2,1)S(1)}, u32[]{:S(2)}, u32[]{:S(2)}) %collective-permute-start.19) | collective-permute-done | bytes 213024 | tf_op jit(solution)/shard_map/ppermute | solution.py:373
  126.4 1.1 collective-permute-start.22
  127.5 0.5 collective-permute-start.24
  128.0 1.7 %shard_map.143 = (f32[3072,256]{1,0:T(8,128)}, f32[4,256]{1,0:T(4,128)S(1)}) custom-call(s32[4]{0:T(128)S(1)} %pad_add_fusion.place_ref, bf16[4,104,256]{2,1,0:T(8,128)(2,1)S(1)} %collective-permute-done.18.refs_0_, bf16[4,104,256]{2,1,0:T(8,128)(2,1)S(1)} %collective-permute-done.19.refs_1_, ...), custom_call_target="tpu_custom_call", output_to_operand_aliasing={{0}: (4, {})} | custom-call | bytes 2097152 | tf_op jit(solution)/shard_map/pallas_call | solution.py:303
  129.7 2.2 %shard_map.144 = (f32[3072,256]{1,0:T(8,128)}, f32[4,256]{1,0:T(4,128)}) custom-call(s32[4]{0:T(128)S(1)} %pad_add_fusion.place_ref, bf16[4,104,256]{2,1,0:T(8,128)(2,1)S(1)} %collective-permute-done.22.refs_0_, bf16[4,104,256]{2,1,0:T(8,128)(2,1)S(1)} %collective-permute-done.23.refs_1_, ...), custom_call_target="tpu_custom_call", output_to_operand_aliasing={{0}: (4, {})} | custom-call | bytes 2097152 | tf_op jit(solution)/shard_map/pallas_call | solution.py:303
  (53 shorter events, 2.3 us)
Async XLA Ops:
  2.1 20.4 %all-to-all-start = ((s32[32,1,32]{2,1,0:T(1,128)}), s32[32,1,32]{2,1,0:T(1,128)S(1)}, u32[]{:S(2)}, u32[]{:S(2)}) async-start(s32[32,1,32]{2,1,0:T(1,128)} %compare_select_fusion), calls=%async_computation | async-start | bytes 32768 | tf_op jit(solution)/shard_map/all_to_all | solution.py:397
  15.0 1.2 copy-start
  16.6 11.5 %copy-start.5 = (s32[2,256]{1,0:T(2,128)S(1)}, s32[2,256]{1,0:T(2,128)}, u32[]{:S(2)}) copy-start(s32[2,256]{1,0:T(2,128)} %param.11) | copy-start | bytes 6148
  16.6 11.5 %copy-start.6 = (s32[1,2]{1,0:T(1,128)S(1)}, s32[1,2]{1,0:T(1,128)}, u32[]{:S(2)}) copy-start(s32[1,2]{1,0:T(1,128)} %param.10) | copy-start | bytes 28
  24.1 17.0 %copy-start.4 = (f32[4,256]{1,0:T(4,128)S(1)}, f32[4,256]{1,0:T(4,128)}, u32[]{:S(2)}) copy-start(f32[4,256]{1,0:T(4,128)} %gain_ref.1) | copy-start | bytes 12292
  24.1 17.0 %all-to-all-start.1 = ((bf16[32,32,256]{2,1,0:T(8,128)(2,1)}), bf16[32,32,256]{2,1,0:T(8,128)(2,1)S(1)}, u32[]{:S(2)}, u32[]{:S(2)}) async-start(bf16[32,32,256]{2,1,0:T(8,128)(2,1)} %shard_map.130), calls=%async_computation.1 | async-start | bytes 1048576 | tf_op jit(solution)/shard_map/all_to_all | solution.py:408
  41.1 1.0 copy-start.3
  48.3 10.2 %collective-permute-start = (bf16[16,104,256]{2,1,0:T(8,128)(2,1)}, bf16[16,104,256]{2,1,0:T(8,128)(2,1)S(1)}, u32[]{:S(2)}, u32[]{:S(2)}) collective-permute-start(bf16[16,104,256]{2,1,0:T(8,128)(2,1)} %get-tuple-element.55), channel_id=1, source_target_pairs={{0,1},{1,0},{2,3},{3,2},{4,5},{5,4},{6,7},{7,6},{8,9},{9,8},{10,11... | collective-permute-start | bytes 2555912 | tf_op jit(solution)/shard_map/ppermute | solution.py:377
  53.5 24.2 %all-to-all-start.2 = ((bf16[32,32,256]{2,1,0:T(8,128)(2,1)}), bf16[32,32,256]{2,1,0:T(8,128)(2,1)S(1)}, u32[]{:S(2)}, u32[]{:S(2)}) async-start(bf16[32,32,256]{2,1,0:T(8,128)(2,1)} %bitcast.24), calls=%async_computation.2 | async-start | bytes 1048576 | tf_op jit(solution)/shard_map/all_to_all | solution.py:444
  58.7 8.2 %collective-permute-start.1 = (bf16[4,104,256]{2,1,0:T(8,128)(2,1)S(1)}, bf16[4,104,256]{2,1,0:T(8,128)(2,1)S(1)}, u32[]{:S(2)}, u32[]{:S(2)}) collective-permute-start(bf16[4,104,256]{2,1,0:T(8,128)(2,1)S(1)} %get-tuple-element.57), channel_id=1, source_target_pairs={{0,4},{2,6},{4,0},{6,2},{1,5},{3,7},{5,1},{7,3},{8,12},{10,14},{12... | collective-permute-start | bytes 638984 | tf_op jit(solution)/shard_map/ppermute | solution.py:373
  61.7 10.3 %collective-permute-start.2 = (bf16[4,104,256]{2,1,0:T(8,128)(2,1)S(1)}, bf16[4,104,256]{2,1,0:T(8,128)(2,1)S(1)}, u32[]{:S(2)}, u32[]{:S(2)}) collective-permute-start(bf16[4,104,256]{2,1,0:T(8,128)(2,1)S(1)} %get-tuple-element.58), channel_id=1, source_target_pairs={{0,2},{2,4},{4,6},{6,0},{1,3},{3,5},{5,7},{7,1},{8,10},{10,12},{12... | collective-permute-start | bytes 638984 | tf_op jit(solution)/shard_map/ppermute | solution.py:373
  62.1 9.9 %collective-permute-start.3 = (bf16[4,104,256]{2,1,0:T(8,128)(2,1)S(1)}, bf16[4,104,256]{2,1,0:T(8,128)(2,1)S(1)}, u32[]{:S(2)}, u32[]{:S(2)}) collective-permute-start(bf16[4,104,256]{2,1,0:T(8,128)(2,1)S(1)} %get-tuple-element.59), channel_id=1, source_target_pairs={{0,6},{2,0},{4,2},{6,4},{1,7},{3,1},{5,3},{7,5},{8,14},{10,8},{12,... | collective-permute-start | bytes 638984 | tf_op jit(solution)/shard_map/ppermute | solution.py:373
  72.1 46.5 %copy-start.1 = (bf16[2048,256]{1,0:T(8,128)(2,1)S(1)}, bf16[2048,256]{1,0:T(8,128)(2,1)}, u32[]{:S(2)}) copy-start(bf16[2048,256]{1,0:T(8,128)(2,1)} %refs_2_.1) | copy-start | bytes 3145732
  72.1 46.5 %copy-start.2 = (f32[2048]{0:T(1024)S(1)}, f32[2048]{0:T(1024)}, u32[]{:S(2)}) copy-start(f32[2048]{0:T(1024)} %param.16) | copy-start | bytes 24580
  72.2 5.4 %collective-permute-start.4 = (bf16[1,104,256]{2,1,0:T(8,128)(2,1)S(1)}, bf16[1,104,256]{2,1,0:T(8,128)(2,1)S(1)}, u32[]{:S(2)}, u32[]{:S(2)}) collective-permute-start(bf16[1,104,256]{2,1,0:T(8,128)(2,1)S(1)} %get-tuple-element.61), channel_id=1, source_target_pairs={{0,128},{64,192},{128,0},{192,64},{1,129},{65,193},{129,1},{193,65... | collective-permute-start | bytes 159752 | tf_op jit(solution)/shard_map/ppermute | solution.py:373
  74.9 4.2 %collective-permute-start.5 = (bf16[1,104,256]{2,1,0:T(8,128)(2,1)S(1)}, bf16[1,104,256]{2,1,0:T(8,128)(2,1)S(1)}, u32[]{:S(2)}, u32[]{:S(2)}) collective-permute-start(bf16[1,104,256]{2,1,0:T(8,128)(2,1)S(1)} %get-tuple-element.62), channel_id=1, source_target_pairs={{0,64},{64,128},{128,192},{192,0},{1,65},{65,129},{129,193},{193,1... | collective-permute-start | bytes 159752 | tf_op jit(solution)/shard_map/ppermute | solution.py:373
  75.3 3.9 %collective-permute-start.6 = (bf16[1,104,256]{2,1,0:T(8,128)(2,1)S(1)}, bf16[1,104,256]{2,1,0:T(8,128)(2,1)S(1)}, u32[]{:S(2)}, u32[]{:S(2)}) collective-permute-start(bf16[1,104,256]{2,1,0:T(8,128)(2,1)S(1)} %get-tuple-element.63), channel_id=1, source_target_pairs={{0,192},{64,0},{128,64},{192,128},{1,193},{65,1},{129,65},{193,129... | collective-permute-start | bytes 159752 | tf_op jit(solution)/shard_map/ppermute | solution.py:373
  80.2 4.0 %collective-permute-start.7 = (bf16[4,256,256]{2,1,0:T(8,128)(2,1)S(1)}, bf16[4,256,256]{2,1,0:T(8,128)(2,1)S(1)}, u32[]{:S(2)}, u32[]{:S(2)}) collective-permute-start(bf16[4,256,256]{2,1,0:T(8,128)(2,1)S(1)} %get-tuple-element.68), channel_id=1, source_target_pairs={{0,1},{1,0},{2,3},{3,2},{4,5},{5,4},{6,7},{7,6},{8,9},{9,8},{10,11... | collective-permute-start | bytes 1572872 | tf_op jit(solution)/shard_map/ppermute | solution.py:377
  84.3 9.0 %collective-permute-start.11 = (bf16[2,256,256]{2,1,0:T(8,128)(2,1)S(1)}, bf16[2,256,256]{2,1,0:T(8,128)(2,1)S(1)}, u32[]{:S(2)}, u32[]{:S(2)}) collective-permute-start(bf16[2,256,256]{2,1,0:T(8,128)(2,1)S(1)} %get-tuple-element.76), channel_id=1, source_target_pairs={{0,2},{2,0},{4,6},{6,4},{1,3},{3,1},{5,7},{7,5},{8,10},{10,8},{12,... | collective-permute-start | bytes 786440 | tf_op jit(solution)/shard_map/ppermute | solution.py:377
  85.5 4.9 %collective-permute-start.10 = (bf16[1,104,256]{2,1,0:T(8,128)(2,1)S(1)}, bf16[1,104,256]{2,1,0:T(8,128)(2,1)S(1)}, u32[]{:S(2)}, u32[]{:S(2)}) collective-permute-start(bf16[1,104,256]{2,1,0:T(8,128)(2,1)S(1)} %shard_map.135.a_ref), channel_id=1, source_target_pairs={{0,24},{8,16},{16,8},{24,0},{32,56},{40,48},{48,40},{56,32},{1,25}... | collective-permute-start | bytes 159752 | tf_op jit(solution)/shard_map/ppermute | solution.py:377
  88.6 4.7 %collective-permute-start.9 = (bf16[1,104,256]{2,1,0:T(8,128)(2,1)S(1)}, bf16[1,104,256]{2,1,0:T(8,128)(2,1)S(1)}, u32[]{:S(2)}, u32[]{:S(2)}) collective-permute-start(bf16[1,104,256]{2,1,0:T(8,128)(2,1)S(1)} %shard_map.135.a_ref), channel_id=1, source_target_pairs={{0,16},{8,24},{16,0},{24,8},{32,48},{40,56},{48,32},{56,40},{1,17}... | collective-permute-start | bytes 159752 | tf_op jit(solution)/shard_map/ppermute | solution.py:377
  88.6 4.7 %collective-permute-start.8 = (bf16[1,104,256]{2,1,0:T(8,128)(2,1)S(1)}, bf16[1,104,256]{2,1,0:T(8,128)(2,1)S(1)}, u32[]{:S(2)}, u32[]{:S(2)}) collective-permute-start(bf16[1,104,256]{2,1,0:T(8,128)(2,1)S(1)} %shard_map.135.a_ref), channel_id=1, source_target_pairs={{0,8},{8,0},{16,24},{24,16},{32,40},{40,32},{48,56},{56,48},{1,9},... | collective-permute-start | bytes 159752 | tf_op jit(solution)/shard_map/ppermute | solution.py:377
  93.3 7.0 %collective-permute-start.13 = (bf16[1,256,256]{2,1,0:T(8,128)(2,1)S(1)}, bf16[1,256,256]{2,1,0:T(8,128)(2,1)S(1)}, u32[]{:S(2)}, u32[]{:S(2)}) collective-permute-start(bf16[1,256,256]{2,1,0:T(8,128)(2,1)S(1)} %get-tuple-element.84), channel_id=1, source_target_pairs={{0,6},{2,4},{4,2},{6,0},{1,7},{3,5},{5,3},{7,1},{8,14},{10,12},{12... | collective-permute-start | bytes 393224 | tf_op jit(solution)/shard_map/ppermute | solution.py:377
  95.1 5.2 %collective-permute-start.12 = (bf16[1,104,256]{2,1,0:T(8,128)(2,1)S(1)}, bf16[1,104,256]{2,1,0:T(8,128)(2,1)S(1)}, u32[]{:S(2)}, u32[]{:S(2)}) collective-permute-start(bf16[1,104,256]{2,1,0:T(8,128)(2,1)S(1)} %shard_map.137.a_ref), channel_id=1, source_target_pairs={{0,48},{8,56},{16,32},{24,40},{32,16},{40,24},{48,0},{56,8},{1,49}... | collective-permute-start | bytes 159752 | tf_op jit(solution)/shard_map/ppermute | solution.py:377
  100.3 6.1 %collective-permute-start.16 = (bf16[360,256]{1,0:T(8,128)(2,1)S(1)}, bf16[360,256]{1,0:T(8,128)(2,1)S(1)}, u32[]{:S(2)}, u32[]{:S(2)}) collective-permute-start(bf16[360,256]{1,0:T(8,128)(2,1)S(1)} %shard_map.139.refs_0_), channel_id=1, source_target_pairs={{0,4},{2,6},{4,0},{6,2},{1,5},{3,7},{5,1},{7,3},{8,12},{10,14},{12... | collective-permute-start | bytes 552968 | tf_op jit(solution)/shard_map/ppermute | solution.py:373
  101.2 9.9 %collective-permute-start.15 = (bf16[360,256]{1,0:T(8,128)(2,1)S(1)}, bf16[360,256]{1,0:T(8,128)(2,1)S(1)}, u32[]{:S(2)}, u32[]{:S(2)}) collective-permute-start(bf16[360,256]{1,0:T(8,128)(2,1)S(1)} %shard_map.139.refs_0_), channel_id=1, source_target_pairs={{0,2},{2,4},{4,6},{6,0},{1,3},{3,5},{5,7},{7,1},{8,10},{10,12},{12... | collective-permute-start | bytes 552968 | tf_op jit(solution)/shard_map/ppermute | solution.py:373
  102.0 9.1 %collective-permute-start.14 = (bf16[360,256]{1,0:T(8,128)(2,1)S(1)}, bf16[360,256]{1,0:T(8,128)(2,1)S(1)}, u32[]{:S(2)}, u32[]{:S(2)}) collective-permute-start(bf16[360,256]{1,0:T(8,128)(2,1)S(1)} %shard_map.139.refs_0_), channel_id=1, source_target_pairs={{0,6},{2,0},{4,2},{6,4},{1,7},{3,1},{5,3},{7,5},{8,14},{10,8},{12,... | collective-permute-start | bytes 552968 | tf_op jit(solution)/shard_map/ppermute | solution.py:373
  111.2 7.3 %collective-permute-start.17 = (bf16[4,256,256]{2,1,0:T(8,128)(2,1)S(1)}, bf16[4,256,256]{2,1,0:T(8,128)(2,1)S(1)}, u32[]{:S(2)}, u32[]{:S(2)}) collective-permute-start(bf16[4,256,256]{2,1,0:T(8,128)(2,1)S(1)} %get-tuple-element.89.refs_0_), channel_id=1, source_target_pairs={{0,1},{1,0},{2,3},{3,2},{4,5},{5,4},{6,7},{7,6},{8,9},{9,8},{10,11... | collective-permute-start | bytes 1572872 | tf_op jit(solution)/shard_map/ppermute | solution.py:377
  113.1 4.0 %collective-permute-start.21 = (bf16[4,104,256]{2,1,0:T(8,128)(2,1)S(1)}, bf16[4,104,256]{2,1,0:T(8,128)(2,1)S(1)}, u32[]{:S(2)}, u32[]{:S(2)}) collective-permute-start(bf16[4,104,256]{2,1,0:T(8,128)(2,1)S(1)} %get-tuple-element.92.refs_0_), channel_id=1, source_target_pairs={{0,1},{1,0},{2,3},{3,2},{4,5},{5,4},{6,7},{7,6},{8,9},{9,8},{10,11... | collective-permute-start | bytes 638984 | tf_op jit(solution)/shard_map/ppermute | solution.py:377
  113.2 8.2 %collective-permute-start.20 = (bf16[4,104,256]{2,1,0:T(8,128)(2,1)S(1)}, bf16[4,104,256]{2,1,0:T(8,128)(2,1)S(1)}, u32[]{:S(2)}, u32[]{:S(2)}) collective-permute-start(bf16[4,104,256]{2,1,0:T(8,128)(2,1)S(1)} %get-tuple-element.92.refs_0_), channel_id=1, source_target_pairs={{0,128},{64,192},{128,0},{192,64},{1,129},{65,193},{129,1},{193,65... | collective-permute-start | bytes 638984 | tf_op jit(solution)/shard_map/ppermute | solution.py:373
  114.4 12.1 %collective-permute-start.19 = (bf16[4,104,256]{2,1,0:T(8,128)(2,1)S(1)}, bf16[4,104,256]{2,1,0:T(8,128)(2,1)S(1)}, u32[]{:S(2)}, u32[]{:S(2)}) collective-permute-start(bf16[4,104,256]{2,1,0:T(8,128)(2,1)S(1)} %get-tuple-element.92.refs_0_), channel_id=1, source_target_pairs={{0,64},{64,128},{128,192},{192,0},{1,65},{65,129},{129,193},{193,1... | collective-permute-start | bytes 638984 | tf_op jit(solution)/shard_map/ppermute | solution.py:373
  116.7 9.7 %collective-permute-start.18 = (bf16[4,104,256]{2,1,0:T(8,128)(2,1)S(1)}, bf16[4,104,256]{2,1,0:T(8,128)(2,1)S(1)}, u32[]{:S(2)}, u32[]{:S(2)}) collective-permute-start(bf16[4,104,256]{2,1,0:T(8,128)(2,1)S(1)} %get-tuple-element.92.refs_0_), channel_id=1, source_target_pairs={{0,192},{64,0},{128,64},{192,128},{1,193},{65,1},{129,65},{193,129... | collective-permute-start | bytes 638984 | tf_op jit(solution)/shard_map/ppermute | solution.py:373
  126.4 3.3 %collective-permute-start.22 = (bf16[4,104,256]{2,1,0:T(8,128)(2,1)S(1)}, bf16[4,104,256]{2,1,0:T(8,128)(2,1)S(1)}, u32[]{:S(2)}, u32[]{:S(2)}) collective-permute-start(bf16[4,104,256]{2,1,0:T(8,128)(2,1)S(1)} %collective-permute-done.18.refs_0_), channel_id=1, source_target_pairs={{0,1},{1,0},{2,3},{3,2},{4,5},{5,4},{6,7},{7,6},{8,9},{9,8},{10,11... | collective-permute-start | bytes 638984 | tf_op jit(solution)/shard_map/ppermute | solution.py:377
  127.5 2.2 %collective-permute-start.23 = (bf16[4,104,256]{2,1,0:T(8,128)(2,1)S(1)}, bf16[4,104,256]{2,1,0:T(8,128)(2,1)S(1)}, u32[]{:S(2)}, u32[]{:S(2)}) collective-permute-start(bf16[4,104,256]{2,1,0:T(8,128)(2,1)S(1)} %collective-permute-done.19.refs_1_), channel_id=1, source_target_pairs={{0,1},{1,0},{2,3},{3,2},{4,5},{5,4},{6,7},{7,6},{8,9},{9,8},{10,11... | collective-permute-start | bytes 638984 | tf_op jit(solution)/shard_map/ppermute | solution.py:377
  127.5 2.2 %collective-permute-start.24 = (bf16[4,104,256]{2,1,0:T(8,128)(2,1)S(1)}, bf16[4,104,256]{2,1,0:T(8,128)(2,1)S(1)}, u32[]{:S(2)}, u32[]{:S(2)}) collective-permute-start(bf16[4,104,256]{2,1,0:T(8,128)(2,1)S(1)} %collective-permute-done.20.refs_2_), channel_id=1, source_target_pairs={{0,1},{1,0},{2,3},{3,2},{4,5},{5,4},{6,7},{7,6},{8,9},{9,8},{10,11... | collective-permute-start | bytes 638984 | tf_op jit(solution)/shard_map/ppermute | solution.py:377
